TPU v7x, 256 devices: a whole 4x4x8 slice. The times are simulated.
256 devices in a mesh: snap: 8 (over x, y_hi), coef: 32 (over y_lo, z, core).
Axes of the slice: x: 4, y: 4 (y_hi: 2, y_lo: 2; y = y_hi * 2 + y_lo), z: 8, core: 2. Of those that a mesh axis runs over, the one named last changes fastest.
Arguments:
- queries: bfloat16 [1024, 65536], P('snap', 'coef'), may hold values from -32 to 32
- slab: bfloat16 [16384, 65536], P('snap', 'coef'), may hold values from -32 to 32
- degree: int32 [65536], P('coef'), may hold values from 0 to 255
- degree_weight: float32 [256], replicated, may hold values from 0.05 to 20
- spread: float32 [1], replicated, may hold values from 1048576 to 3145728
Outputs:
- kernel: float32 [1024, 16384], P('coef', 'snap')
All inputs are finite; a program needn't handle non-finite values.
Results may differ from a plain program's by a relative error of at most 0.0003.
Values may be sent and summed in bfloat16 or wider, within the bound.
No kernel may reach another device: no remote copies, remote signals or barrier semaphores. Data moves between devices by JAX's collectives and lax.ppermute only.
A program may use at most 64 MiB of HBM per device.

v0:
```python
import jax
import jax.numpy as jnp
from jax import lax
from jax.sharding import PartitionSpec as P


def body(queries, slab, degree, degree_weight, spread):
    levels = jnp.arange(degree_weight.shape[0], dtype=jnp.int32)
    one_hot_table = (degree[:, None] == levels[None, :]).astype(jnp.float32)
    weight_of = jnp.dot(one_hot_table, degree_weight, precision=lax.Precision.HIGHEST)
    slab_wide = slab.astype(jnp.float32)
    weighted_slab = (slab_wide * weight_of[None, :]).astype(jnp.bfloat16)
    slab_part = jnp.sum(slab_wide * slab_wide * weight_of[None, :], axis=1)
    query_wide = queries.astype(jnp.float32)
    query_part = jnp.sum(query_wide * query_wide * weight_of[None, :], axis=1)
    slab_norm, query_local = lax.psum((slab_part, query_part), "coef")
    query_norm = lax.all_gather(query_local, "snap", axis=0, tiled=True)
    partial_value = lax.dot_general(
        lax.all_gather(queries, "snap", axis=0, tiled=True),
        weighted_slab,
        (((1,), (1,)), ((), ())),
        preferred_element_type=jnp.float32,
    )
    position = lax.axis_index("coef")
    gram_block = lax.psum_scatter(partial_value, "coef", scatter_dimension=0, tiled=True)
    row_count = gram_block.shape[0]
    norms_here = lax.dynamic_slice_in_dim(query_norm, position * row_count, row_count, 0)
    distance = norms_here[:, None] + slab_norm[None, :] - 2.0 * gram_block
    return jnp.exp(-distance / spread[0])


def solution(mesh):
    placed = (P("snap", "coef"), P("snap", "coef"), P("coef"), P(), P())
    return jax.shard_map(
        body, mesh=mesh, in_specs=placed, out_specs=P("coef", "snap"), check_vma=False
    )
```

profile of v0, /device:TPU:32, one launch (start us, length us, event | category | flops | bytes accessed | tf_op | source)
XLA Modules:
  0.0 245.1 jit_solution(697513725615749958)
XLA Ops:
  6.5 0.0 copy-start
  6.5 0.0 all-gather.3.cloned.1.call-start
  6.5 0.7 all-gather.3.cloned.1.call-update
  7.3 0.0 reduce-scatter.4.cloned.1.call-start
  7.3 0.0 copy-done
  7.3 1.7 fusion.9
  9.1 80.2 %all-gather.3.cloned.1.call-done = bf16[1024,2048]{1,0:T(8,128)(2,1)} async-done(((bf16[128,2048]{1,0:T(8,128)(2,1)}), bf16[1024,2048]{1,0:T(8,128)(2,1)}) %all-gather.3.cloned.1.call-update) | async-done | bytes 4194320 | tf_op jit(solution)/shard_map/all_gather | solution.py:19
  89.3 14.5 %fusion.6 = f32[1024,2048]{0,1:T(8,128)} fusion(bf16[1024,2048]{1,0:T(8,128)(2,1)} %all-gather.3.cloned.1.call-done, bf16[2048,2048]{1,0:T(8,128)(2,1)} %param.6, f32[2048]{0:T(1024)S(1)} %bitcast.12), kind=kOutput, calls=%fused_computation.7 | convolution fusion | flops 8602517504 | bytes 20979712 | tf_op jit(solution)/shard_map/dot_general | solution.py:18
  103.8 9.1 %copy.9 = f32[1024,2048]{1,0:T(8,128)} copy(f32[1024,2048]{0,1:T(8,128)} %fusion.6) | data formatting | bytes 16777216
  112.9 0.0 copy-start.1
  112.9 0.0 reduce-scatter.4.cloned.1.call-update
  113.7 0.3 copy-done.1
  114.0 0.2 multiply_reduce_fusion
  114.2 5.7 %fusion.1 = f32[2048]{0:T(1024)S(1)} fusion(bf16[2048,2048]{1,0:T(8,128)(2,1)} %param.6, f32[2048]{0:T(1024)S(1)} %bitcast.14), kind=kLoop, calls=%fused_computation.3 | loop fusion | flops 16775168 | bytes 8404992 | tf_op jit(solution)/shard_map/reduce_sum | solution.py:13
  119.9 53.6 %all-reduce = (f32[2048]{0:T(1024)S(1)}, f32[128]{0:T(128)S(1)}) all-reduce(f32[2048]{0:T(1024)S(1)} %fusion.1, f32[128]{0:T(128)S(1)} %multiply_reduce_fusion), channel_id=1, replica_groups=mesh['snap'=8,'coef'=32] {'coef'}, use_global_device_ids=true, to_apply=%region_3.0 | all-reduce | flops 2176 | bytes 17408 | tf_op jit(solution)/shard_map/psum | solution.py:16
  173.5 20.2 %all-gather = f32[8,1,128]{2,1,0:T(1,128)S(1)} all-gather(f32[1,1,128]{2,1,0:T(1,128)S(1)} %bitcast.16), channel_id=1, replica_groups=mesh['snap'=8,'coef'=32] {'snap'}, dimensions={0}, use_global_device_ids=true | all-gather | bytes 4608 | tf_op jit(solution)/shard_map/all_gather | solution.py:17
  193.7 0.1 dynamic_slice.3
  193.7 42.8 %reduce-scatter.4.cloned.1.call-done = f32[32,2048]{1,0:T(8,128)} async-done(((f32[1024,2048]{1,0:T(8,128)}), f32[32,2048]{1,0:T(8,128)}) %reduce-scatter.4.cloned.1.call-update) | async-done | bytes 262160 | tf_op jit(solution)/shard_map/reduce_scatter | solution.py:25
  236.5 1.8 divide_exponential_fusion
Async XLA Ops:
  6.5 0.8 copy-start
  6.5 82.8 %all-gather.3.cloned.1.call-start = ((), (), s32[]{:S(2)}) async-start(), calls=%async_computation.1 | async-start | bytes 4718592 | tf_op jit(solution)/shard_map/all_gather | solution.py:19
  7.3 229.2 %reduce-scatter.4.cloned.1.call-start = ((), (), s32[]{:S(2)}) async-start(), calls=%async_computation.2 | async-start | bytes 8650752 | tf_op jit(solution)/shard_map/reduce_scatter | solution.py:25
  112.9 1.1 copy-start.1
Sparse Core Ops, SparseCore 0:
  10.0 79.2 all-gather.2
  113.1 123.3 reduce-scatter.3
where the time goes:
time: 250 us; the launch traced here: 245 us
  waiting for transfers between devices  124 us (50%)
  blocking collectives  73.8 us (30%)
  matrix products  16.2 us (6%)
  between operations  14.1 us (6%)
  local copies, waits for them, and re-layouts  9.55 us (4%)
  other arithmetic  7.66 us (3%)
    all_gather x1, waiting for transfers between devices, body(): lax.all_gather(queries, 'snap', axis=0, tiled=True)  80.2 us
    psum x1, blocking collectives, body(): slab_norm, query_local = lax.psum((slab_part, query_part), 'coef')  53.6 us
    reduce_scatter x1, waiting for transfers between devices, body(): lax.psum_scatter(partial_value, 'coef', scatter_dimension=0, tiled=True)  42.8 us
    all_gather x1, blocking collectives, body(): query_norm = lax.all_gather(query_local, 'snap', axis=0, tiled=True)  20.2 us
    dot_general x1, matrix products, body(): lax.dot_general(lax.all_gather(queries, 'snap', axis=0, tiled=True), weig...  14.5 us
    unnamed x5, local copies, waits for them, and re-layouts  9.47 us
    reduce_sum x1, other arithmetic, body(): slab_part = jnp.sum(slab_wide * slab_wide * weight_of[None, :], axis=1)  5.66 us
  transfers between devices with their start and end apart: 2, of which 2 were waited for; matrix products, arithmetic and copies ran while one was open for 3% of the time, Pallas kernels for 0%

commit v1 on v0

v1 whole, which is shorter than its diff:
```python
import jax
import jax.numpy as jnp
from jax import lax
from jax.sharding import Mesh, PartitionSpec as P

X, YH, YL, Z, CORE = 4, 2, 2, 8, 2
SCALE = 2.0 ** -17
COEF = ("yl", "z", "core")
SNAP = ("x", "yh")


def shift(value, axis, by):
    size = {"x": X, "yh": YH, "yl": YL, "z": Z, "core": CORE}[axis]
    return lax.ppermute(value, axis, [(i, (i + by) % size) for i in range(size)])


def gather_queries(own):
    x, yh = lax.axis_index("x"), lax.axis_index("yh")
    pair = shift(own, "yh", 1)
    left, right, far = shift(own, "x", 1), shift(own, "x", -1), shift(own, "x", 2)
    pair_left, pair_right, pair_far = shift(pair, "x", 1), shift(pair, "x", -1), shift(far, "yh", 1)
    rows = own.shape[0]
    out = jnp.zeros((rows * X * YH, own.shape[1]), own.dtype)
    for block, dx, dy in (
        (own, 0, 0), (pair, 0, 1), (left, -1, 0), (right, 1, 0), (far, 2, 0),
        (pair_left, -1, 1), (pair_right, 1, 1), (pair_far, 2, 1),
    ):
        source = ((x + dx + X) % X) * YH + (yh + dy) % YH
        out = lax.dynamic_update_slice(out, block, (source * rows, 0))
    return out


def pack(value):
    return (value * SCALE).astype(jnp.float16)


def unpack(value):
    return value.astype(jnp.float32) * (1.0 / SCALE)


def reduce_z(held):
    z = lax.axis_index("z")

    def dest(k):
        return lax.dynamic_index_in_dim(held, (z + k + Z) % Z, 1, keepdims=False)

    minus = shift(pack(jnp.stack([dest(-1), dest(-3)])), "z", -1)
    plus = shift(pack(jnp.stack([dest(1), dest(3)])), "z", 1)
    across = dest(4)
    minus2 = shift(pack(across[0]), "z", -2)
    plus2 = shift(pack(across[1]), "z", 2)
    sum_minus = dest(-2) + unpack(minus[1])
    sum_minus = jnp.stack([sum_minus[0] + unpack(minus2), sum_minus[1]])
    sum_plus = dest(2) + unpack(plus[1])
    sum_plus = jnp.stack([sum_plus[0], sum_plus[1] + unpack(plus2)])
    last_minus = shift(pack(sum_minus), "z", -2)
    last_plus = shift(pack(sum_plus), "z", 2)
    return dest(0) + unpack(minus[0]) + unpack(plus[0]) + unpack(last_minus) + unpack(last_plus)


def body(queries, slab, degree, degree_weight, spread):
    levels = jnp.arange(degree_weight.shape[0], dtype=jnp.int32)
    one_hot_table = (degree[:, None] == levels[None, :]).astype(jnp.float32)
    weight_of = jnp.dot(one_hot_table, degree_weight, precision=lax.Precision.HIGHEST)
    slab_wide = slab.astype(jnp.float32)
    weighted_slab = (slab_wide * weight_of[None, :]).astype(jnp.bfloat16)
    slab_part = jnp.sum(slab_wide * slab_wide * weight_of[None, :], axis=1)
    every = gather_queries(queries)
    query_wide = every.astype(jnp.float32)
    query_part = jnp.sum(query_wide * query_wide * weight_of[None, :], axis=1)
    gram_part = lax.dot_general(
        every, weighted_slab, (((1,), (1,)), ((), ())), preferred_element_type=jnp.float32
    )
    partial = query_part[:, None] + slab_part[None, :] - 2.0 * gram_part
    columns = partial.shape[1]
    partial = partial.reshape(YL, Z, CORE, -1, columns)
    core = lax.axis_index("core")
    mine = lax.dynamic_index_in_dim(partial, core, 2, keepdims=False)
    other = lax.dynamic_index_in_dim(partial, 1 - core, 2, keepdims=False)
    held = mine + shift(other, "core", 1)
    summed = reduce_z(held)
    yl = lax.axis_index("yl")
    mine = lax.dynamic_index_in_dim(summed, yl, 0, keepdims=False)
    other = lax.dynamic_index_in_dim(summed, 1 - yl, 0, keepdims=False)
    distance = mine + shift(other, "yl", 1)
    return jnp.exp(-distance / spread[0])


def solution(mesh):
    fine = Mesh(mesh.devices.reshape(X, YH, YL, Z, CORE), ("x", "yh", "yl", "z", "core"))
    placed = (P(SNAP, COEF), P(SNAP, COEF), P(COEF), P(), P())
    return jax.shard_map(
        body, mesh=fine, in_specs=placed, out_specs=P(COEF, SNAP), check_vma=False
    )
```

time: 250 us -> 129 us (0.52); the launches traced: 245 us -> 127 us
  blocking collectives: 73.8 us -> 0 us
  waiting for transfers between devices: 124 us -> 52.2 us
  starting transfers between devices: 0.04 us -> 25.4 us
  between operations: 14.1 us -> 0.83 us
  other arithmetic: 7.66 us -> 18.1 us
  local copies, waits for them, and re-layouts: 9.55 us -> 15.9 us
    all_gather x1 -> x0, waiting for transfers between devices: 80.2 us -> none  [body(): lax.all_gather(queries, 'snap', axis=0, tiled=True)]
    psum x1 -> x0, blocking collectives: 53.6 us -> none  [body(): slab_norm, query_local = lax.psum((slab_part, query_part), 'coef')]
    ppermute x0 -> x15, waiting for transfers between devices: none -> 52.2 us  [shift(): lax.ppermute(value, axis, [(i, (i + by) % size) for i in range(size)])]
    reduce_scatter x1 -> x0, waiting for transfers between devices: 42.8 us -> none  [body(): lax.psum_scatter(partial_value, 'coef', scatter_dimension=0, tiled=True)]
    ppermute x0 -> x15, starting transfers between devices: none -> 25.4 us  [shift(): lax.ppermute(value, axis, [(i, (i + by) % size) for i in range(size)])]
    all_gather x1 -> x0, blocking collectives: 20.2 us -> none  [body(): query_norm = lax.all_gather(query_local, 'snap', axis=0, tiled=True)]
    add x0 -> x3, other arithmetic: none -> 6.86 us  [the longest x1 4.23 us: body(): held = mine + shift(other, 'core', 1)]
    dynamic_update_slice x0 -> x8, local copies, waits for them, and re-layouts: none -> 6.75 us  [gather_queries(): out = lax.dynamic_update_slice(out, block, (source * rows, 0))]
  transfers between devices with their start and end apart: 2 -> 15, of which waited for: 2 -> 9; matrix products, arithmetic and copies ran while one was open for 3% -> 15% of each run, Pallas kernels for 0% -> 0%
where the time goes in v1:
time: 129 us; the launch traced here: 127 us
  waiting for transfers between devices  52.2 us (40%)
  starting transfers between devices  25.4 us (20%)
  other arithmetic  18.1 us (14%)
  local copies, waits for them, and re-layouts  15.9 us (12%)
  matrix products  14.3 us (11%)
    ppermute x15, waiting for transfers between devices, shift(): lax.ppermute(value, axis, [(i, (i + by) % size) for i in range(size)])  52.2 us
    ppermute x15, starting transfers between devices, shift(): lax.ppermute(value, axis, [(i, (i + by) % size) for i in range(size)])  25.4 us
    dot_general x1, matrix products, body(): lax.dot_general(every, weighted_slab, (((1,), (1,)), ((), ())), preferred...  12.6 us
    dynamic_update_slice x8, local copies, waits for them, and re-layouts, gather_queries(): out = lax.dynamic_update_slice(out, block, (source * rows, 0))  6.75 us
    reduce_sum x1, other arithmetic, body(): slab_part = jnp.sum(slab_wide * slab_wide * weight_of[None, :], axis=1)  5.68 us
    add x1, other arithmetic, body(): held = mine + shift(other, 'core', 1)  4.23 us
    unnamed x8, local copies, waits for them, and re-layouts  4.03 us
    reduce_sum x1, other arithmetic, body(): query_part = jnp.sum(query_wide * query_wide * weight_of[None, :], axis=1)  3.36 us
  transfers between devices with their start and end apart: 15, of which 9 were waited for; matrix products, arithmetic and copies ran while one was open for 15% of the time, Pallas kernels for 0%

profile of v1, /device:TPU:32, one launch (start us, length us, event | category | flops | bytes accessed | tf_op | source)
XLA Modules:
  0.0 126.7 jit_solution(13556883405762567485)
XLA Ops:
  0.0 0.0 copy-start
  0.0 3.2 %collective-permute-start = (bf16[128,2048]{1,0:T(8,128)(2,1)}, bf16[128,2048]{1,0:T(8,128)(2,1)S(1)}, u32[]{:S(2)}, u32[]{:S(2)}) collective-permute-start(bf16[128,2048]{1,0:T(8,128)(2,1)} %param.5), channel_id=1, source_target_pairs={{0,32},{32,0},{1,33},{33,1},{2,34},{34,2},{3,35},{35,3},{4,36},{36... | collective-permute-start | bytes 1572872 | tf_op jit(solution)/shard_map/ppermute | solution.py:14
  3.2 1.5 %collective-permute-start.1 = (bf16[128,2048]{1,0:T(8,128)(2,1)}, bf16[128,2048]{1,0:T(8,128)(2,1)S(1)}, u32[]{:S(2)}, u32[]{:S(2)}) collective-permute-start(bf16[128,2048]{1,0:T(8,128)(2,1)} %param.5), channel_id=1, source_target_pairs={{0,64},{64,128},{128,192},{192,0},{1,65},{65,129},{129,193},{193,1... | collective-permute-start | bytes 1572872 | tf_op jit(solution)/shard_map/ppermute | solution.py:14
  4.7 1.7 %collective-permute-start.2 = (bf16[128,2048]{1,0:T(8,128)(2,1)}, bf16[128,2048]{1,0:T(8,128)(2,1)S(1)}, u32[]{:S(2)}, u32[]{:S(2)}) collective-permute-start(bf16[128,2048]{1,0:T(8,128)(2,1)} %param.5), channel_id=1, source_target_pairs={{0,192},{64,0},{128,64},{192,128},{1,193},{65,1},{129,65},{193,129... | collective-permute-start | bytes 1572872 | tf_op jit(solution)/shard_map/ppermute | solution.py:14
  6.4 1.8 %collective-permute-start.3 = (bf16[128,2048]{1,0:T(8,128)(2,1)}, bf16[128,2048]{1,0:T(8,128)(2,1)S(1)}, u32[]{:S(2)}, u32[]{:S(2)}) collective-permute-start(bf16[128,2048]{1,0:T(8,128)(2,1)} %param.5), channel_id=1, source_target_pairs={{0,128},{64,192},{128,0},{192,64},{1,129},{65,193},{129,1},{193,65... | collective-permute-start | bytes 1572872 | tf_op jit(solution)/shard_map/ppermute | solution.py:14
  8.2 0.0 copy-done
  8.3 1.7 %fusion.8 = f32[1,2048]{1,0:T(1,128)S(1)} fusion(f32[256,1]{0,1:T(1,128)S(1)} %bitcast.69, s32[2048]{0:T(1024)} %param.7), kind=kOutput, calls=%fused_computation.12 | convolution fusion | flops 6815744 | bytes 17408 | tf_op jit(solution)/shard_map/dot_general | solution.py:64
  10.0 5.7 %fusion.1 = f32[2048]{0:T(1024)S(1)} fusion(bf16[2048,2048]{1,0:T(8,128)(2,1)} %param.6, f32[2048]{0:T(1024)S(1)} %bitcast.72), kind=kLoop, calls=%fused_computation.3 | loop fusion | flops 16775168 | bytes 8404992 | tf_op jit(solution)/shard_map/reduce_sum | solution.py:67
  15.7 0.0 copy-start.3
  15.7 2.5 %broadcast_in_dim.2 = bf16[1024,2048]{1,0:T(8,128)(2,1)} broadcast(bf16[]{:T(256)} %constant.164.clone.1), dimensions={} | broadcast | bytes 4194306 | tf_op jit(solution)/shard_map/broadcast_in_dim | solution.py:23
  18.2 0.0 copy-done.3
  18.2 0.8 constant_dynamic-update-slice_fusion.7
  19.0 0.0 collective-permute-done
  19.0 0.6 collective-permute-start.4
  19.7 2.6 %collective-permute-start.5 = (bf16[128,2048]{1,0:T(8,128)(2,1)S(1)}, bf16[128,2048]{1,0:T(8,128)(2,1)S(1)}, u32[]{:S(2)}, u32[]{:S(2)}) collective-permute-start(bf16[128,2048]{1,0:T(8,128)(2,1)S(1)} %collective-permute-done), channel_id=1, source_target_pairs={{0,192},{64,0},{128,64},{192,128},{1,193},{65,1},{129,65},{193,129... | collective-permute-start | bytes 1572872 | tf_op jit(solution)/shard_map/ppermute | solution.py:14
  22.3 9.5 %collective-permute-done.3 = bf16[128,2048]{1,0:T(8,128)(2,1)S(1)} collective-permute-done((bf16[128,2048]{1,0:T(8,128)(2,1)}, bf16[128,2048]{1,0:T(8,128)(2,1)S(1)}, u32[]{:S(2)}, u32[]{:S(2)}) %collective-permute-start.3) | collective-permute-done | bytes 524320 | tf_op jit(solution)/shard_map/ppermute | solution.py:14
  31.7 0.3 collective-permute-start.6
  32.1 0.8 constant_dynamic-update-slice_fusion.6
  32.9 0.0 collective-permute-done.1
  32.9 0.8 constant_dynamic-update-slice_fusion.5
  33.7 0.0 collective-permute-done.2
  33.7 0.9 constant_dynamic-update-slice_fusion.4
  34.6 0.9 constant_dynamic-update-slice_fusion.3
  35.5 6.0 %collective-permute-done.4 = bf16[128,2048]{1,0:T(8,128)(2,1)S(1)} collective-permute-done((bf16[128,2048]{1,0:T(8,128)(2,1)S(1)}, bf16[128,2048]{1,0:T(8,128)(2,1)S(1)}, u32[]{:S(2)}, u32[]{:S(2)}) %collective-permute-start.4) | collective-permute-done | bytes 524320 | tf_op jit(solution)/shard_map/ppermute | solution.py:14
  41.5 0.8 constant_dynamic-update-slice_fusion.2
  42.3 0.0 collective-permute-done.5
  42.3 0.9 constant_dynamic-update-slice_fusion.1
  43.2 1.1 collective-permute-done.6
  44.2 0.8 constant_dynamic-update-slice_fusion
  45.1 3.4 %multiply_reduce_fusion = f32[1024]{0:T(1024)S(1)} fusion(bf16[1024,2048]{1,0:T(8,128)(2,1)} %constant_dynamic-update-slice_fusion, f32[2048]{0:T(1024)S(1)} %bitcast.73), kind=kLoop, calls=%fused_computation.8 | loop fusion | flops 8387584 | bytes 4206592 | tf_op jit(solution)/shard_map/reduce_sum | solution.py:70
  48.5 12.6 %multiply_subtract_fusion = f32[1024,2048]{1,0:T(8,128)S(1)} fusion(bf16[1024,2048]{1,0:T(8,128)(2,1)} %constant_dynamic-update-slice_fusion, bf16[2048,2048]{1,0:T(8,128)(2,1)} %param.6, f32[2048]{0:T(1024)S(1)} %bitcast.74, f32[2048]{0:T(1024)S(1)} %fusion.1, f32[1024]{0:T(1024)S(1)} %multiply_reduce_fusion), kind=kOutput, calls=%fused_computation.6 | convolution fusion | flops 8608808960 | bytes 20992000 | tf_op jit(solution)/shard_map/dot_general | solution.py:71
  61.1 0.0 copy-start.2
  61.1 2.4 %dynamic-slice_bitcast_fusion = f32[2,8,32,2048]{3,2,1,0:T(8,128)} fusion(f32[2,8,2,32,2048]{4,3,2,1,0:T(8,128)S(1)} %bitcast.70, s32[]{:T(128)S(6)} %select_n.157), kind=kLoop, calls=%fused_computation.10 | loop fusion | bytes 8388612 | tf_op jit(solution)/shard_map/jit(dynamic_index_in_dim)/squeeze | solution.py:79
  63.5 2.1 %copy-done.2 = f32[1024,2048]{1,0:T(8,128)} copy-done((f32[1024,2048]{1,0:T(8,128)}, f32[1024,2048]{1,0:T(8,128)S(1)}, u32[]{:S(2)}) %copy-start.2) | copy-done | bytes 8388632
  65.5 0.0 collective-permute-start.7
  65.5 7.5 %collective-permute-done.7 = f32[2,8,32,2048]{3,2,1,0:T(8,128)} collective-permute-done((f32[2,8,32,2048]{3,2,1,0:T(8,128)}, f32[2,8,32,2048]{3,2,1,0:T(8,128)}, u32[]{:S(2)}, u32[]{:S(2)}) %collective-permute-start.7) | collective-permute-done | bytes 4194336 | tf_op jit(solution)/shard_map/ppermute | solution.py:14
  73.0 4.2 %bitcast_add_fusion = f32[2,8,32,2048]{3,2,1,0:T(8,128)S(1)} fusion(f32[2,8,32,2048]{3,2,1,0:T(8,128)} %collective-permute-done.7, f32[2,8,2,32,2048]{4,3,2,1,0:T(8,128)} %bitcast.71, s32[]{:T(128)S(6)} %select_n.156), kind=kLoop, calls=%fused_computation.9 | loop fusion | flops 1048576 | bytes 12582916 | tf_op jit(solution)/shard_map/add | solution.py:80
  77.3 0.0 copy-start.1
  77.3 2.0 %copy-done.1 = f32[2,8,32,2048]{3,2,1,0:T(8,128)} copy-done((f32[2,8,32,2048]{3,2,1,0:T(8,128)}, f32[2,8,32,2048]{3,2,1,0:T(8,128)S(1)}, u32[]{:S(2)}) %copy-start.1) | copy-done | bytes 4194328
  79.2 0.1 dynamic-slice_bitcast_fusion.4
  79.4 0.1 fusion.10
  79.5 2.0 %collective-permute-start.9 = (f16[2,2,32,2048]{3,2,1,0:T(8,128)(2,1)S(1)}, f16[2,2,32,2048]{3,2,1,0:T(8,128)(2,1)S(1)}, u32[]{:S(2)}, u32[]{:S(2)}) collective-permute-start(f16[2,2,32,2048]{3,2,1,0:T(8,128)(2,1)S(1)} %fusion.10), channel_id=1, source_target_pairs={{0,2},{2,4},{4,6},{6,8},{8,10},{10,12},{12,14},{14,0},{1,3},{3,5},... | collective-permute-start | bytes 1572872 | tf_op jit(solution)/shard_map/ppermute | solution.py:14
  81.5 0.1 fusion.9
  81.6 0.2 collective-permute-start.8
  81.8 1.1 fusion.25
  82.8 5.5 %collective-permute-start.10 = (f16[32,2048]{1,0:T(8,128)(2,1)S(1)}, f16[32,2048]{1,0:T(8,128)(2,1)S(1)}, u32[]{:S(2)}, u32[]{:S(2)}) collective-permute-start(f16[32,2048]{1,0:T(8,128)(2,1)S(1)} %get-tuple-element.5), channel_id=1, source_target_pairs={{0,12},{2,14},{4,0},{6,2},{8,4},{10,6},{12,8},{14,10},{1,13},{3,15... | collective-permute-start | bytes 393224 | tf_op jit(solution)/shard_map/ppermute | solution.py:14
  88.3 0.0 collective-permute-start.12
  88.3 8.2 %collective-permute-done.9 = f16[2,2,32,2048]{3,2,1,0:T(8,128)(2,1)S(1)} collective-permute-done((f16[2,2,32,2048]{3,2,1,0:T(8,128)(2,1)S(1)}, f16[2,2,32,2048]{3,2,1,0:T(8,128)(2,1)S(1)}, u32[]{:S(2)}, u32[]{:S(2)}) %collective-permute-start.9) | collective-permute-done | bytes 524320 | tf_op jit(solution)/shard_map/ppermute | solution.py:14
  96.6 0.0 collective-permute-done.8
  96.6 1.4 %bitcast_add_fusion.2 = (f32[2,32,2048]{2,1,0:T(8,128)S(1)}, f32[2,32,2048]{2,1,0:T(8,128)S(1)}) fusion(f32[2,8,32,2048]{3,2,1,0:T(8,128)} %copy-done.1, s32[]{:T(128)S(6)} %select_n.169, f16[2,2,32,2048]{3,2,1,0:T(8,128)(2,1)S(1)} %collective-permute-done.8, f16[2,2,32,2048]{3,2,1,0:T(8,128)(2,1)S(1)} %collective-permute-done.9, s32[]{:T(128)S(6)} %select_n.173), kind=kLoop, calls=%fused_computation.23 | loop fusion | flops 786432 | bytes 2621448 | tf_op jit(solution)/shard_map/add | solution.py:52
  98.0 3.4 %collective-permute-done.10 = f16[32,2048]{1,0:T(8,128)(2,1)S(1)} collective-permute-done((f16[32,2048]{1,0:T(8,128)(2,1)S(1)}, f16[32,2048]{1,0:T(8,128)(2,1)S(1)}, u32[]{:S(2)}, u32[]{:S(2)}) %collective-permute-start.10) | collective-permute-done | bytes 131104 | tf_op jit(solution)/shard_map/ppermute | solution.py:14
  101.5 4.0 %collective-permute-start.11 = (f16[2,32,2048]{2,1,0:T(8,128)(2,1)S(1)}, f16[2,32,2048]{2,1,0:T(8,128)(2,1)S(1)}, u32[]{:S(2)}, u32[]{:S(2)}) collective-permute-start(f16[2,32,2048]{2,1,0:T(8,128)(2,1)S(1)} %fusion.12), channel_id=1, source_target_pairs={{0,12},{2,14},{4,0},{6,2},{8,4},{10,6},{12,8},{14,10},{1,13},{3,15... | collective-permute-start | bytes 786440 | tf_op jit(solution)/shard_map/ppermute | solution.py:14
  105.5 0.0 collective-permute-done.12
  105.6 1.1 collective-permute-start.13
  106.8 7.4 %collective-permute-done.11 = f16[2,32,2048]{2,1,0:T(8,128)(2,1)S(1)} collective-permute-done((f16[2,32,2048]{2,1,0:T(8,128)(2,1)S(1)}, f16[2,32,2048]{2,1,0:T(8,128)(2,1)S(1)}, u32[]{:S(2)}, u32[]{:S(2)}) %collective-permute-start.11) | collective-permute-done | bytes 262176 | tf_op jit(solution)/shard_map/ppermute | solution.py:14
  114.2 4.0 %collective-permute-done.13 = f16[2,32,2048]{2,1,0:T(8,128)(2,1)S(1)} collective-permute-done((f16[2,32,2048]{2,1,0:T(8,128)(2,1)S(1)}, f16[2,32,2048]{2,1,0:T(8,128)(2,1)S(1)}, u32[]{:S(2)}, u32[]{:S(2)}) %collective-permute-start.13) | collective-permute-done | bytes 262176 | tf_op jit(solution)/shard_map/ppermute | solution.py:14
  118.2 1.3 %fusion.15 = f32[2,32,2048]{2,1,0:T(8,128)S(1)} fusion(f16[2,32,2048]{2,1,0:T(8,128)(2,1)S(1)} %collective-permute-done.13, f16[2,32,2048]{2,1,0:T(8,128)(2,1)S(1)} %collective-permute-done.11, f32[2,8,32,2048]{3,2,1,0:T(8,128)} %copy-done.1, s32[]{:T(128)S(6)} %select_n.159, f16[2,2,32,2048]{3,2,1,0:T(8,128)(2,1)S(1)} %collective-permute-done.9, ...), kind=kLoop, calls=%fused_computation.26 | loop fusion | flops 1572864 | bytes 2097156 | tf_op jit(solution)/shard_map/add | solution.py:58
  119.5 0.7 collective-permute-start.14
  120.9 5.1 %collective-permute-done.14 = f32[32,2048]{1,0:T(8,128)S(1)} collective-permute-done((f32[32,2048]{1,0:T(8,128)S(1)}, f32[32,2048]{1,0:T(8,128)S(1)}, u32[]{:S(2)}, u32[]{:S(2)}) %collective-permute-start.14) | collective-permute-done | bytes 262176 | tf_op jit(solution)/shard_map/ppermute | solution.py:14
  125.9 0.8 fusion.24
  (7 shorter events, 0.2 us)
Async XLA Ops:
  0.0 8.3 %copy-start = (f32[256]{0:T(256)S(1)}, f32[256]{0:T(256)}, u32[]{:S(2)}) copy-start(f32[256]{0:T(256)} %param.8) | copy-start | bytes 3076
  0.0 19.0 %collective-permute-start = (bf16[128,2048]{1,0:T(8,128)(2,1)}, bf16[128,2048]{1,0:T(8,128)(2,1)S(1)}, u32[]{:S(2)}, u32[]{:S(2)}) collective-permute-start(bf16[128,2048]{1,0:T(8,128)(2,1)} %param.5), channel_id=1, source_target_pairs={{0,32},{32,0},{1,33},{33,1},{2,34},{34,2},{3,35},{35,3},{4,36},{36... | collective-permute-start | bytes 1572872 | tf_op jit(solution)/shard_map/ppermute | solution.py:14
  3.2 29.7 %collective-permute-start.1 = (bf16[128,2048]{1,0:T(8,128)(2,1)}, bf16[128,2048]{1,0:T(8,128)(2,1)S(1)}, u32[]{:S(2)}, u32[]{:S(2)}) collective-permute-start(bf16[128,2048]{1,0:T(8,128)(2,1)} %param.5), channel_id=1, source_target_pairs={{0,64},{64,128},{128,192},{192,0},{1,65},{65,129},{129,193},{193,1... | collective-permute-start | bytes 1572872 | tf_op jit(solution)/shard_map/ppermute | solution.py:14
  4.7 29.1 %collective-permute-start.2 = (bf16[128,2048]{1,0:T(8,128)(2,1)}, bf16[128,2048]{1,0:T(8,128)(2,1)S(1)}, u32[]{:S(2)}, u32[]{:S(2)}) collective-permute-start(bf16[128,2048]{1,0:T(8,128)(2,1)} %param.5), channel_id=1, source_target_pairs={{0,192},{64,0},{128,64},{192,128},{1,193},{65,1},{129,65},{193,129... | collective-permute-start | bytes 1572872 | tf_op jit(solution)/shard_map/ppermute | solution.py:14
  6.4 25.3 %collective-permute-start.3 = (bf16[128,2048]{1,0:T(8,128)(2,1)}, bf16[128,2048]{1,0:T(8,128)(2,1)S(1)}, u32[]{:S(2)}, u32[]{:S(2)}) collective-permute-start(bf16[128,2048]{1,0:T(8,128)(2,1)} %param.5), channel_id=1, source_target_pairs={{0,128},{64,192},{128,0},{192,64},{1,129},{65,193},{129,1},{193,65... | collective-permute-start | bytes 1572872 | tf_op jit(solution)/shard_map/ppermute | solution.py:14
  15.7 2.5 %copy-start.3 = (bf16[128,2048]{1,0:T(8,128)(2,1)S(1)}, bf16[128,2048]{1,0:T(8,128)(2,1)}, u32[]{:S(2)}) copy-start(bf16[128,2048]{1,0:T(8,128)(2,1)} %param.5) | copy-start | bytes 1572868
  19.0 22.4 %collective-permute-start.4 = (bf16[128,2048]{1,0:T(8,128)(2,1)S(1)}, bf16[128,2048]{1,0:T(8,128)(2,1)S(1)}, u32[]{:S(2)}, u32[]{:S(2)}) collective-permute-start(bf16[128,2048]{1,0:T(8,128)(2,1)S(1)} %collective-permute-done), channel_id=1, source_target_pairs={{0,64},{64,128},{128,192},{192,0},{1,65},{65,129},{129,193},{193,1... | collective-permute-start | bytes 1572872 | tf_op jit(solution)/shard_map/ppermute | solution.py:14
  19.7 22.6 %collective-permute-start.5 = (bf16[128,2048]{1,0:T(8,128)(2,1)S(1)}, bf16[128,2048]{1,0:T(8,128)(2,1)S(1)}, u32[]{:S(2)}, u32[]{:S(2)}) collective-permute-start(bf16[128,2048]{1,0:T(8,128)(2,1)S(1)} %collective-permute-done), channel_id=1, source_target_pairs={{0,192},{64,0},{128,64},{192,128},{1,193},{65,1},{129,65},{193,129... | collective-permute-start | bytes 1572872 | tf_op jit(solution)/shard_map/ppermute | solution.py:14
  31.7 12.5 %collective-permute-start.6 = (bf16[128,2048]{1,0:T(8,128)(2,1)S(1)}, bf16[128,2048]{1,0:T(8,128)(2,1)S(1)}, u32[]{:S(2)}, u32[]{:S(2)}) collective-permute-start(bf16[128,2048]{1,0:T(8,128)(2,1)S(1)} %collective-permute-done.3), channel_id=1, source_target_pairs={{0,32},{32,0},{1,33},{33,1},{2,34},{34,2},{3,35},{35,3},{4,36},{36... | collective-permute-start | bytes 1572872 | tf_op jit(solution)/shard_map/ppermute | solution.py:14
  61.1 4.5 %copy-start.2 = (f32[1024,2048]{1,0:T(8,128)}, f32[1024,2048]{1,0:T(8,128)S(1)}, u32[]{:S(2)}) copy-start(f32[1024,2048]{1,0:T(8,128)S(1)} %multiply_subtract_fusion) | copy-start | bytes 25165828
  65.5 7.5 %collective-permute-start.7 = (f32[2,8,32,2048]{3,2,1,0:T(8,128)}, f32[2,8,32,2048]{3,2,1,0:T(8,128)}, u32[]{:S(2)}, u32[]{:S(2)}) collective-permute-start(f32[2,8,32,2048]{3,2,1,0:T(8,128)} %dynamic-slice_bitcast_fusion), channel_id=1, source_target_pairs={{0,1},{1,0},{2,3},{3,2},{4,5},{5,4},{6,7},{7,6},{8,9},{9,8},{10,11... | collective-permute-start | bytes 12582920 | tf_op jit(solution)/shard_map/ppermute | solution.py:14
  77.3 2.0 %copy-start.1 = (f32[2,8,32,2048]{3,2,1,0:T(8,128)}, f32[2,8,32,2048]{3,2,1,0:T(8,128)S(1)}, u32[]{:S(2)}) copy-start(f32[2,8,32,2048]{3,2,1,0:T(8,128)S(1)} %bitcast_add_fusion) | copy-start | bytes 12582916
  79.5 17.1 %collective-permute-start.9 = (f16[2,2,32,2048]{3,2,1,0:T(8,128)(2,1)S(1)}, f16[2,2,32,2048]{3,2,1,0:T(8,128)(2,1)S(1)}, u32[]{:S(2)}, u32[]{:S(2)}) collective-permute-start(f16[2,2,32,2048]{3,2,1,0:T(8,128)(2,1)S(1)} %fusion.10), channel_id=1, source_target_pairs={{0,2},{2,4},{4,6},{6,8},{8,10},{10,12},{12,14},{14,0},{1,3},{3,5},... | collective-permute-start | bytes 1572872 | tf_op jit(solution)/shard_map/ppermute | solution.py:14
  81.6 15.0 %collective-permute-start.8 = (f16[2,2,32,2048]{3,2,1,0:T(8,128)(2,1)S(1)}, f16[2,2,32,2048]{3,2,1,0:T(8,128)(2,1)S(1)}, u32[]{:S(2)}, u32[]{:S(2)}) collective-permute-start(f16[2,2,32,2048]{3,2,1,0:T(8,128)(2,1)S(1)} %fusion.9), channel_id=1, source_target_pairs={{0,14},{2,0},{4,2},{6,4},{8,6},{10,8},{12,10},{14,12},{1,15},{3,1}... | collective-permute-start | bytes 1572872 | tf_op jit(solution)/shard_map/ppermute | solution.py:14
  82.8 18.6 %collective-permute-start.10 = (f16[32,2048]{1,0:T(8,128)(2,1)S(1)}, f16[32,2048]{1,0:T(8,128)(2,1)S(1)}, u32[]{:S(2)}, u32[]{:S(2)}) collective-permute-start(f16[32,2048]{1,0:T(8,128)(2,1)S(1)} %get-tuple-element.5), channel_id=1, source_target_pairs={{0,12},{2,14},{4,0},{6,2},{8,4},{10,6},{12,8},{14,10},{1,13},{3,15... | collective-permute-start | bytes 393224 | tf_op jit(solution)/shard_map/ppermute | solution.py:14
  88.3 17.2 %collective-permute-start.12 = (f16[32,2048]{1,0:T(8,128)(2,1)S(1)}, f16[32,2048]{1,0:T(8,128)(2,1)S(1)}, u32[]{:S(2)}, u32[]{:S(2)}) collective-permute-start(f16[32,2048]{1,0:T(8,128)(2,1)S(1)} %get-tuple-element.6), channel_id=1, source_target_pairs={{0,4},{2,6},{4,8},{6,10},{8,12},{10,14},{12,0},{14,2},{1,5},{3,7},... | collective-permute-start | bytes 393224 | tf_op jit(solution)/shard_map/ppermute | solution.py:14
  101.5 12.7 %collective-permute-start.11 = (f16[2,32,2048]{2,1,0:T(8,128)(2,1)S(1)}, f16[2,32,2048]{2,1,0:T(8,128)(2,1)S(1)}, u32[]{:S(2)}, u32[]{:S(2)}) collective-permute-start(f16[2,32,2048]{2,1,0:T(8,128)(2,1)S(1)} %fusion.12), channel_id=1, source_target_pairs={{0,12},{2,14},{4,0},{6,2},{8,4},{10,6},{12,8},{14,10},{1,13},{3,15... | collective-permute-start | bytes 786440 | tf_op jit(solution)/shard_map/ppermute | solution.py:14
  105.6 12.5 %collective-permute-start.13 = (f16[2,32,2048]{2,1,0:T(8,128)(2,1)S(1)}, f16[2,32,2048]{2,1,0:T(8,128)(2,1)S(1)}, u32[]{:S(2)}, u32[]{:S(2)}) collective-permute-start(f16[2,32,2048]{2,1,0:T(8,128)(2,1)S(1)} %fusion.13), channel_id=1, source_target_pairs={{0,4},{2,6},{4,8},{6,10},{8,12},{10,14},{12,0},{14,2},{1,5},{3,7},... | collective-permute-start | bytes 786440 | tf_op jit(solution)/shard_map/ppermute | solution.py:14
  119.5 6.5 %collective-permute-start.14 = (f32[32,2048]{1,0:T(8,128)S(1)}, f32[32,2048]{1,0:T(8,128)S(1)}, u32[]{:S(2)}, u32[]{:S(2)}) collective-permute-start(f32[32,2048]{1,0:T(8,128)S(1)} %dynamic-slice_bitcast_fusion.5), channel_id=1, source_target_pairs={{0,16},{16,0},{1,17},{17,1},{2,18},{18,2},{3,19},{19,3},{4,20},{20... | collective-permute-start | bytes 786440 | tf_op jit(solution)/shard_map/ppermute | solution.py:14

commit v2 on v0

v2 whole, which is shorter than its diff:
```python
import functools

import jax
import jax.numpy as jnp
from jax import lax
from jax.experimental import pallas as pl
from jax.experimental.pallas import tpu as pltpu
from jax.sharding import Mesh, PartitionSpec as P

X, YH, YL, Z, CORE = 4, 2, 2, 8, 2
SCALE = 2.0 ** -17
COEF = ("yl", "z", "core")
SNAP = ("x", "yh")
GROUP = 32
CUT = GROUP // 2
KEPT = 2 * GROUP
EARLY = ((0, 0), (0, 1), (-1, 0), (1, 0))
LATE = ((2, 0), (2, 1), (-1, 1), (1, 1))
TILE = 256
VMEM = pl.BlockSpec(memory_space=pltpu.VMEM)
SMEM = pl.BlockSpec(memory_space=pltpu.SMEM)


def shift(value, axis, by):
    size = {"x": X, "yh": YH, "yl": YL, "z": Z, "core": CORE}[axis]
    return lax.ppermute(value, axis, [(i, (i + by) % size) for i in range(size)])


def pack(value):
    return (value * SCALE).astype(jnp.float16)


def unpack(value):
    return value.astype(jnp.float32) * (1.0 / SCALE)


def params(mib):
    return pltpu.CompilerParams(vmem_limit_bytes=mib * 2**20)


def cost(flops, moved):
    return pl.CostEstimate(flops=flops, bytes_accessed=moved, transcendentals=0)


def prepare_kernel(weight, slab, weighted, norm):
    wide = slab[...].astype(jnp.float32)
    scaled = wide * weight[...]
    weighted[...] = scaled.astype(jnp.bfloat16)
    total = jnp.sum(scaled * wide, axis=1, keepdims=True)
    norm[...] = jnp.transpose(jnp.broadcast_to(total, (total.shape[0], 128)))[0:1, :]


def prepare(weight, slab):
    rows, depth = slab.shape
    return pl.pallas_call(
        prepare_kernel,
        grid=(rows // TILE,),
        in_specs=[
            pl.BlockSpec((1, depth), lambda i: (0, 0)),
            pl.BlockSpec((TILE, depth), lambda i: (i, 0)),
        ],
        out_specs=[
            pl.BlockSpec((TILE, depth), lambda i: (i, 0)),
            pl.BlockSpec((1, TILE), lambda i: (0, i)),
        ],
        out_shape=[
            jax.ShapeDtypeStruct((rows, depth), jnp.bfloat16),
            jax.ShapeDtypeStruct((1, rows), jnp.float32),
        ],
        compiler_params=params(12),
        cost_estimate=cost(0, 2**20),
        name="prepare",
    )(weight, slab)


def row_offset(place, offset, low):
    source_x = lax.rem(place[0] + offset[0] + X, X)
    source_yh = lax.rem(place[1] + offset[1], YH)
    yl_from_here = lax.rem(source_x // 2 + place[2], YL)
    z_to = lax.rem(source_x, 2) * 4 + source_yh * 2 + low
    z_from_here = lax.rem(z_to - place[3] + Z, Z)
    return pl.multiple_of((yl_from_here * Z + z_from_here) * GROUP, GROUP)


def early_kernel(offsets, place, weight, slab_norm, slab, *refs):
    count = len(offsets)
    blocks, (other, held, rows, norms) = refs[:count], refs[count:]
    for half in range(CORE):
        for i, block in enumerate(blocks):
            at = pl.ds((half * count + i) * KEPT, KEPT)
            piece = block[half * KEPT : (half + 1) * KEPT, :]
            rows[at, :] = piece
            wide = piece.astype(jnp.float32)
            norms[at, :] = jnp.sum(wide * wide * weight[...], axis=1, keepdims=True)

    @pl.loop(0, slab.shape[0] // TILE)
    def _(n):
        at = pl.ds(pl.multiple_of(n * TILE, TILE), TILE)
        gram = lax.dot_general(
            rows[...], slab[at, :], (((1,), (1,)), ((), ())), preferred_element_type=jnp.float32
        )
        value = norms[...] + slab_norm[:, at] - 2.0 * gram
        other[:, at] = value[: count * KEPT]
        for i, offset in enumerate(offsets):
            for low in range(2):
                start = (count + i) * KEPT + low * GROUP
                held[pl.ds(row_offset(place, offset, low), GROUP), at] = value[start : start + GROUP]


def early_partial(offsets, place, weight, slab_norm, slab, blocks, estimate):
    columns, depth = slab.shape
    kept = len(offsets) * KEPT
    arguments = [place, weight, slab_norm, slab, *blocks]
    return pl.pallas_call(
        functools.partial(early_kernel, offsets),
        in_specs=[SMEM] + [VMEM] * (len(arguments) - 1),
        out_specs=[VMEM, VMEM],
        out_shape=[
            jax.ShapeDtypeStruct((kept, columns), jnp.float32),
            jax.ShapeDtypeStruct((YL * Z * GROUP, columns), jnp.float32),
        ],
        scratch_shapes=[
            pltpu.VMEM((kept * CORE, depth), jnp.bfloat16),
            pltpu.VMEM((kept * CORE, 1), jnp.float32),
        ],
        compiler_params=params(24),
        cost_estimate=estimate,
        name="early_partial",
    )(*arguments)


def add_kernel(offsets, count, place, *refs):
    parts, more, (held, out) = refs[:count], refs[count:-2], refs[-2:]
    for i, offset in enumerate(offsets):
        for low in range(2):
            start = (i * 2 + low) * GROUP
            at = pl.ds(row_offset(place, offset, low), GROUP)
            total = more[0][start : start + GROUP, :] if more else held[at, :]
            part, start = (parts[0], start) if count == 1 else (parts[i], low * GROUP)
            out[at, :] = total + part[start : start + GROUP, :]


def add_into(offsets, place, parts, mine, held, estimate):
    more = [] if mine is None else [mine]
    count = len(parts) + len(more)
    return pl.pallas_call(
        functools.partial(add_kernel, offsets, len(parts)),
        in_specs=[SMEM] + [VMEM] * (count + 1),
        out_specs=VMEM,
        out_shape=jax.ShapeDtypeStruct(held.shape, held.dtype),
        input_output_aliases={count + 1: 0},
        compiler_params=params(16),
        cost_estimate=estimate,
        name="add_into",
    )(place, *parts, *more, held)


def body(queries, slab, degree, degree_weight, spread):
    x, yh, yl, z, core = (lax.axis_index(a) for a in ("x", "yh", "yl", "z", "core"))
    columns, depth = slab.shape

    own = queries.reshape(2, CORE, GROUP, depth)
    own = jnp.concatenate(
        [lax.dynamic_index_in_dim(own, c, 1, keepdims=False).reshape(-1, depth) for c in (1 - core, core)]
    )
    pair = shift(own, "yh", 1)
    far = shift(own, "x", 2)
    left, right = shift(own, "x", 1), shift(own, "x", -1)

    levels = jnp.arange(degree_weight.shape[0], dtype=jnp.int32)
    one_hot_table = (degree[:, None] == levels[None, :]).astype(jnp.float32)
    weight_of = jnp.dot(one_hot_table, degree_weight, precision=lax.Precision.HIGHEST)[None, :]
    weighted_slab, slab_norm = prepare(weight_of, slab)

    pair_left, pair_right = shift(pair, "x", 1), shift(pair, "x", -1)
    pair_far = shift(far, "yh", 1)

    place = jnp.stack([x, yh, yl, z]).astype(jnp.int32)
    small = cost(0, 2**16)
    early_other, held = early_partial(
        EARLY, place, weight_of, slab_norm, weighted_slab, [own, pair, left, right], cost(3 * 10**10, 2**16)
    )
    pieces = [shift(early_other, "core", 1)]
    held = add_into(EARLY, place, pieces, None, held, small)

    def partial(blocks):
        rows = jnp.concatenate(blocks)
        wide = rows.astype(jnp.float32)
        norm = jnp.sum(wide * wide * weight_of, axis=1)
        gram = lax.dot_general(
            rows, weighted_slab, (((1,), (1,)), ((), ())), preferred_element_type=jnp.float32
        )
        return norm[:, None] + slab_norm - 2.0 * gram

    late = lax.optimization_barrier((far, pair_far, pair_left, pair_right, early_other))[:4]
    late_other = shift(partial([b[:KEPT] for b in late]), "core", 1)
    late_mine = partial([b[KEPT:] for b in late])
    held = add_into(LATE, place, [late_other], late_mine, held, small)

    held = held.reshape(YL, Z, GROUP, columns)

    def second(k):
        return held[:, k % Z, CUT:]

    across = shift(pack(held[1, :, :CUT]), "yl", 1)
    minus = shift(pack(jnp.stack([second(-1), second(-3)])), "z", -1)
    plus = shift(pack(jnp.stack([second(1), second(3)])), "z", 1)
    opposite = shift(pack(second(4)), "z", -2)

    def first(k):
        return held[0, k % Z, :CUT] + unpack(across[k % Z])

    minus_first = shift(pack(jnp.stack([first(-1), first(-3)])), "z", -1)
    plus_first = shift(pack(jnp.stack([first(1), first(3)])), "z", 1)
    sum_minus = second(-2) + unpack(minus[1]) + unpack(opposite)
    sum_plus = second(2) + unpack(plus[1])
    last_minus = shift(pack(sum_minus), "z", -2)
    last_plus = shift(jnp.concatenate([pack(sum_plus), pack(first(4))[None]]), "z", 2)

    second_sum = second(0) + unpack(minus[0]) + unpack(plus[0]) + unpack(last_minus) + unpack(last_plus[:2])
    second_sum = second_sum[0] + shift(second_sum[1], "yl", 1)

    first_minus = first(-2) + unpack(minus_first[1])
    first_plus = first(2) + unpack(plus_first[1]) + unpack(last_plus[2])
    end_minus = shift(pack(first_minus), "z", -2)
    end_plus = shift(pack(first_plus), "z", 2)
    first_sum = first(0) + unpack(minus_first[0]) + unpack(plus_first[0]) + unpack(end_minus) + unpack(end_plus)

    distance = jnp.concatenate([first_sum, second_sum], axis=0)
    return jnp.exp(-distance / spread[0])


def solution(mesh):
    fine = Mesh(mesh.devices.reshape(X, YH, YL, Z, CORE), ("x", "yh", "yl", "z", "core"))
    placed = (P(SNAP, COEF), P(SNAP, COEF), P(COEF), P(), P())
    return jax.shard_map(
        body, mesh=fine, in_specs=placed, out_specs=P(COEF, SNAP), check_vma=False
    )
```

time: 250 us -> 94.8 us (0.38); the launches traced: 245 us -> 94.7 us
  waiting for transfers between devices: 124 us -> 36.9 us
  blocking collectives: 73.8 us -> 0 us
  starting transfers between devices: 0.04 us -> 31.3 us
  between operations: 14.1 us -> 0.84 us
  Pallas kernels: 0 us -> 12.6 us
  matrix products: 16.2 us -> 5.91 us
  other arithmetic: 7.66 us -> 2.39 us
  local copies, waits for them, and re-layouts: 9.55 us -> 4.68 us
    all_gather x1 -> x0, waiting for transfers between devices: 80.2 us -> none  [body(): lax.all_gather(queries, 'snap', axis=0, tiled=True)]
    psum x1 -> x0, blocking collectives: 53.6 us -> none  [body(): slab_norm, query_local = lax.psum((slab_part, query_part), 'coef')]
    reduce_scatter x1 -> x0, waiting for transfers between devices: 42.8 us -> none  [body(): lax.psum_scatter(partial_value, 'coef', scatter_dimension=0, tiled=True)]
    ppermute x0 -> x20, waiting for transfers between devices: none -> 36.9 us  [shift(): lax.ppermute(value, axis, [(i, (i + by) % size) for i in range(size)])]
    ppermute x0 -> x20, starting transfers between devices: none -> 31.3 us  [shift(): lax.ppermute(value, axis, [(i, (i + by) % size) for i in range(size)])]
    all_gather x1 -> x0, blocking collectives: 20.2 us -> none  [body(): query_norm = lax.all_gather(query_local, 'snap', axis=0, tiled=True)]
    pallas_call x0 -> x4, Pallas kernels: none -> 12.6 us  [the longest x1 7.19 us: early_partial(): pl.pallas_call(functools.partial(early_kernel, offsets), in_specs=[SMEM]...]
    dot_general x1 -> x2, matrix products: 14.5 us -> 4.87 us  [partial(): lax.dot_general(rows, weighted_slab, (((1,), (1,)), ((), ())), preferred_...]
  transfers between devices with their start and end apart: 2 -> 20, of which waited for: 2 -> 12; matrix products, arithmetic and copies ran while one was open for 3% -> 8% of each run, Pallas kernels for 0% -> 13%
where the time goes in v2:
time: 94.8 us; the launch traced here: 94.7 us
  waiting for transfers between devices  36.9 us (39%)
  starting transfers between devices  31.3 us (33%)
  Pallas kernels  12.6 us (13%)
  matrix products  5.91 us (6%)
  local copies, waits for them, and re-layouts  4.68 us (5%)
  other arithmetic  2.39 us (3%)
    ppermute x20, waiting for transfers between devices, shift(): lax.ppermute(value, axis, [(i, (i + by) % size) for i in range(size)])  36.9 us
    ppermute x20, starting transfers between devices, shift(): lax.ppermute(value, axis, [(i, (i + by) % size) for i in range(size)])  31.3 us
    pallas_call x1, Pallas kernels, early_partial(): pl.pallas_call(functools.partial(early_kernel, offsets), in_specs=[SMEM]...  7.19 us
    dot_general x2, matrix products, partial(): lax.dot_general(rows, weighted_slab, (((1,), (1,)), ((), ())), preferred_...  4.87 us
    pallas_call x1, Pallas kernels, prepare(): pl.pallas_call(prepare_kernel, grid=(rows // TILE,), in_specs=[pl.BlockSp...  3.87 us
    unnamed x6, local copies, waits for them, and re-layouts  3.41 us
  transfers between devices with their start and end apart: 20, of which 12 were waited for; matrix products, arithmetic and copies ran while one was open for 8% of the time, Pallas kernels for 13%

profile of v2, /device:TPU:32, one launch (start us, length us, event | category | flops | bytes accessed | tf_op | source)
XLA Modules:
  0.0 94.7 jit_solution(17563731757790325434)
XLA Ops:
  0.0 0.0 copy-start
  0.0 1.1 %constant_dynamic-slice_fusion.1 = (bf16[2,1,32,2048]{3,2,1,0:T(8,128)(2,1)S(1)}, bf16[2,1,32,2048]{3,2,1,0:T(8,128)(2,1)S(1)}) fusion(bf16[2,2,32,2048]{3,2,1,0:T(8,128)(2,1)} %bitcast.171, s32[]{:T(128)S(6)} %select_n.7, s32[]{:T(128)S(6)} %select_n.8), kind=kLoop, calls=%fused_computation.82 | loop fusion | bytes 1048584 | tf_op jit(solution)/shard_map/jit(dynamic_index_in_dim)/dynamic_slice | solution.py:164
  1.2 3.3 %collective-permute-start.2 = (bf16[128,2048]{1,0:T(8,128)(2,1)S(1)}, bf16[128,2048]{1,0:T(8,128)(2,1)S(1)}, u32[]{:S(2)}, u32[]{:S(2)}) collective-permute-start(bf16[128,2048]{1,0:T(8,128)(2,1)S(1)} %pad_maximum_fusion.2.refs_0_), channel_id=1, source_target_pairs={{0,32},{32,0},{1,33},{33,1},{2,34},{34,2},{3,35},{35,3},{4,36},{36... | collective-permute-start | bytes 1572872 | tf_op jit(solution)/shard_map/ppermute | solution.py:26
  4.4 3.0 %collective-permute-start = (bf16[128,2048]{1,0:T(8,128)(2,1)S(1)}, bf16[128,2048]{1,0:T(8,128)(2,1)S(1)}, u32[]{:S(2)}, u32[]{:S(2)}) collective-permute-start(bf16[128,2048]{1,0:T(8,128)(2,1)S(1)} %pad_maximum_fusion.2.refs_0_), channel_id=1, source_target_pairs={{0,128},{64,192},{128,0},{192,64},{1,129},{65,193},{129,1},{193,65... | collective-permute-start | bytes 1572872 | tf_op jit(solution)/shard_map/ppermute | solution.py:26
  7.5 1.1 %collective-permute-start.6 = (bf16[128,2048]{1,0:T(8,128)(2,1)S(1)}, bf16[128,2048]{1,0:T(8,128)(2,1)S(1)}, u32[]{:S(2)}, u32[]{:S(2)}) collective-permute-start(bf16[128,2048]{1,0:T(8,128)(2,1)S(1)} %pad_maximum_fusion.2.refs_0_), channel_id=1, source_target_pairs={{0,192},{64,0},{128,64},{192,128},{1,193},{65,1},{129,65},{193,129... | collective-permute-start | bytes 1572872 | tf_op jit(solution)/shard_map/ppermute | solution.py:26
  8.6 0.9 collective-permute-start.5
  9.5 0.0 copy-done
  9.5 0.0 copy-done.2
  9.5 1.0 %fusion.2.weight = f32[1,2048]{1,0:T(1,128)S(1)} fusion(f32[256,1]{0,1:T(1,128)S(1)} %bitcast.158, s32[2048]{0:T(1024)S(1)} %copy-done.2), kind=kOutput, calls=%fused_computation.7 | convolution fusion | flops 6815744 | bytes 17408 | tf_op jit(solution)/shard_map/dot_general | solution.py:172
  10.5 3.4 %copy-done.1 = bf16[2048,2048]{1,0:T(8,128)(2,1)S(1)} copy-done((bf16[2048,2048]{1,0:T(8,128)(2,1)S(1)}, bf16[2048,2048]{1,0:T(8,128)(2,1)}, u32[]{:S(2)}) %copy-start.1) | copy-done | bytes 8388632
  13.9 3.9 %prepare.1 = (bf16[2048,2048]{1,0:T(8,128)(2,1)S(1)}, f32[1,2048]{1,0:T(1,128)S(1)}) custom-call(f32[1,2048]{1,0:T(1,128)S(1)} %fusion.2.weight, bf16[2048,2048]{1,0:T(8,128)(2,1)S(1)} %copy-done.1), custom_call_target="tpu_custom_call" | custom-call | bytes 1048576 | tf_op jit(solution)/shard_map/prepare/pallas_call | solution.py:55
  17.8 0.1 pad_add_fusion.place
  17.9 0.0 collective-permute-done.2.refs_1_
  17.9 2.4 %collective-permute-start.4 = (bf16[128,2048]{1,0:T(8,128)(2,1)S(1)}, bf16[128,2048]{1,0:T(8,128)(2,1)S(1)}, u32[]{:S(2)}, u32[]{:S(2)}) collective-permute-start(bf16[128,2048]{1,0:T(8,128)(2,1)S(1)} %collective-permute-done.2.refs_1_), channel_id=1, source_target_pairs={{0,192},{64,0},{128,64},{192,128},{1,193},{65,1},{129,65},{193,129... | collective-permute-start | bytes 1572872 | tf_op jit(solution)/shard_map/ppermute | solution.py:26
  20.3 0.0 collective-permute-start.3
  20.3 0.5 collective-permute-done
  20.8 1.5 %collective-permute-start.1 = (bf16[128,2048]{1,0:T(8,128)(2,1)S(1)}, bf16[128,2048]{1,0:T(8,128)(2,1)S(1)}, u32[]{:S(2)}, u32[]{:S(2)}) collective-permute-start(bf16[128,2048]{1,0:T(8,128)(2,1)S(1)} %collective-permute-done), channel_id=1, source_target_pairs={{0,32},{32,0},{1,33},{33,1},{2,34},{34,2},{3,35},{35,3},{4,36},{36... | collective-permute-start | bytes 1572872 | tf_op jit(solution)/shard_map/ppermute | solution.py:26
  22.4 9.8 %collective-permute-done.6.refs_3_ = bf16[128,2048]{1,0:T(8,128)(2,1)S(1)} collective-permute-done((bf16[128,2048]{1,0:T(8,128)(2,1)S(1)}, bf16[128,2048]{1,0:T(8,128)(2,1)S(1)}, u32[]{:S(2)}, u32[]{:S(2)}) %collective-permute-start.6) | collective-permute-done | bytes 524320 | tf_op jit(solution)/shard_map/ppermute | solution.py:26
  32.2 0.0 collective-permute-done.5.refs_2_
  32.2 7.2 %early_partial.1 = (f32[256,2048]{1,0:T(8,128)S(1)}, f32[512,2048]{1,0:T(8,128)S(1)}) custom-call(s32[4]{0:T(128)S(1)} %pad_add_fusion.place, f32[1,2048]{1,0:T(1,128)S(1)} %fusion.2.weight, f32[1,2048]{1,0:T(1,128)S(1)} %get-tuple-element.13.slab_norm, bf16[2048,2048]{1,0:T(8,128)(2,1)S(1)} %get-tuple-element.14.slab, ...), custom_call_target="tpu_custom_call" | custom-call | flops 30000001024 | bytes 65536 | tf_op jit(solution)/shard_map/early_partial/pallas_call | solution.py:114
  39.4 0.1 collective-permute-start.8
  39.5 2.5 %collective-permute-done.4 = bf16[128,2048]{1,0:T(8,128)(2,1)S(1)} collective-permute-done((bf16[128,2048]{1,0:T(8,128)(2,1)S(1)}, bf16[128,2048]{1,0:T(8,128)(2,1)S(1)}, u32[]{:S(2)}, u32[]{:S(2)}) %collective-permute-start.4) | collective-permute-done | bytes 524320 | tf_op jit(solution)/shard_map/ppermute | solution.py:26
  41.9 0.0 collective-permute-done.3
  41.9 0.0 collective-permute-done.1
  41.9 0.1 fusion.49
  42.0 0.1 fusion.51
  42.1 0.6 multiply_reduce_fusion
  42.7 2.4 %fusion = f32[256,2048]{1,0:T(8,128)S(1)} fusion(bf16[2048,2048]{1,0:T(8,128)(2,1)S(1)} %get-tuple-element.14.slab, f32[2048]{0:T(1024)S(1)} %bitcast.167, f32[256]{0:T(256)S(1)} %get-tuple-element.22, bf16[64,2048]{1,0:T(8,128)(2,1)S(1)} %get-tuple-element.50, bf16[64,2048]{1,0:T(8,128)(2,1)S(1)} %get-tuple-element.41, ...), kind=kOutput, calls=%fused_computation.2 | convolution fusion | flops 2153250816 | bytes 11543552 | tf_op jit(solution)/shard_map/dot_general | solution.py:190
  45.2 0.3 collective-permute-start.7
  45.5 2.4 %fusion.1.refs_1_ = f32[256,2048]{1,0:T(8,128)S(1)} fusion(bf16[2048,2048]{1,0:T(8,128)(2,1)S(1)} %get-tuple-element.14.slab, f32[256]{0:T(256)S(1)} %get-tuple-element.21, f32[2048]{0:T(1024)S(1)} %bitcast.168, bf16[64,2048]{1,0:T(8,128)(2,1)S(1)} %get-tuple-element.49, bf16[64,2048]{1,0:T(8,128)(2,1)S(1)} %get-tuple-element.42, ...), kind=kOutput, calls=%fused_computation.3 | convolution fusion | flops 2153250816 | bytes 11543552 | tf_op jit(solution)/shard_map/dot_general | solution.py:190
  47.9 0.0 collective-permute-done.8.refs_0_
  47.9 0.8 add_into.2.refs_2_
  48.7 0.9 collective-permute-done.7.refs_0_
  49.6 0.8 add_into.3
  50.4 0.1 slice_bitcast_fusion.5
  50.5 5.5 %collective-permute-start.17 = (f16[2,16,2048]{2,1,0:T(8,128)(2,1)S(1)}, f16[2,16,2048]{2,1,0:T(8,128)(2,1)S(1)}, u32[]{:S(2)}, u32[]{:S(2)}) collective-permute-start(f16[2,16,2048]{2,1,0:T(8,128)(2,1)S(1)} %get-tuple-element.35), channel_id=1, source_target_pairs={{0,12},{2,14},{4,0},{6,2},{8,4},{10,6},{12,8},{14,10},{1,13},{3,15... | collective-permute-start | bytes 393224 | tf_op jit(solution)/shard_map/ppermute | solution.py:26
  56.0 1.1 %collective-permute-start.16 = (f16[2,2,16,2048]{3,2,1,0:T(8,128)(2,1)S(1)}, f16[2,2,16,2048]{3,2,1,0:T(8,128)(2,1)S(1)}, u32[]{:S(2)}, u32[]{:S(2)}) collective-permute-start(f16[2,2,16,2048]{3,2,1,0:T(8,128)(2,1)S(1)} %fusion.7), channel_id=1, source_target_pairs={{0,14},{2,0},{4,2},{6,4},{8,6},{10,8},{12,10},{14,12},{1,15},{3,1}... | collective-permute-start | bytes 786440 | tf_op jit(solution)/shard_map/ppermute | solution.py:26
  57.2 1.1 %collective-permute-start.13 = (f16[2,2,16,2048]{3,2,1,0:T(8,128)(2,1)S(1)}, f16[2,2,16,2048]{3,2,1,0:T(8,128)(2,1)S(1)}, u32[]{:S(2)}, u32[]{:S(2)}) collective-permute-start(f16[2,2,16,2048]{3,2,1,0:T(8,128)(2,1)S(1)} %fusion.6), channel_id=1, source_target_pairs={{0,2},{2,4},{4,6},{6,8},{8,10},{10,12},{12,14},{14,0},{1,3},{3,5},... | collective-permute-start | bytes 786440 | tf_op jit(solution)/shard_map/ppermute | solution.py:26
  58.2 0.1 fusion.5
  58.4 0.8 collective-permute-start.9
  59.1 1.5 %collective-permute-done.17 = f16[2,16,2048]{2,1,0:T(8,128)(2,1)S(1)} collective-permute-done((f16[2,16,2048]{2,1,0:T(8,128)(2,1)S(1)}, f16[2,16,2048]{2,1,0:T(8,128)(2,1)S(1)}, u32[]{:S(2)}, u32[]{:S(2)}) %collective-permute-start.17) | collective-permute-done | bytes 131104 | tf_op jit(solution)/shard_map/ppermute | solution.py:26
  60.6 5.4 %collective-permute-done.16 = f16[2,2,16,2048]{3,2,1,0:T(8,128)(2,1)S(1)} collective-permute-done((f16[2,2,16,2048]{3,2,1,0:T(8,128)(2,1)S(1)}, f16[2,2,16,2048]{3,2,1,0:T(8,128)(2,1)S(1)}, u32[]{:S(2)}, u32[]{:S(2)}) %collective-permute-start.16) | collective-permute-done | bytes 262176 | tf_op jit(solution)/shard_map/ppermute | solution.py:26
  66.0 0.0 collective-permute-done.13
  66.0 0.1 fusion.19
  66.1 5.4 %collective-permute-done.9 = f16[8,16,2048]{2,1,0:T(8,128)(2,1)S(1)} collective-permute-done((f16[8,16,2048]{2,1,0:T(8,128)(2,1)S(1)}, f16[8,16,2048]{2,1,0:T(8,128)(2,1)S(1)}, u32[]{:S(2)}, u32[]{:S(2)}) %collective-permute-start.9) | collective-permute-done | bytes 524320 | tf_op jit(solution)/shard_map/ppermute | solution.py:26
  71.6 0.1 fusion.41
  71.7 0.4 collective-permute-start.11
  72.1 1.1 %collective-permute-start.14 = (f16[3,16,2048]{2,1,0:T(8,128)(2,1)S(1)}, f16[3,16,2048]{2,1,0:T(8,128)(2,1)S(1)}, u32[]{:S(2)}, u32[]{:S(2)}) collective-permute-start(f16[3,16,2048]{2,1,0:T(8,128)(2,1)S(1)} %pad_maximum_fusion.3), channel_id=1, source_target_pairs={{0,4},{2,6},{4,8},{6,10},{8,12},{10,14},{12,0},{14,2},{1,5},{3,7},... | collective-permute-start | bytes 589832 | tf_op jit(solution)/shard_map/ppermute | solution.py:26
  73.2 0.8 collective-permute-start.10
  74.7 4.2 %collective-permute-start.18 = (f16[2,16,2048]{2,1,0:T(8,128)(2,1)S(1)}, f16[2,16,2048]{2,1,0:T(8,128)(2,1)S(1)}, u32[]{:S(2)}, u32[]{:S(2)}) collective-permute-start(f16[2,16,2048]{2,1,0:T(8,128)(2,1)S(1)} %get-tuple-element.31), channel_id=1, source_target_pairs={{0,12},{2,14},{4,0},{6,2},{8,4},{10,6},{12,8},{14,10},{1,13},{3,15... | collective-permute-start | bytes 393224 | tf_op jit(solution)/shard_map/ppermute | solution.py:26
  78.9 0.0 collective-permute-done.11
  78.9 2.5 %collective-permute-done.10 = f16[2,16,2048]{2,1,0:T(8,128)(2,1)S(1)} collective-permute-done((f16[2,16,2048]{2,1,0:T(8,128)(2,1)S(1)}, f16[2,16,2048]{2,1,0:T(8,128)(2,1)S(1)}, u32[]{:S(2)}, u32[]{:S(2)}) %collective-permute-start.10) | collective-permute-done | bytes 131104 | tf_op jit(solution)/shard_map/ppermute | solution.py:26
  81.4 4.2 %collective-permute-done.14 = f16[3,16,2048]{2,1,0:T(8,128)(2,1)S(1)} collective-permute-done((f16[3,16,2048]{2,1,0:T(8,128)(2,1)S(1)}, f16[3,16,2048]{2,1,0:T(8,128)(2,1)S(1)}, u32[]{:S(2)}, u32[]{:S(2)}) %collective-permute-start.14) | collective-permute-done | bytes 196640 | tf_op jit(solution)/shard_map/ppermute | solution.py:26
  85.6 0.1 fusion.37
  85.7 1.4 %collective-permute-start.12 = (f16[16,2048]{1,0:T(8,128)(2,1)S(1)}, f16[16,2048]{1,0:T(8,128)(2,1)S(1)}, u32[]{:S(2)}, u32[]{:S(2)}) collective-permute-start(f16[16,2048]{1,0:T(8,128)(2,1)S(1)} %get-tuple-element.23), channel_id=1, source_target_pairs={{0,12},{2,14},{4,0},{6,2},{8,4},{10,6},{12,8},{14,10},{1,13},{3,15... | collective-permute-start | bytes 196616 | tf_op jit(solution)/shard_map/ppermute | solution.py:26
  87.2 1.6 %collective-permute-start.15 = (f16[16,2048]{1,0:T(8,128)(2,1)S(1)}, f16[16,2048]{1,0:T(8,128)(2,1)S(1)}, u32[]{:S(2)}, u32[]{:S(2)}) collective-permute-start(f16[16,2048]{1,0:T(8,128)(2,1)S(1)} %get-tuple-element.24), channel_id=1, source_target_pairs={{0,4},{2,6},{4,8},{6,10},{8,12},{10,14},{12,0},{14,2},{1,5},{3,7},... | collective-permute-start | bytes 196616 | tf_op jit(solution)/shard_map/ppermute | solution.py:26
  88.7 0.0 collective-permute-done.18
  88.7 0.1 fusion.16
  88.9 0.8 collective-permute-start.19
  89.6 1.3 %collective-permute-done.12 = f16[16,2048]{1,0:T(8,128)(2,1)S(1)} collective-permute-done((f16[16,2048]{1,0:T(8,128)(2,1)S(1)}, f16[16,2048]{1,0:T(8,128)(2,1)S(1)}, u32[]{:S(2)}, u32[]{:S(2)}) %collective-permute-start.12) | collective-permute-done | bytes 65568 | tf_op jit(solution)/shard_map/ppermute | solution.py:26
  91.0 2.6 %collective-permute-done.15 = f16[16,2048]{1,0:T(8,128)(2,1)S(1)} collective-permute-done((f16[16,2048]{1,0:T(8,128)(2,1)S(1)}, f16[16,2048]{1,0:T(8,128)(2,1)S(1)}, u32[]{:S(2)}, u32[]{:S(2)}) %collective-permute-start.15) | collective-permute-done | bytes 65568 | tf_op jit(solution)/shard_map/ppermute | solution.py:26
  93.5 0.1 fusion.46
  93.6 0.3 collective-permute-done.19
  93.9 0.8 fusion.23
  (10 shorter events, 0.3 us)
Async XLA Ops:
  0.0 9.5 %copy-start = (f32[256]{0:T(256)S(1)}, f32[256]{0:T(256)}, u32[]{:S(2)}) copy-start(f32[256]{0:T(256)} %param.8) | copy-start | bytes 3076
  0.0 9.5 %copy-start.2 = (s32[2048]{0:T(1024)S(1)}, s32[2048]{0:T(1024)}, u32[]{:S(2)}) copy-start(s32[2048]{0:T(1024)} %param.7) | copy-start | bytes 24580
  1.2 16.7 %collective-permute-start.2 = (bf16[128,2048]{1,0:T(8,128)(2,1)S(1)}, bf16[128,2048]{1,0:T(8,128)(2,1)S(1)}, u32[]{:S(2)}, u32[]{:S(2)}) collective-permute-start(bf16[128,2048]{1,0:T(8,128)(2,1)S(1)} %pad_maximum_fusion.2.refs_0_), channel_id=1, source_target_pairs={{0,32},{32,0},{1,33},{33,1},{2,34},{34,2},{3,35},{35,3},{4,36},{36... | collective-permute-start | bytes 1572872 | tf_op jit(solution)/shard_map/ppermute | solution.py:26
  4.4 16.4 %collective-permute-start = (bf16[128,2048]{1,0:T(8,128)(2,1)S(1)}, bf16[128,2048]{1,0:T(8,128)(2,1)S(1)}, u32[]{:S(2)}, u32[]{:S(2)}) collective-permute-start(bf16[128,2048]{1,0:T(8,128)(2,1)S(1)} %pad_maximum_fusion.2.refs_0_), channel_id=1, source_target_pairs={{0,128},{64,192},{128,0},{192,64},{1,129},{65,193},{129,1},{193,65... | collective-permute-start | bytes 1572872 | tf_op jit(solution)/shard_map/ppermute | solution.py:26
  7.5 24.7 %collective-permute-start.6 = (bf16[128,2048]{1,0:T(8,128)(2,1)S(1)}, bf16[128,2048]{1,0:T(8,128)(2,1)S(1)}, u32[]{:S(2)}, u32[]{:S(2)}) collective-permute-start(bf16[128,2048]{1,0:T(8,128)(2,1)S(1)} %pad_maximum_fusion.2.refs_0_), channel_id=1, source_target_pairs={{0,192},{64,0},{128,64},{192,128},{1,193},{65,1},{129,65},{193,129... | collective-permute-start | bytes 1572872 | tf_op jit(solution)/shard_map/ppermute | solution.py:26
  8.6 23.6 %collective-permute-start.5 = (bf16[128,2048]{1,0:T(8,128)(2,1)S(1)}, bf16[128,2048]{1,0:T(8,128)(2,1)S(1)}, u32[]{:S(2)}, u32[]{:S(2)}) collective-permute-start(bf16[128,2048]{1,0:T(8,128)(2,1)S(1)} %pad_maximum_fusion.2.refs_0_), channel_id=1, source_target_pairs={{0,64},{64,128},{128,192},{192,0},{1,65},{65,129},{129,193},{193,1... | collective-permute-start | bytes 1572872 | tf_op jit(solution)/shard_map/ppermute | solution.py:26
  10.5 3.4 %copy-start.1 = (bf16[2048,2048]{1,0:T(8,128)(2,1)S(1)}, bf16[2048,2048]{1,0:T(8,128)(2,1)}, u32[]{:S(2)}) copy-start(bf16[2048,2048]{1,0:T(8,128)(2,1)} %slab.1) | copy-start | bytes 25165828
  17.9 24.0 %collective-permute-start.4 = (bf16[128,2048]{1,0:T(8,128)(2,1)S(1)}, bf16[128,2048]{1,0:T(8,128)(2,1)S(1)}, u32[]{:S(2)}, u32[]{:S(2)}) collective-permute-start(bf16[128,2048]{1,0:T(8,128)(2,1)S(1)} %collective-permute-done.2.refs_1_), channel_id=1, source_target_pairs={{0,192},{64,0},{128,64},{192,128},{1,193},{65,1},{129,65},{193,129... | collective-permute-start | bytes 1572872 | tf_op jit(solution)/shard_map/ppermute | solution.py:26
  20.3 21.6 %collective-permute-start.3 = (bf16[128,2048]{1,0:T(8,128)(2,1)S(1)}, bf16[128,2048]{1,0:T(8,128)(2,1)S(1)}, u32[]{:S(2)}, u32[]{:S(2)}) collective-permute-start(bf16[128,2048]{1,0:T(8,128)(2,1)S(1)} %collective-permute-done.2.refs_1_), channel_id=1, source_target_pairs={{0,64},{64,128},{128,192},{192,0},{1,65},{65,129},{129,193},{193,1... | collective-permute-start | bytes 1572872 | tf_op jit(solution)/shard_map/ppermute | solution.py:26
  20.8 21.1 %collective-permute-start.1 = (bf16[128,2048]{1,0:T(8,128)(2,1)S(1)}, bf16[128,2048]{1,0:T(8,128)(2,1)S(1)}, u32[]{:S(2)}, u32[]{:S(2)}) collective-permute-start(bf16[128,2048]{1,0:T(8,128)(2,1)S(1)} %collective-permute-done), channel_id=1, source_target_pairs={{0,32},{32,0},{1,33},{33,1},{2,34},{34,2},{3,35},{35,3},{4,36},{36... | collective-permute-start | bytes 1572872 | tf_op jit(solution)/shard_map/ppermute | solution.py:26
  39.4 8.6 %collective-permute-start.8 = (f32[256,2048]{1,0:T(8,128)S(1)}, f32[256,2048]{1,0:T(8,128)S(1)}, u32[]{:S(2)}, u32[]{:S(2)}) collective-permute-start(f32[256,2048]{1,0:T(8,128)S(1)} %get-tuple-element.15), channel_id=1, source_target_pairs={{0,1},{1,0},{2,3},{3,2},{4,5},{5,4},{6,7},{7,6},{8,9},{9,8},{10,11... | collective-permute-start | bytes 6291464 | tf_op jit(solution)/shard_map/ppermute | solution.py:26
  45.2 4.4 %collective-permute-start.7 = (f32[256,2048]{1,0:T(8,128)S(1)}, f32[256,2048]{1,0:T(8,128)S(1)}, u32[]{:S(2)}, u32[]{:S(2)}) collective-permute-start(f32[256,2048]{1,0:T(8,128)S(1)} %fusion), channel_id=1, source_target_pairs={{0,1},{1,0},{2,3},{3,2},{4,5},{5,4},{6,7},{7,6},{8,9},{9,8},{10,11... | collective-permute-start | bytes 6291464 | tf_op jit(solution)/shard_map/ppermute | solution.py:26
  50.5 10.1 %collective-permute-start.17 = (f16[2,16,2048]{2,1,0:T(8,128)(2,1)S(1)}, f16[2,16,2048]{2,1,0:T(8,128)(2,1)S(1)}, u32[]{:S(2)}, u32[]{:S(2)}) collective-permute-start(f16[2,16,2048]{2,1,0:T(8,128)(2,1)S(1)} %get-tuple-element.35), channel_id=1, source_target_pairs={{0,12},{2,14},{4,0},{6,2},{8,4},{10,6},{12,8},{14,10},{1,13},{3,15... | collective-permute-start | bytes 393224 | tf_op jit(solution)/shard_map/ppermute | solution.py:26
  56.0 10.0 %collective-permute-start.16 = (f16[2,2,16,2048]{3,2,1,0:T(8,128)(2,1)S(1)}, f16[2,2,16,2048]{3,2,1,0:T(8,128)(2,1)S(1)}, u32[]{:S(2)}, u32[]{:S(2)}) collective-permute-start(f16[2,2,16,2048]{3,2,1,0:T(8,128)(2,1)S(1)} %fusion.7), channel_id=1, source_target_pairs={{0,14},{2,0},{4,2},{6,4},{8,6},{10,8},{12,10},{14,12},{1,15},{3,1}... | collective-permute-start | bytes 786440 | tf_op jit(solution)/shard_map/ppermute | solution.py:26
  57.2 8.8 %collective-permute-start.13 = (f16[2,2,16,2048]{3,2,1,0:T(8,128)(2,1)S(1)}, f16[2,2,16,2048]{3,2,1,0:T(8,128)(2,1)S(1)}, u32[]{:S(2)}, u32[]{:S(2)}) collective-permute-start(f16[2,2,16,2048]{3,2,1,0:T(8,128)(2,1)S(1)} %fusion.6), channel_id=1, source_target_pairs={{0,2},{2,4},{4,6},{6,8},{8,10},{10,12},{12,14},{14,0},{1,3},{3,5},... | collective-permute-start | bytes 786440 | tf_op jit(solution)/shard_map/ppermute | solution.py:26
  58.4 13.2 %collective-permute-start.9 = (f16[8,16,2048]{2,1,0:T(8,128)(2,1)S(1)}, f16[8,16,2048]{2,1,0:T(8,128)(2,1)S(1)}, u32[]{:S(2)}, u32[]{:S(2)}) collective-permute-start(f16[8,16,2048]{2,1,0:T(8,128)(2,1)S(1)} %fusion.5), channel_id=1, source_target_pairs={{0,16},{16,0},{1,17},{17,1},{2,18},{18,2},{3,19},{19,3},{4,20},{20... | collective-permute-start | bytes 1572872 | tf_op jit(solution)/shard_map/ppermute | solution.py:26
  71.7 7.2 %collective-permute-start.11 = (f16[2,16,2048]{2,1,0:T(8,128)(2,1)S(1)}, f16[2,16,2048]{2,1,0:T(8,128)(2,1)S(1)}, u32[]{:S(2)}, u32[]{:S(2)}) collective-permute-start(f16[2,16,2048]{2,1,0:T(8,128)(2,1)S(1)} %fusion.21), channel_id=1, source_target_pairs={{0,2},{2,4},{4,6},{6,8},{8,10},{10,12},{12,14},{14,0},{1,3},{3,5},... | collective-permute-start | bytes 393224 | tf_op jit(solution)/shard_map/ppermute | solution.py:26
  72.1 13.5 %collective-permute-start.14 = (f16[3,16,2048]{2,1,0:T(8,128)(2,1)S(1)}, f16[3,16,2048]{2,1,0:T(8,128)(2,1)S(1)}, u32[]{:S(2)}, u32[]{:S(2)}) collective-permute-start(f16[3,16,2048]{2,1,0:T(8,128)(2,1)S(1)} %pad_maximum_fusion.3), channel_id=1, source_target_pairs={{0,4},{2,6},{4,8},{6,10},{8,12},{10,14},{12,0},{14,2},{1,5},{3,7},... | collective-permute-start | bytes 589832 | tf_op jit(solution)/shard_map/ppermute | solution.py:26
  73.2 8.2 %collective-permute-start.10 = (f16[2,16,2048]{2,1,0:T(8,128)(2,1)S(1)}, f16[2,16,2048]{2,1,0:T(8,128)(2,1)S(1)}, u32[]{:S(2)}, u32[]{:S(2)}) collective-permute-start(f16[2,16,2048]{2,1,0:T(8,128)(2,1)S(1)} %fusion.20), channel_id=1, source_target_pairs={{0,14},{2,0},{4,2},{6,4},{8,6},{10,8},{12,10},{14,12},{1,15},{3,1}... | collective-permute-start | bytes 393224 | tf_op jit(solution)/shard_map/ppermute | solution.py:26
  74.7 14.0 %collective-permute-start.18 = (f16[2,16,2048]{2,1,0:T(8,128)(2,1)S(1)}, f16[2,16,2048]{2,1,0:T(8,128)(2,1)S(1)}, u32[]{:S(2)}, u32[]{:S(2)}) collective-permute-start(f16[2,16,2048]{2,1,0:T(8,128)(2,1)S(1)} %get-tuple-element.31), channel_id=1, source_target_pairs={{0,12},{2,14},{4,0},{6,2},{8,4},{10,6},{12,8},{14,10},{1,13},{3,15... | collective-permute-start | bytes 393224 | tf_op jit(solution)/shard_map/ppermute | solution.py:26
  85.7 5.2 %collective-permute-start.12 = (f16[16,2048]{1,0:T(8,128)(2,1)S(1)}, f16[16,2048]{1,0:T(8,128)(2,1)S(1)}, u32[]{:S(2)}, u32[]{:S(2)}) collective-permute-start(f16[16,2048]{1,0:T(8,128)(2,1)S(1)} %get-tuple-element.23), channel_id=1, source_target_pairs={{0,12},{2,14},{4,0},{6,2},{8,4},{10,6},{12,8},{14,10},{1,13},{3,15... | collective-permute-start | bytes 196616 | tf_op jit(solution)/shard_map/ppermute | solution.py:26
  87.2 6.4 %collective-permute-start.15 = (f16[16,2048]{1,0:T(8,128)(2,1)S(1)}, f16[16,2048]{1,0:T(8,128)(2,1)S(1)}, u32[]{:S(2)}, u32[]{:S(2)}) collective-permute-start(f16[16,2048]{1,0:T(8,128)(2,1)S(1)} %get-tuple-element.24), channel_id=1, source_target_pairs={{0,4},{2,6},{4,8},{6,10},{8,12},{10,14},{12,0},{14,2},{1,5},{3,7},... | collective-permute-start | bytes 196616 | tf_op jit(solution)/shard_map/ppermute | solution.py:26
  88.9 5.1 %collective-permute-start.19 = (f32[16,2048]{1,0:T(8,128)S(1)}, f32[16,2048]{1,0:T(8,128)S(1)}, u32[]{:S(2)}, u32[]{:S(2)}) collective-permute-start(f32[16,2048]{1,0:T(8,128)S(1)} %slice_bitcast_fusion.7), channel_id=1, source_target_pairs={{0,16},{16,0},{1,17},{17,1},{2,18},{18,2},{3,19},{19,3},{4,20},{20... | collective-permute-start | bytes 393224 | tf_op jit(solution)/shard_map/ppermute | solution.py:26

commit v3 on v2

--- a/solution.py
+++ b/solution.py
@@ -14,8 +14,8 @@
 GROUP = 32
 CUT = GROUP // 2
 KEPT = 2 * GROUP
-EARLY = ((0, 0), (0, 1), (-1, 0), (1, 0))
-LATE = ((2, 0), (2, 1), (-1, 1), (1, 1))
+EARLY = ((0, 0), (0, 1), (-1, 0), (1, 0), (2, 0))
+LATE = ((2, 1), (-1, 1), (1, 1))
 TILE = 256
 VMEM = pl.BlockSpec(memory_space=pltpu.VMEM)
 SMEM = pl.BlockSpec(memory_space=pltpu.SMEM)
@@ -84,11 +84,12 @@
 
 def early_kernel(offsets, place, weight, slab_norm, slab, *refs):
     count = len(offsets)
-    blocks, (other, held, rows, norms) = refs[:count], refs[count:]
+    blocks, (other, held, rows, norms) = refs[:-4], refs[-4:]
+    blocks = (blocks[:count], blocks[count:])
     for half in range(CORE):
-        for i, block in enumerate(blocks):
+        for i, block in enumerate(blocks[half]):
             at = pl.ds((half * count + i) * KEPT, KEPT)
-            piece = block[half * KEPT : (half + 1) * KEPT, :]
+            piece = block[...]
             rows[at, :] = piece
             wide = piece.astype(jnp.float32)
             norms[at, :] = jnp.sum(wide * wide * weight[...], axis=1, keepdims=True)
@@ -160,25 +161,35 @@
     columns, depth = slab.shape
 
     own = queries.reshape(2, CORE, GROUP, depth)
-    own = jnp.concatenate(
-        [lax.dynamic_index_in_dim(own, c, 1, keepdims=False).reshape(-1, depth) for c in (1 - core, core)]
-    )
+    own_other, own_mine = (
+        lax.dynamic_index_in_dim(own, c, 1, keepdims=False).reshape(-1, depth) for c in (1 - core, core)
+    )
+    own = jnp.concatenate([own_other, own_mine])
+    right_other, left_mine = shift(own_other, "x", -1), shift(own_mine, "x", 1)
     pair = shift(own, "yh", 1)
-    far = shift(own, "x", 2)
-    left, right = shift(own, "x", 1), shift(own, "x", -1)
 
     levels = jnp.arange(degree_weight.shape[0], dtype=jnp.int32)
     one_hot_table = (degree[:, None] == levels[None, :]).astype(jnp.float32)
     weight_of = jnp.dot(one_hot_table, degree_weight, precision=lax.Precision.HIGHEST)[None, :]
+    next_other, next_mine, weight_of = lax.optimization_barrier((own_other, own_mine, weight_of))
+    left_other, right_mine = shift(next_other, "x", 1), shift(next_mine, "x", -1)
     weighted_slab, slab_norm = prepare(weight_of, slab)
 
+    far_other, far_mine = shift(right_other, "x", -1), shift(left_mine, "x", 1)
     pair_left, pair_right = shift(pair, "x", 1), shift(pair, "x", -1)
-    pair_far = shift(far, "yh", 1)
+    pair_far = shift(jnp.concatenate([far_other, far_mine]), "yh", 1)
 
     place = jnp.stack([x, yh, yl, z]).astype(jnp.int32)
     small = cost(0, 2**16)
     early_other, held = early_partial(
-        EARLY, place, weight_of, slab_norm, weighted_slab, [own, pair, left, right], cost(3 * 10**10, 2**16)
+        EARLY,
+        place,
+        weight_of,
+        slab_norm,
+        weighted_slab,
+        [own_other, pair[:KEPT], left_other, right_other, far_other]
+        + [own_mine, pair[KEPT:], left_mine, right_mine, far_mine],
+        cost(3 * 10**10, 2**16),
     )
     pieces = [shift(early_other, "core", 1)]
     held = add_into(EARLY, place, pieces, None, held, small)
@@ -192,7 +203,7 @@
         )
         return norm[:, None] + slab_norm - 2.0 * gram
 
-    late = lax.optimization_barrier((far, pair_far, pair_left, pair_right, early_other))[:4]
+    late = lax.optimization_barrier((pair_far, pair_left, pair_right, early_other))[:3]
     late_other = shift(partial([b[:KEPT] for b in late]), "core", 1)
     late_mine = partial([b[KEPT:] for b in late])
     held = add_into(LATE, place, [late_other], late_mine, held, small)
@@ -206,27 +217,30 @@
     minus = shift(pack(jnp.stack([second(-1), second(-3)])), "z", -1)
     plus = shift(pack(jnp.stack([second(1), second(3)])), "z", 1)
     opposite = shift(pack(second(4)), "z", -2)
+    across, minus, plus, opposite = lax.optimization_barrier((across, minus, plus, opposite))
 
     def first(k):
         return held[0, k % Z, :CUT] + unpack(across[k % Z])
 
+    second_here = second(0) + unpack(minus[0]) + unpack(plus[0])
+    second_minus = second(-2) + unpack(minus[1]) + unpack(opposite)
+    second_plus = second(2) + unpack(plus[1])
+    across_second = shift(pack(jnp.stack([second_here[1], second_minus[1], second_plus[1]])), "yl", 1)
     minus_first = shift(pack(jnp.stack([first(-1), first(-3)])), "z", -1)
     plus_first = shift(pack(jnp.stack([first(1), first(3)])), "z", 1)
-    sum_minus = second(-2) + unpack(minus[1]) + unpack(opposite)
-    sum_plus = second(2) + unpack(plus[1])
-    last_minus = shift(pack(sum_minus), "z", -2)
-    last_plus = shift(jnp.concatenate([pack(sum_plus), pack(first(4))[None]]), "z", 2)
-
-    second_sum = second(0) + unpack(minus[0]) + unpack(plus[0]) + unpack(last_minus) + unpack(last_plus[:2])
-    second_sum = second_sum[0] + shift(second_sum[1], "yl", 1)
-
-    first_minus = first(-2) + unpack(minus_first[1])
-    first_plus = first(2) + unpack(plus_first[1]) + unpack(last_plus[2])
-    end_minus = shift(pack(first_minus), "z", -2)
-    end_plus = shift(pack(first_plus), "z", 2)
-    first_sum = first(0) + unpack(minus_first[0]) + unpack(plus_first[0]) + unpack(end_minus) + unpack(end_plus)
-
-    distance = jnp.concatenate([first_sum, second_sum], axis=0)
+    opposite_first = shift(pack(first(4)), "z", 2)
+    across_second, minus_first, plus_first, opposite_first = lax.optimization_barrier(
+        (across_second, minus_first, plus_first, opposite_first)
+    )
+
+    end_minus = jnp.stack([first(-2) + unpack(minus_first[1]), second_minus[0] + unpack(across_second[1])])
+    end_plus = jnp.stack(
+        [first(2) + unpack(plus_first[1]) + unpack(opposite_first), second_plus[0] + unpack(across_second[2])]
+    )
+    end_minus, end_plus = shift(pack(end_minus), "z", -2), shift(pack(end_plus), "z", 2)
+    first_sum = first(0) + unpack(minus_first[0]) + unpack(plus_first[0])
+    second_sum = second_here[0] + unpack(across_second[0])
+    distance = jnp.concatenate([first_sum, second_sum]) + (unpack(end_minus) + unpack(end_plus)).reshape(GROUP, columns)
     return jnp.exp(-distance / spread[0])
 
 

time: 94.8 us -> 91.3 us (0.963); the launches traced: 94.7 us -> 89.5 us
  waiting for transfers between devices: 36.9 us -> 18 us
  starting transfers between devices: 31.3 us -> 42.9 us
  Pallas kernels: 12.6 us -> 13.9 us
    ppermute x20 -> x22, waiting for transfers between devices: 36.9 us -> 18 us  [shift(): lax.ppermute(value, axis, [(i, (i + by) % size) for i in range(size)])]
    ppermute x20 -> x22, starting transfers between devices: 31.3 us -> 42.9 us  [shift(): lax.ppermute(value, axis, [(i, (i + by) % size) for i in range(size)])]
    pallas_call x1, Pallas kernels: 7.19 us -> 8.41 us  [early_partial(): pl.pallas_call(functools.partial(early_kernel, offsets), in_specs=[SMEM]...]
  transfers between devices with their start and end apart: 20 -> 22, of which waited for: 12 -> 5; matrix products, arithmetic and copies ran while one was open for 8% -> 9% of each run, Pallas kernels for 13% -> 15%
where the time goes in v3:
time: 91.3 us; the launch traced here: 89.5 us
  starting transfers between devices  42.9 us (47%)
  waiting for transfers between devices  18 us (20%)
  Pallas kernels  13.9 us (15%)
  matrix products  6.84 us (7%)
  local copies, waits for them, and re-layouts  4.66 us (5%)
  other arithmetic  2.28 us (2%)
  between operations  0.95 us (1%)
    ppermute x22, starting transfers between devices, shift(): lax.ppermute(value, axis, [(i, (i + by) % size) for i in range(size)])  42.9 us
    ppermute x22, waiting for transfers between devices, shift(): lax.ppermute(value, axis, [(i, (i + by) % size) for i in range(size)])  18 us
    pallas_call x1, Pallas kernels, early_partial(): pl.pallas_call(functools.partial(early_kernel, offsets), in_specs=[SMEM]...  8.41 us
    dot_general x2, matrix products, partial(): lax.dot_general(rows, weighted_slab, (((1,), (1,)), ((), ())), preferred_...  5.79 us
    pallas_call x1, Pallas kernels, prepare(): pl.pallas_call(prepare_kernel, grid=(rows // TILE,), in_specs=[pl.BlockSp...  3.87 us
    unnamed x6, local copies, waits for them, and re-layouts  3.39 us
  transfers between devices with their start and end apart: 22, of which 5 were waited for; matrix products, arithmetic and copies ran while one was open for 9% of the time, Pallas kernels for 15%

profile of v3, /device:TPU:32, one launch (start us, length us, event | category | flops | bytes accessed | tf_op | source)
XLA Modules:
  0.0 89.5 jit_solution(17505276079918164211)
XLA Ops:
  0.0 0.0 copy-start
  0.0 1.1 %constant_dynamic-slice_fusion = (bf16[2,1,32,2048]{3,2,1,0:T(8,128)(2,1)S(1)}, bf16[2,1,32,2048]{3,2,1,0:T(8,128)(2,1)S(1)}) fusion(bf16[2,2,32,2048]{3,2,1,0:T(8,128)(2,1)} %bitcast.154, s32[]{:T(128)S(6)} %select_n.8, s32[]{:T(128)S(6)} %select_n.7), kind=kLoop, calls=%fused_computation.79 | loop fusion | bytes 1048584 | tf_op jit(solution)/shard_map/jit(dynamic_index_in_dim)/dynamic_slice | solution.py:165
  1.1 1.6 %collective-permute-start.2 = (bf16[64,2048]{1,0:T(8,128)(2,1)S(1)}, bf16[64,2048]{1,0:T(8,128)(2,1)S(1)}, u32[]{:S(2)}, u32[]{:S(2)}) collective-permute-start(bf16[64,2048]{1,0:T(8,128)(2,1)S(1)} %bitcast.143), channel_id=1, source_target_pairs={{0,64},{64,128},{128,192},{192,0},{1,65},{65,129},{129,193},{193,1... | collective-permute-start | bytes 786440 | tf_op jit(solution)/shard_map/ppermute | solution.py:26
  2.7 1.7 %collective-permute-start = (bf16[64,2048]{1,0:T(8,128)(2,1)S(1)}, bf16[64,2048]{1,0:T(8,128)(2,1)S(1)}, u32[]{:S(2)}, u32[]{:S(2)}) collective-permute-start(bf16[64,2048]{1,0:T(8,128)(2,1)S(1)} %bitcast.147), channel_id=1, source_target_pairs={{0,192},{64,0},{128,64},{192,128},{1,193},{65,1},{129,65},{193,129... | collective-permute-start | bytes 786440 | tf_op jit(solution)/shard_map/ppermute | solution.py:26
  4.5 3.3 %collective-permute-start.5 = (bf16[128,2048]{1,0:T(8,128)(2,1)S(1)}, bf16[128,2048]{1,0:T(8,128)(2,1)S(1)}, u32[]{:S(2)}, u32[]{:S(2)}) collective-permute-start(bf16[128,2048]{1,0:T(8,128)(2,1)S(1)} %pad_maximum_fusion.3), channel_id=1, source_target_pairs={{0,32},{32,0},{1,33},{33,1},{2,34},{34,2},{3,35},{35,3},{4,36},{36... | collective-permute-start | bytes 1572872 | tf_op jit(solution)/shard_map/ppermute | solution.py:26
  7.7 2.7 %collective-permute-done.2.refs_7_ = bf16[64,2048]{1,0:T(8,128)(2,1)S(1)} collective-permute-done((bf16[64,2048]{1,0:T(8,128)(2,1)S(1)}, bf16[64,2048]{1,0:T(8,128)(2,1)S(1)}, u32[]{:S(2)}, u32[]{:S(2)}) %collective-permute-start.2) | collective-permute-done | bytes 262176 | tf_op jit(solution)/shard_map/ppermute | solution.py:26
  10.4 0.3 collective-permute-start.3
  10.7 0.0 collective-permute-done.refs_3_
  10.7 3.0 %collective-permute-start.1 = (bf16[64,2048]{1,0:T(8,128)(2,1)S(1)}, bf16[64,2048]{1,0:T(8,128)(2,1)S(1)}, u32[]{:S(2)}, u32[]{:S(2)}) collective-permute-start(bf16[64,2048]{1,0:T(8,128)(2,1)S(1)} %collective-permute-done.refs_3_), channel_id=1, source_target_pairs={{0,192},{64,0},{128,64},{192,128},{1,193},{65,1},{129,65},{193,129... | collective-permute-start | bytes 786440 | tf_op jit(solution)/shard_map/ppermute | solution.py:26
  13.7 0.0 copy-done.2
  13.7 1.0 %fusion.2.weight = f32[1,2048]{1,0:T(1,128)S(1)} fusion(f32[256,1]{0,1:T(1,128)S(1)} %bitcast.135, s32[2048]{0:T(1024)S(1)} %copy-done.2), kind=kOutput, calls=%fused_computation.5 | convolution fusion | flops 6815744 | bytes 17408 | tf_op jit(solution)/shard_map/dot_general | solution.py:173
  14.7 0.0 collective-permute-start.8
  14.8 3.2 %collective-permute-start.9 = (bf16[64,2048]{1,0:T(8,128)(2,1)S(1)}, bf16[64,2048]{1,0:T(8,128)(2,1)S(1)}, u32[]{:S(2)}, u32[]{:S(2)}) collective-permute-start(bf16[64,2048]{1,0:T(8,128)(2,1)S(1)} %bitcast.145), channel_id=1, source_target_pairs={{0,192},{64,0},{128,64},{192,128},{1,193},{65,1},{129,65},{193,129... | collective-permute-start | bytes 786440 | tf_op jit(solution)/shard_map/ppermute | solution.py:26
  18.0 3.4 %copy-done.1 = bf16[2048,2048]{1,0:T(8,128)(2,1)S(1)} copy-done((bf16[2048,2048]{1,0:T(8,128)(2,1)S(1)}, bf16[2048,2048]{1,0:T(8,128)(2,1)}, u32[]{:S(2)}) %copy-start.1) | copy-done | bytes 8388632
  21.4 3.9 %prepare.1 = (bf16[2048,2048]{1,0:T(8,128)(2,1)S(1)}, f32[1,2048]{1,0:T(1,128)S(1)}) custom-call(f32[1,2048]{1,0:T(1,128)S(1)} %fusion.2.weight, bf16[2048,2048]{1,0:T(8,128)(2,1)S(1)} %copy-done.1), custom_call_target="tpu_custom_call" | custom-call | bytes 1048576 | tf_op jit(solution)/shard_map/prepare/pallas_call | solution.py:55
  25.3 0.1 pad_add_fusion.place
  25.3 0.0 collective-permute-done.3.refs_9_
  25.3 0.0 collective-permute-done.1.refs_4_
  25.4 3.3 %collective-permute-start.4 = (bf16[128,2048]{1,0:T(8,128)(2,1)S(1)}, bf16[128,2048]{1,0:T(8,128)(2,1)S(1)}, u32[]{:S(2)}, u32[]{:S(2)}) collective-permute-start(bf16[128,2048]{1,0:T(8,128)(2,1)S(1)} %pad_maximum_fusion.2), channel_id=1, source_target_pairs={{0,32},{32,0},{1,33},{33,1},{2,34},{34,2},{3,35},{35,3},{4,36},{36... | collective-permute-start | bytes 1572872 | tf_op jit(solution)/shard_map/ppermute | solution.py:26
  28.7 0.0 collective-permute-done.5
  28.7 0.0 collective-permute-start.6
  28.7 3.2 %collective-permute-start.7 = (bf16[128,2048]{1,0:T(8,128)(2,1)S(1)}, bf16[128,2048]{1,0:T(8,128)(2,1)S(1)}, u32[]{:S(2)}, u32[]{:S(2)}) collective-permute-start(bf16[128,2048]{1,0:T(8,128)(2,1)S(1)} %collective-permute-done.5), channel_id=1, source_target_pairs={{0,192},{64,0},{128,64},{192,128},{1,193},{65,1},{129,65},{193,129... | collective-permute-start | bytes 1572872 | tf_op jit(solution)/shard_map/ppermute | solution.py:26
  32.0 0.0 collective-permute-done.8.refs_2_
  32.0 0.0 collective-permute-done.9.refs_8_
  32.0 8.4 %early_partial.1 = (f32[320,2048]{1,0:T(8,128)S(1)}, f32[512,2048]{1,0:T(8,128)S(1)}) custom-call(s32[4]{0:T(128)S(1)} %pad_add_fusion.place, f32[1,2048]{1,0:T(1,128)S(1)} %fusion.2.weight, f32[1,2048]{1,0:T(1,128)S(1)} %get-tuple-element.24.slab_norm, bf16[2048,2048]{1,0:T(8,128)(2,1)S(1)} %get-tuple-element.25.slab, bf16[64,2048]{1,0:T(8,128)(2,1)S(1)} %bitcast.150, ...), custom_call_target="tpu_custom_call" | custom-call | flops 30000001024 | bytes 65536 | tf_op jit(solution)/shard_map/early_partial/pallas_call | solution.py:115
  40.4 0.3 collective-permute-start.11
  40.7 0.0 collective-permute-done.4
  40.7 0.6 collective-permute-done.6
  41.3 0.0 collective-permute-done.7
  41.3 0.1 fusion.42
  41.4 0.5 multiply_reduce_fusion
  41.9 2.9 %fusion = f32[192,2048]{1,0:T(8,128)S(1)} fusion(bf16[2048,2048]{1,0:T(8,128)(2,1)S(1)} %get-tuple-element.25.slab, f32[2048]{0:T(1024)S(1)} %bitcast.152, f32[192]{0:T(256)S(1)} %get-tuple-element.42, bf16[64,2048]{1,0:T(8,128)(2,1)S(1)} %get-tuple-element.61, bf16[64,2048]{1,0:T(8,128)(2,1)S(1)} %get-tuple-element.71, ...), kind=kOutput, calls=%fused_computation.2 | convolution fusion | flops 1614151680 | bytes 10756864 | tf_op jit(solution)/shard_map/dot_general | solution.py:201
  44.8 0.1 collective-permute-start.10
  44.9 2.9 %fusion.1.refs_1_ = f32[192,2048]{1,0:T(8,128)S(1)} fusion(bf16[2048,2048]{1,0:T(8,128)(2,1)S(1)} %get-tuple-element.25.slab, f32[192]{0:T(256)S(1)} %get-tuple-element.41, f32[2048]{0:T(1024)S(1)} %bitcast.153, bf16[64,2048]{1,0:T(8,128)(2,1)S(1)} %get-tuple-element.62, bf16[64,2048]{1,0:T(8,128)(2,1)S(1)} %get-tuple-element.70, ...), kind=kOutput, calls=%fused_computation.3 | convolution fusion | flops 1614151680 | bytes 10756864 | tf_op jit(solution)/shard_map/dot_general | solution.py:201
  47.8 0.0 collective-permute-done.11.refs_0_
  47.8 0.9 add_into.2.refs_2_
  48.7 0.0 collective-permute-done.10.refs_0_
  48.7 0.7 add_into.3
  49.5 0.1 fusion.5
  49.6 0.1 fusion.22
  49.7 0.8 collective-permute-start.12
  50.5 0.2 collective-permute-start.13
  50.7 2.0 %collective-permute-start.14 = (f16[2,2,16,2048]{3,2,1,0:T(8,128)(2,1)S(1)}, f16[2,2,16,2048]{3,2,1,0:T(8,128)(2,1)S(1)}, u32[]{:S(2)}, u32[]{:S(2)}) collective-permute-start(f16[2,2,16,2048]{3,2,1,0:T(8,128)(2,1)S(1)} %fusion.7), channel_id=1, source_target_pairs={{0,2},{2,4},{4,6},{6,8},{8,10},{10,12},{12,14},{14,0},{1,3},{3,5},... | collective-permute-start | bytes 786440 | tf_op jit(solution)/shard_map/ppermute | solution.py:26
  52.7 6.6 %collective-permute-start.15 = (f16[2,16,2048]{2,1,0:T(8,128)(2,1)S(1)}, f16[2,16,2048]{2,1,0:T(8,128)(2,1)S(1)}, u32[]{:S(2)}, u32[]{:S(2)}) collective-permute-start(f16[2,16,2048]{2,1,0:T(8,128)(2,1)S(1)} %get-tuple-element.52), channel_id=1, source_target_pairs={{0,12},{2,14},{4,0},{6,2},{8,4},{10,6},{12,8},{14,10},{1,13},{3,15... | collective-permute-start | bytes 393224 | tf_op jit(solution)/shard_map/ppermute | solution.py:26
  59.3 4.7 %collective-permute-done.15 = f16[2,16,2048]{2,1,0:T(8,128)(2,1)S(1)} collective-permute-done((f16[2,16,2048]{2,1,0:T(8,128)(2,1)S(1)}, f16[2,16,2048]{2,1,0:T(8,128)(2,1)S(1)}, u32[]{:S(2)}, u32[]{:S(2)}) %collective-permute-start.15) | collective-permute-done | bytes 131104 | tf_op jit(solution)/shard_map/ppermute | solution.py:26
  64.1 0.0 collective-permute-done.13
  64.1 0.0 collective-permute-done.14
  64.1 0.0 collective-permute-done.12
  64.1 0.1 fusion.11
  64.3 1.4 %collective-permute-start.16 = (f16[3,16,2048]{2,1,0:T(8,128)(2,1)S(1)}, f16[3,16,2048]{2,1,0:T(8,128)(2,1)S(1)}, u32[]{:S(2)}, u32[]{:S(2)}) collective-permute-start(f16[3,16,2048]{2,1,0:T(8,128)(2,1)S(1)} %fusion.8), channel_id=1, source_target_pairs={{0,16},{16,0},{1,17},{17,1},{2,18},{18,2},{3,19},{19,3},{4,20},{20... | collective-permute-start | bytes 589832 | tf_op jit(solution)/shard_map/ppermute | solution.py:26
  65.8 0.1 fusion.34
  65.9 4.1 %collective-permute-start.17 = (f16[2,16,2048]{2,1,0:T(8,128)(2,1)S(1)}, f16[2,16,2048]{2,1,0:T(8,128)(2,1)S(1)}, u32[]{:S(2)}, u32[]{:S(2)}) collective-permute-start(f16[2,16,2048]{2,1,0:T(8,128)(2,1)S(1)} %fusion.15), channel_id=1, source_target_pairs={{0,14},{2,0},{4,2},{6,4},{8,6},{10,8},{12,10},{14,12},{1,15},{3,1}... | collective-permute-start | bytes 393224 | tf_op jit(solution)/shard_map/ppermute | solution.py:26
  70.0 1.3 %collective-permute-start.18 = (f16[2,16,2048]{2,1,0:T(8,128)(2,1)S(1)}, f16[2,16,2048]{2,1,0:T(8,128)(2,1)S(1)}, u32[]{:S(2)}, u32[]{:S(2)}) collective-permute-start(f16[2,16,2048]{2,1,0:T(8,128)(2,1)S(1)} %fusion.16), channel_id=1, source_target_pairs={{0,2},{2,4},{4,6},{6,8},{8,10},{10,12},{12,14},{14,0},{1,3},{3,5},... | collective-permute-start | bytes 393224 | tf_op jit(solution)/shard_map/ppermute | solution.py:26
  71.3 2.3 %collective-permute-start.19 = (f16[16,2048]{1,0:T(8,128)(2,1)S(1)}, f16[16,2048]{1,0:T(8,128)(2,1)S(1)}, u32[]{:S(2)}, u32[]{:S(2)}) collective-permute-start(f16[16,2048]{1,0:T(8,128)(2,1)S(1)} %fusion.32), channel_id=1, source_target_pairs={{0,4},{2,6},{4,8},{6,10},{8,12},{10,14},{12,0},{14,2},{1,5},{3,7},... | collective-permute-start | bytes 196616 | tf_op jit(solution)/shard_map/ppermute | solution.py:26
  73.6 5.7 %collective-permute-done.19 = f16[16,2048]{1,0:T(8,128)(2,1)S(1)} collective-permute-done((f16[16,2048]{1,0:T(8,128)(2,1)S(1)}, f16[16,2048]{1,0:T(8,128)(2,1)S(1)}, u32[]{:S(2)}, u32[]{:S(2)}) %collective-permute-start.19) | collective-permute-done | bytes 65568 | tf_op jit(solution)/shard_map/ppermute | solution.py:26
  79.3 0.0 collective-permute-done.17
  79.3 0.0 collective-permute-done.18
  79.3 0.0 collective-permute-done.16
  79.4 0.1 fusion.26
  79.5 0.9 collective-permute-start.21
  80.4 3.4 %collective-permute-start.20 = (f16[2,16,2048]{2,1,0:T(8,128)(2,1)S(1)}, f16[2,16,2048]{2,1,0:T(8,128)(2,1)S(1)}, u32[]{:S(2)}, u32[]{:S(2)}) collective-permute-start(f16[2,16,2048]{2,1,0:T(8,128)(2,1)S(1)} %fusion.20), channel_id=1, source_target_pairs={{0,12},{2,14},{4,0},{6,2},{8,4},{10,6},{12,8},{14,10},{1,13},{3,15... | collective-permute-start | bytes 393224 | tf_op jit(solution)/shard_map/ppermute | solution.py:26
  84.5 4.2 %collective-permute-done.21 = f16[2,16,2048]{2,1,0:T(8,128)(2,1)S(1)} collective-permute-done((f16[2,16,2048]{2,1,0:T(8,128)(2,1)S(1)}, f16[2,16,2048]{2,1,0:T(8,128)(2,1)S(1)}, u32[]{:S(2)}, u32[]{:S(2)}) %collective-permute-start.21) | collective-permute-done | bytes 131104 | tf_op jit(solution)/shard_map/ppermute | solution.py:26
  88.7 0.0 collective-permute-done.20
  88.8 0.8 fusion.19
  (21 shorter events, 0.6 us)
Async XLA Ops:
  0.0 13.7 %copy-start = (f32[256]{0:T(256)S(1)}, f32[256]{0:T(256)}, u32[]{:S(2)}) copy-start(f32[256]{0:T(256)} %param.8) | copy-start | bytes 3076
  0.0 13.7 %copy-start.2 = (s32[2048]{0:T(1024)S(1)}, s32[2048]{0:T(1024)}, u32[]{:S(2)}) copy-start(s32[2048]{0:T(1024)} %param.7) | copy-start | bytes 24580
  1.1 9.3 %collective-permute-start.2 = (bf16[64,2048]{1,0:T(8,128)(2,1)S(1)}, bf16[64,2048]{1,0:T(8,128)(2,1)S(1)}, u32[]{:S(2)}, u32[]{:S(2)}) collective-permute-start(bf16[64,2048]{1,0:T(8,128)(2,1)S(1)} %bitcast.143), channel_id=1, source_target_pairs={{0,64},{64,128},{128,192},{192,0},{1,65},{65,129},{129,193},{193,1... | collective-permute-start | bytes 786440 | tf_op jit(solution)/shard_map/ppermute | solution.py:26
  2.7 8.0 %collective-permute-start = (bf16[64,2048]{1,0:T(8,128)(2,1)S(1)}, bf16[64,2048]{1,0:T(8,128)(2,1)S(1)}, u32[]{:S(2)}, u32[]{:S(2)}) collective-permute-start(bf16[64,2048]{1,0:T(8,128)(2,1)S(1)} %bitcast.147), channel_id=1, source_target_pairs={{0,192},{64,0},{128,64},{192,128},{1,193},{65,1},{129,65},{193,129... | collective-permute-start | bytes 786440 | tf_op jit(solution)/shard_map/ppermute | solution.py:26
  4.5 24.2 %collective-permute-start.5 = (bf16[128,2048]{1,0:T(8,128)(2,1)S(1)}, bf16[128,2048]{1,0:T(8,128)(2,1)S(1)}, u32[]{:S(2)}, u32[]{:S(2)}) collective-permute-start(bf16[128,2048]{1,0:T(8,128)(2,1)S(1)} %pad_maximum_fusion.3), channel_id=1, source_target_pairs={{0,32},{32,0},{1,33},{33,1},{2,34},{34,2},{3,35},{35,3},{4,36},{36... | collective-permute-start | bytes 1572872 | tf_op jit(solution)/shard_map/ppermute | solution.py:26
  10.4 14.9 %collective-permute-start.3 = (bf16[64,2048]{1,0:T(8,128)(2,1)S(1)}, bf16[64,2048]{1,0:T(8,128)(2,1)S(1)}, u32[]{:S(2)}, u32[]{:S(2)}) collective-permute-start(bf16[64,2048]{1,0:T(8,128)(2,1)S(1)} %collective-permute-done.2.refs_7_), channel_id=1, source_target_pairs={{0,64},{64,128},{128,192},{192,0},{1,65},{65,129},{129,193},{193,1... | collective-permute-start | bytes 786440 | tf_op jit(solution)/shard_map/ppermute | solution.py:26
  10.7 14.6 %collective-permute-start.1 = (bf16[64,2048]{1,0:T(8,128)(2,1)S(1)}, bf16[64,2048]{1,0:T(8,128)(2,1)S(1)}, u32[]{:S(2)}, u32[]{:S(2)}) collective-permute-start(bf16[64,2048]{1,0:T(8,128)(2,1)S(1)} %collective-permute-done.refs_3_), channel_id=1, source_target_pairs={{0,192},{64,0},{128,64},{192,128},{1,193},{65,1},{129,65},{193,129... | collective-permute-start | bytes 786440 | tf_op jit(solution)/shard_map/ppermute | solution.py:26
  14.7 17.2 %collective-permute-start.8 = (bf16[64,2048]{1,0:T(8,128)(2,1)S(1)}, bf16[64,2048]{1,0:T(8,128)(2,1)S(1)}, u32[]{:S(2)}, u32[]{:S(2)}) collective-permute-start(bf16[64,2048]{1,0:T(8,128)(2,1)S(1)} %bitcast.149), channel_id=1, source_target_pairs={{0,64},{64,128},{128,192},{192,0},{1,65},{65,129},{129,193},{193,1... | collective-permute-start | bytes 786440 | tf_op jit(solution)/shard_map/ppermute | solution.py:26
  14.8 17.2 %collective-permute-start.9 = (bf16[64,2048]{1,0:T(8,128)(2,1)S(1)}, bf16[64,2048]{1,0:T(8,128)(2,1)S(1)}, u32[]{:S(2)}, u32[]{:S(2)}) collective-permute-start(bf16[64,2048]{1,0:T(8,128)(2,1)S(1)} %bitcast.145), channel_id=1, source_target_pairs={{0,192},{64,0},{128,64},{192,128},{1,193},{65,1},{129,65},{193,129... | collective-permute-start | bytes 786440 | tf_op jit(solution)/shard_map/ppermute | solution.py:26
  18.0 3.4 %copy-start.1 = (bf16[2048,2048]{1,0:T(8,128)(2,1)S(1)}, bf16[2048,2048]{1,0:T(8,128)(2,1)}, u32[]{:S(2)}) copy-start(bf16[2048,2048]{1,0:T(8,128)(2,1)} %slab.1) | copy-start | bytes 25165828
  25.4 15.3 %collective-permute-start.4 = (bf16[128,2048]{1,0:T(8,128)(2,1)S(1)}, bf16[128,2048]{1,0:T(8,128)(2,1)S(1)}, u32[]{:S(2)}, u32[]{:S(2)}) collective-permute-start(bf16[128,2048]{1,0:T(8,128)(2,1)S(1)} %pad_maximum_fusion.2), channel_id=1, source_target_pairs={{0,32},{32,0},{1,33},{33,1},{2,34},{34,2},{3,35},{35,3},{4,36},{36... | collective-permute-start | bytes 1572872 | tf_op jit(solution)/shard_map/ppermute | solution.py:26
  28.7 12.6 %collective-permute-start.6 = (bf16[128,2048]{1,0:T(8,128)(2,1)S(1)}, bf16[128,2048]{1,0:T(8,128)(2,1)S(1)}, u32[]{:S(2)}, u32[]{:S(2)}) collective-permute-start(bf16[128,2048]{1,0:T(8,128)(2,1)S(1)} %collective-permute-done.5), channel_id=1, source_target_pairs={{0,64},{64,128},{128,192},{192,0},{1,65},{65,129},{129,193},{193,1... | collective-permute-start | bytes 1572872 | tf_op jit(solution)/shard_map/ppermute | solution.py:26
  28.7 12.6 %collective-permute-start.7 = (bf16[128,2048]{1,0:T(8,128)(2,1)S(1)}, bf16[128,2048]{1,0:T(8,128)(2,1)S(1)}, u32[]{:S(2)}, u32[]{:S(2)}) collective-permute-start(bf16[128,2048]{1,0:T(8,128)(2,1)S(1)} %collective-permute-done.5), channel_id=1, source_target_pairs={{0,192},{64,0},{128,64},{192,128},{1,193},{65,1},{129,65},{193,129... | collective-permute-start | bytes 1572872 | tf_op jit(solution)/shard_map/ppermute | solution.py:26
  40.4 7.4 %collective-permute-start.11 = (f32[320,2048]{1,0:T(8,128)S(1)}, f32[320,2048]{1,0:T(8,128)S(1)}, u32[]{:S(2)}, u32[]{:S(2)}) collective-permute-start(f32[320,2048]{1,0:T(8,128)S(1)} %get-tuple-element.28), channel_id=1, source_target_pairs={{0,1},{1,0},{2,3},{3,2},{4,5},{5,4},{6,7},{7,6},{8,9},{9,8},{10,11... | collective-permute-start | bytes 7864328 | tf_op jit(solution)/shard_map/ppermute | solution.py:26
  44.8 3.9 %collective-permute-start.10 = (f32[192,2048]{1,0:T(8,128)S(1)}, f32[192,2048]{1,0:T(8,128)S(1)}, u32[]{:S(2)}, u32[]{:S(2)}) collective-permute-start(f32[192,2048]{1,0:T(8,128)S(1)} %fusion), channel_id=1, source_target_pairs={{0,1},{1,0},{2,3},{3,2},{4,5},{5,4},{6,7},{7,6},{8,9},{9,8},{10,11... | collective-permute-start | bytes 4718600 | tf_op jit(solution)/shard_map/ppermute | solution.py:26
  49.7 14.4 %collective-permute-start.12 = (f16[8,16,2048]{2,1,0:T(8,128)(2,1)S(1)}, f16[8,16,2048]{2,1,0:T(8,128)(2,1)S(1)}, u32[]{:S(2)}, u32[]{:S(2)}) collective-permute-start(f16[8,16,2048]{2,1,0:T(8,128)(2,1)S(1)} %fusion.5), channel_id=1, source_target_pairs={{0,16},{16,0},{1,17},{17,1},{2,18},{18,2},{3,19},{19,3},{4,20},{20... | collective-permute-start | bytes 1572872 | tf_op jit(solution)/shard_map/ppermute | solution.py:26
  50.5 13.6 %collective-permute-start.13 = (f16[2,2,16,2048]{3,2,1,0:T(8,128)(2,1)S(1)}, f16[2,2,16,2048]{3,2,1,0:T(8,128)(2,1)S(1)}, u32[]{:S(2)}, u32[]{:S(2)}) collective-permute-start(f16[2,2,16,2048]{3,2,1,0:T(8,128)(2,1)S(1)} %fusion.6), channel_id=1, source_target_pairs={{0,14},{2,0},{4,2},{6,4},{8,6},{10,8},{12,10},{14,12},{1,15},{3,1}... | collective-permute-start | bytes 786440 | tf_op jit(solution)/shard_map/ppermute | solution.py:26
  50.7 13.4 %collective-permute-start.14 = (f16[2,2,16,2048]{3,2,1,0:T(8,128)(2,1)S(1)}, f16[2,2,16,2048]{3,2,1,0:T(8,128)(2,1)S(1)}, u32[]{:S(2)}, u32[]{:S(2)}) collective-permute-start(f16[2,2,16,2048]{3,2,1,0:T(8,128)(2,1)S(1)} %fusion.7), channel_id=1, source_target_pairs={{0,2},{2,4},{4,6},{6,8},{8,10},{10,12},{12,14},{14,0},{1,3},{3,5},... | collective-permute-start | bytes 786440 | tf_op jit(solution)/shard_map/ppermute | solution.py:26
  52.7 11.4 %collective-permute-start.15 = (f16[2,16,2048]{2,1,0:T(8,128)(2,1)S(1)}, f16[2,16,2048]{2,1,0:T(8,128)(2,1)S(1)}, u32[]{:S(2)}, u32[]{:S(2)}) collective-permute-start(f16[2,16,2048]{2,1,0:T(8,128)(2,1)S(1)} %get-tuple-element.52), channel_id=1, source_target_pairs={{0,12},{2,14},{4,0},{6,2},{8,4},{10,6},{12,8},{14,10},{1,13},{3,15... | collective-permute-start | bytes 393224 | tf_op jit(solution)/shard_map/ppermute | solution.py:26
  64.3 14.9 %collective-permute-start.16 = (f16[3,16,2048]{2,1,0:T(8,128)(2,1)S(1)}, f16[3,16,2048]{2,1,0:T(8,128)(2,1)S(1)}, u32[]{:S(2)}, u32[]{:S(2)}) collective-permute-start(f16[3,16,2048]{2,1,0:T(8,128)(2,1)S(1)} %fusion.8), channel_id=1, source_target_pairs={{0,16},{16,0},{1,17},{17,1},{2,18},{18,2},{3,19},{19,3},{4,20},{20... | collective-permute-start | bytes 589832 | tf_op jit(solution)/shard_map/ppermute | solution.py:26
  65.9 13.4 %collective-permute-start.17 = (f16[2,16,2048]{2,1,0:T(8,128)(2,1)S(1)}, f16[2,16,2048]{2,1,0:T(8,128)(2,1)S(1)}, u32[]{:S(2)}, u32[]{:S(2)}) collective-permute-start(f16[2,16,2048]{2,1,0:T(8,128)(2,1)S(1)} %fusion.15), channel_id=1, source_target_pairs={{0,14},{2,0},{4,2},{6,4},{8,6},{10,8},{12,10},{14,12},{1,15},{3,1}... | collective-permute-start | bytes 393224 | tf_op jit(solution)/shard_map/ppermute | solution.py:26
  70.0 9.3 %collective-permute-start.18 = (f16[2,16,2048]{2,1,0:T(8,128)(2,1)S(1)}, f16[2,16,2048]{2,1,0:T(8,128)(2,1)S(1)}, u32[]{:S(2)}, u32[]{:S(2)}) collective-permute-start(f16[2,16,2048]{2,1,0:T(8,128)(2,1)S(1)} %fusion.16), channel_id=1, source_target_pairs={{0,2},{2,4},{4,6},{6,8},{8,10},{10,12},{12,14},{14,0},{1,3},{3,5},... | collective-permute-start | bytes 393224 | tf_op jit(solution)/shard_map/ppermute | solution.py:26
  71.3 8.0 %collective-permute-start.19 = (f16[16,2048]{1,0:T(8,128)(2,1)S(1)}, f16[16,2048]{1,0:T(8,128)(2,1)S(1)}, u32[]{:S(2)}, u32[]{:S(2)}) collective-permute-start(f16[16,2048]{1,0:T(8,128)(2,1)S(1)} %fusion.32), channel_id=1, source_target_pairs={{0,4},{2,6},{4,8},{6,10},{8,12},{10,14},{12,0},{14,2},{1,5},{3,7},... | collective-permute-start | bytes 196616 | tf_op jit(solution)/shard_map/ppermute | solution.py:26
  79.5 9.2 %collective-permute-start.21 = (f16[2,16,2048]{2,1,0:T(8,128)(2,1)S(1)}, f16[2,16,2048]{2,1,0:T(8,128)(2,1)S(1)}, u32[]{:S(2)}, u32[]{:S(2)}) collective-permute-start(f16[2,16,2048]{2,1,0:T(8,128)(2,1)S(1)} %fusion.21), channel_id=1, source_target_pairs={{0,4},{2,6},{4,8},{6,10},{8,12},{10,14},{12,0},{14,2},{1,5},{3,7},... | collective-permute-start | bytes 393224 | tf_op jit(solution)/shard_map/ppermute | solution.py:26
  80.4 8.3 %collective-permute-start.20 = (f16[2,16,2048]{2,1,0:T(8,128)(2,1)S(1)}, f16[2,16,2048]{2,1,0:T(8,128)(2,1)S(1)}, u32[]{:S(2)}, u32[]{:S(2)}) collective-permute-start(f16[2,16,2048]{2,1,0:T(8,128)(2,1)S(1)} %fusion.20), channel_id=1, source_target_pairs={{0,12},{2,14},{4,0},{6,2},{8,4},{10,6},{12,8},{14,10},{1,13},{3,15... | collective-permute-start | bytes 393224 | tf_op jit(solution)/shard_map/ppermute | solution.py:26

commit v4 on v3

--- a/solution.py
+++ b/solution.py
@@ -13,10 +13,13 @@
 SNAP = ("x", "yh")
 GROUP = 32
 CUT = GROUP // 2
+SPLIT = 1024
 KEPT = 2 * GROUP
 EARLY = ((0, 0), (0, 1), (-1, 0), (1, 0), (2, 0))
 LATE = ((2, 1), (-1, 1), (1, 1))
 TILE = 256
+WIDE = 512
+SLOTS = 4
 VMEM = pl.BlockSpec(memory_space=pltpu.VMEM)
 SMEM = pl.BlockSpec(memory_space=pltpu.SMEM)
 
@@ -42,32 +45,47 @@
     return pl.CostEstimate(flops=flops, bytes_accessed=moved, transcendentals=0)
 
 
-def prepare_kernel(weight, slab, weighted, norm):
-    wide = slab[...].astype(jnp.float32)
-    scaled = wide * weight[...]
-    weighted[...] = scaled.astype(jnp.bfloat16)
-    total = jnp.sum(scaled * wide, axis=1, keepdims=True)
-    norm[...] = jnp.transpose(jnp.broadcast_to(total, (total.shape[0], 128)))[0:1, :]
+def prepare_kernel(weight, slab, weighted, norm, parts, arrived):
+    steps = slab.shape[0] // TILE
+
+    def fetch(step):
+        slot = lax.rem(step, SLOTS)
+        rows = pl.ds(pl.multiple_of(step * TILE, TILE), TILE)
+        return pltpu.make_async_copy(slab.at[rows, :], parts.at[slot], arrived.at[slot])
+
+    for step in range(SLOTS):
+        fetch(step).start()
+
+    @pl.loop(0, steps)
+    def _(step):
+        fetch(step).wait()
+        at = pl.ds(pl.multiple_of(step * TILE, TILE), TILE)
+        wide = parts[lax.rem(step, SLOTS)].astype(jnp.float32)
+        scaled = wide * weight[...]
+        weighted[at, :] = scaled.astype(jnp.bfloat16)
+        total = jnp.sum(scaled * wide, axis=1, keepdims=True)
+        norm[:, at] = jnp.transpose(jnp.broadcast_to(total, (TILE, 128)))[0:1, :]
+
+        @pl.when(step + SLOTS < steps)
+        def _():
+            fetch(step + SLOTS).start()
 
 
 def prepare(weight, slab):
     rows, depth = slab.shape
     return pl.pallas_call(
         prepare_kernel,
-        grid=(rows // TILE,),
-        in_specs=[
-            pl.BlockSpec((1, depth), lambda i: (0, 0)),
-            pl.BlockSpec((TILE, depth), lambda i: (i, 0)),
-        ],
-        out_specs=[
-            pl.BlockSpec((TILE, depth), lambda i: (i, 0)),
-            pl.BlockSpec((1, TILE), lambda i: (0, i)),
-        ],
+        in_specs=[VMEM, pl.BlockSpec(memory_space=pltpu.HBM)],
+        out_specs=[VMEM, VMEM],
         out_shape=[
             jax.ShapeDtypeStruct((rows, depth), jnp.bfloat16),
             jax.ShapeDtypeStruct((1, rows), jnp.float32),
         ],
-        compiler_params=params(12),
+        scratch_shapes=[
+            pltpu.VMEM((SLOTS, TILE, depth), jnp.bfloat16),
+            pltpu.SemaphoreType.DMA((SLOTS,)),
+        ],
+        compiler_params=params(44),
         cost_estimate=cost(0, 2**20),
         name="prepare",
     )(weight, slab)
@@ -94,9 +112,9 @@
             wide = piece.astype(jnp.float32)
             norms[at, :] = jnp.sum(wide * wide * weight[...], axis=1, keepdims=True)
 
-    @pl.loop(0, slab.shape[0] // TILE)
+    @pl.loop(0, slab.shape[0] // WIDE)
     def _(n):
-        at = pl.ds(pl.multiple_of(n * TILE, TILE), TILE)
+        at = pl.ds(pl.multiple_of(n * WIDE, WIDE), WIDE)
         gram = lax.dot_general(
             rows[...], slab[at, :], (((1,), (1,)), ((), ())), preferred_element_type=jnp.float32
         )
@@ -211,36 +229,40 @@
     held = held.reshape(YL, Z, GROUP, columns)
 
     def second(k):
-        return held[:, k % Z, CUT:]
-
-    across = shift(pack(held[1, :, :CUT]), "yl", 1)
+        return held[:, k % Z, :, SPLIT:]
+
+    across = shift(pack(held[1, :, :, :SPLIT]), "yl", 1)
+    plus = shift(pack(jnp.stack([second(1), second(3)])), "z", 1)
     minus = shift(pack(jnp.stack([second(-1), second(-3)])), "z", -1)
-    plus = shift(pack(jnp.stack([second(1), second(3)])), "z", 1)
-    opposite = shift(pack(second(4)), "z", -2)
-    across, minus, plus, opposite = lax.optimization_barrier((across, minus, plus, opposite))
+    far_plus = shift(pack(second(4)[:, CUT:]), "z", 2)
+    far_minus = shift(pack(second(4)[:, :CUT]), "z", -2)
+    across, plus, minus, far_plus, far_minus = lax.optimization_barrier((across, plus, minus, far_plus, far_minus))
 
     def first(k):
-        return held[0, k % Z, :CUT] + unpack(across[k % Z])
+        return held[0, k % Z, :, :SPLIT] + unpack(across[k % Z])
 
     second_here = second(0) + unpack(minus[0]) + unpack(plus[0])
-    second_minus = second(-2) + unpack(minus[1]) + unpack(opposite)
-    second_plus = second(2) + unpack(plus[1])
+    top, bottom = ((0, 0), (0, CUT), (0, 0)), ((0, 0), (CUT, 0), (0, 0))
+    second_minus = second(-2) + unpack(minus[1]) + jnp.pad(unpack(far_minus), top)
+    second_plus = second(2) + unpack(plus[1]) + jnp.pad(unpack(far_plus), bottom)
     across_second = shift(pack(jnp.stack([second_here[1], second_minus[1], second_plus[1]])), "yl", 1)
+    plus_first = shift(pack(jnp.stack([first(1), first(3)])), "z", 1)
     minus_first = shift(pack(jnp.stack([first(-1), first(-3)])), "z", -1)
-    plus_first = shift(pack(jnp.stack([first(1), first(3)])), "z", 1)
     opposite_first = shift(pack(first(4)), "z", 2)
-    across_second, minus_first, plus_first, opposite_first = lax.optimization_barrier(
-        (across_second, minus_first, plus_first, opposite_first)
-    )
-
-    end_minus = jnp.stack([first(-2) + unpack(minus_first[1]), second_minus[0] + unpack(across_second[1])])
-    end_plus = jnp.stack(
-        [first(2) + unpack(plus_first[1]) + unpack(opposite_first), second_plus[0] + unpack(across_second[2])]
-    )
-    end_minus, end_plus = shift(pack(end_minus), "z", -2), shift(pack(end_plus), "z", 2)
+    across_second, plus_first, minus_first, opposite_first = lax.optimization_barrier(
+        (across_second, plus_first, minus_first, opposite_first)
+    )
+
+    end_minus = jnp.concatenate(
+        [first(-2) + unpack(minus_first[1]), second_minus[0] + unpack(across_second[1])], axis=1
+    )
+    end_plus = jnp.concatenate(
+        [first(2) + unpack(plus_first[1]) + unpack(opposite_first), second_plus[0] + unpack(across_second[2])], axis=1
+    )
+    end_plus, end_minus = shift(pack(end_plus), "z", 2), shift(pack(end_minus), "z", -2)
     first_sum = first(0) + unpack(minus_first[0]) + unpack(plus_first[0])
     second_sum = second_here[0] + unpack(across_second[0])
-    distance = jnp.concatenate([first_sum, second_sum]) + (unpack(end_minus) + unpack(end_plus)).reshape(GROUP, columns)
+    distance = jnp.concatenate([first_sum, second_sum], axis=1) + unpack(end_minus) + unpack(end_plus)
     return jnp.exp(-distance / spread[0])
 
 

time: 91.3 us -> 87.4 us (0.957)
  local copies, waits for them, and re-layouts: 4.66 us -> 1.41 us
  starting transfers between devices: 42.9 us -> 40.5 us
  waiting for transfers between devices: 18 us -> 20 us
    unnamed x6 -> x4, local copies, waits for them, and re-layouts: 3.39 us -> 0.01 us
    ppermute x22 -> x23, starting transfers between devices: 42.9 us -> 40.5 us  [shift(): lax.ppermute(value, axis, [(i, (i + by) % size) for i in range(size)])]
    ppermute x22 -> x23, waiting for transfers between devices: 18 us -> 20 us  [shift(): lax.ppermute(value, axis, [(i, (i + by) % size) for i in range(size)])]
    pallas_call x1, Pallas kernels: 3.87 us -> 4.89 us  [prepare(): pl.pallas_call(prepare_kernel, in_specs=[VMEM, pl.BlockSpec(memory_space=...]
  transfers between devices with their start and end apart: 22 -> 23, of which waited for: 5 -> 6; matrix products, arithmetic and copies ran while one was open for 9% -> 9% of each run, Pallas kernels for 15% -> 15%
where the time goes in v4:
time: 87.4 us; the launch traced here: 86.1 us
  starting transfers between devices  40.5 us (46%)
  waiting for transfers between devices  20 us (23%)
  Pallas kernels  14 us (16%)
  matrix products  6.91 us (8%)
  other arithmetic  2.29 us (3%)
  local copies, waits for them, and re-layouts  1.41 us (2%)
  between operations  0.98 us (1%)
    ppermute x23, starting transfers between devices, shift(): lax.ppermute(value, axis, [(i, (i + by) % size) for i in range(size)])  40.5 us
    ppermute x23, waiting for transfers between devices, shift(): lax.ppermute(value, axis, [(i, (i + by) % size) for i in range(size)])  20 us
    pallas_call x1, Pallas kernels, early_partial(): pl.pallas_call(functools.partial(early_kernel, offsets), in_specs=[SMEM]...  7.56 us
    dot_general x2, matrix products, partial(): lax.dot_general(rows, weighted_slab, (((1,), (1,)), ((), ())), preferred_...  5.86 us
    pallas_call x1, Pallas kernels, prepare(): pl.pallas_call(prepare_kernel, in_specs=[VMEM, pl.BlockSpec(memory_space=...  4.89 us
  transfers between devices with their start and end apart: 23, of which 6 were waited for; matrix products, arithmetic and copies ran while one was open for 9% of the time, Pallas kernels for 15%

profile of v4, /device:TPU:32, one launch (start us, length us, event | category | flops | bytes accessed | tf_op | source)
XLA Modules:
  0.0 86.1 jit_solution(13865412015284115841)
XLA Ops:
  0.0 1.1 %constant_dynamic-slice_fusion = (bf16[2,1,32,2048]{3,2,1,0:T(8,128)(2,1)S(1)}, bf16[2,1,32,2048]{3,2,1,0:T(8,128)(2,1)S(1)}) fusion(bf16[2,2,32,2048]{3,2,1,0:T(8,128)(2,1)} %bitcast.161, s32[]{:T(128)S(6)} %select_n.8, s32[]{:T(128)S(6)} %select_n.7), kind=kLoop, calls=%fused_computation.85 | loop fusion | bytes 1048584 | tf_op jit(solution)/shard_map/jit(dynamic_index_in_dim)/dynamic_slice | solution.py:183
  1.1 1.6 %collective-permute-start.2 = (bf16[64,2048]{1,0:T(8,128)(2,1)S(1)}, bf16[64,2048]{1,0:T(8,128)(2,1)S(1)}, u32[]{:S(2)}, u32[]{:S(2)}) collective-permute-start(bf16[64,2048]{1,0:T(8,128)(2,1)S(1)} %bitcast.150), channel_id=1, source_target_pairs={{0,64},{64,128},{128,192},{192,0},{1,65},{65,129},{129,193},{193,1... | collective-permute-start | bytes 786440 | tf_op jit(solution)/shard_map/ppermute | solution.py:29
  2.7 1.7 %collective-permute-start = (bf16[64,2048]{1,0:T(8,128)(2,1)S(1)}, bf16[64,2048]{1,0:T(8,128)(2,1)S(1)}, u32[]{:S(2)}, u32[]{:S(2)}) collective-permute-start(bf16[64,2048]{1,0:T(8,128)(2,1)S(1)} %bitcast.154), channel_id=1, source_target_pairs={{0,192},{64,0},{128,64},{192,128},{1,193},{65,1},{129,65},{193,129... | collective-permute-start | bytes 786440 | tf_op jit(solution)/shard_map/ppermute | solution.py:29
  4.5 3.3 %collective-permute-start.5 = (bf16[128,2048]{1,0:T(8,128)(2,1)S(1)}, bf16[128,2048]{1,0:T(8,128)(2,1)S(1)}, u32[]{:S(2)}, u32[]{:S(2)}) collective-permute-start(bf16[128,2048]{1,0:T(8,128)(2,1)S(1)} %pad_maximum_fusion.3), channel_id=1, source_target_pairs={{0,32},{32,0},{1,33},{33,1},{2,34},{34,2},{3,35},{35,3},{4,36},{36... | collective-permute-start | bytes 1572872 | tf_op jit(solution)/shard_map/ppermute | solution.py:29
  7.7 2.7 %collective-permute-done.2.refs_7_ = bf16[64,2048]{1,0:T(8,128)(2,1)S(1)} collective-permute-done((bf16[64,2048]{1,0:T(8,128)(2,1)S(1)}, bf16[64,2048]{1,0:T(8,128)(2,1)S(1)}, u32[]{:S(2)}, u32[]{:S(2)}) %collective-permute-start.2) | collective-permute-done | bytes 262176 | tf_op jit(solution)/shard_map/ppermute | solution.py:29
  10.4 0.3 collective-permute-start.3
  10.7 0.0 collective-permute-done.refs_3_
  10.7 3.0 %collective-permute-start.1 = (bf16[64,2048]{1,0:T(8,128)(2,1)S(1)}, bf16[64,2048]{1,0:T(8,128)(2,1)S(1)}, u32[]{:S(2)}, u32[]{:S(2)}) collective-permute-start(bf16[64,2048]{1,0:T(8,128)(2,1)S(1)} %collective-permute-done.refs_3_), channel_id=1, source_target_pairs={{0,192},{64,0},{128,64},{192,128},{1,193},{65,1},{129,65},{193,129... | collective-permute-start | bytes 786440 | tf_op jit(solution)/shard_map/ppermute | solution.py:29
  13.7 1.0 %fusion.2.weight = f32[1,2048]{1,0:T(1,128)S(1)} fusion(f32[256,1]{0,1:T(1,128)S(1)} %bitcast.143, s32[2048]{0:T(1024)S(1)} %copy-done.1), kind=kOutput, calls=%fused_computation.5 | convolution fusion | flops 6815744 | bytes 17408 | tf_op jit(solution)/shard_map/dot_general | solution.py:191
  14.7 0.0 collective-permute-start.8
  14.8 3.2 %collective-permute-start.9 = (bf16[64,2048]{1,0:T(8,128)(2,1)S(1)}, bf16[64,2048]{1,0:T(8,128)(2,1)S(1)}, u32[]{:S(2)}, u32[]{:S(2)}) collective-permute-start(bf16[64,2048]{1,0:T(8,128)(2,1)S(1)} %bitcast.152), channel_id=1, source_target_pairs={{0,192},{64,0},{128,64},{192,128},{1,193},{65,1},{129,65},{193,129... | collective-permute-start | bytes 786440 | tf_op jit(solution)/shard_map/ppermute | solution.py:29
  18.0 4.9 %prepare.1 = (bf16[2048,2048]{1,0:T(8,128)(2,1)S(1)}, f32[1,2048]{1,0:T(1,128)S(1)}) custom-call(f32[1,2048]{1,0:T(1,128)S(1)} %fusion.2.weight, bf16[2048,2048]{1,0:T(8,128)(2,1)} %slab.1), custom_call_target="tpu_custom_call" | custom-call | bytes 1048576 | tf_op jit(solution)/shard_map/prepare/pallas_call | solution.py:76
  22.9 0.1 pad_add_fusion.place
  23.0 0.0 collective-permute-done.3.refs_9_
  23.0 0.0 collective-permute-done.1.refs_4_
  23.0 3.3 %collective-permute-start.4 = (bf16[128,2048]{1,0:T(8,128)(2,1)S(1)}, bf16[128,2048]{1,0:T(8,128)(2,1)S(1)}, u32[]{:S(2)}, u32[]{:S(2)}) collective-permute-start(bf16[128,2048]{1,0:T(8,128)(2,1)S(1)} %pad_maximum_fusion.2), channel_id=1, source_target_pairs={{0,32},{32,0},{1,33},{33,1},{2,34},{34,2},{3,35},{35,3},{4,36},{36... | collective-permute-start | bytes 1572872 | tf_op jit(solution)/shard_map/ppermute | solution.py:29
  26.3 0.0 collective-permute-done.5
  26.3 0.0 collective-permute-start.6
  26.3 3.2 %collective-permute-start.7 = (bf16[128,2048]{1,0:T(8,128)(2,1)S(1)}, bf16[128,2048]{1,0:T(8,128)(2,1)S(1)}, u32[]{:S(2)}, u32[]{:S(2)}) collective-permute-start(bf16[128,2048]{1,0:T(8,128)(2,1)S(1)} %collective-permute-done.5), channel_id=1, source_target_pairs={{0,192},{64,0},{128,64},{192,128},{1,193},{65,1},{129,65},{193,129... | collective-permute-start | bytes 1572872 | tf_op jit(solution)/shard_map/ppermute | solution.py:29
  29.6 0.0 collective-permute-done.8.refs_2_
  29.6 0.0 collective-permute-done.9.refs_8_
  29.6 7.6 %early_partial.1 = (f32[320,2048]{1,0:T(8,128)S(1)}, f32[512,2048]{1,0:T(8,128)S(1)}) custom-call(s32[4]{0:T(128)S(1)} %pad_add_fusion.place, f32[1,2048]{1,0:T(1,128)S(1)} %fusion.2.weight, f32[1,2048]{1,0:T(1,128)S(1)} %get-tuple-element.25.slab_norm, bf16[2048,2048]{1,0:T(8,128)(2,1)S(1)} %get-tuple-element.26.slab, bf16[64,2048]{1,0:T(8,128)(2,1)S(1)} %bitcast.157, ...), custom_call_target="tpu_custom_call" | custom-call | flops 30000001024 | bytes 65536 | tf_op jit(solution)/shard_map/early_partial/pallas_call | solution.py:133
  37.2 0.3 collective-permute-start.11
  37.5 0.0 collective-permute-done.4
  37.5 1.4 %collective-permute-done.6 = bf16[128,2048]{1,0:T(8,128)(2,1)S(1)} collective-permute-done((bf16[128,2048]{1,0:T(8,128)(2,1)S(1)}, bf16[128,2048]{1,0:T(8,128)(2,1)S(1)}, u32[]{:S(2)}, u32[]{:S(2)}) %collective-permute-start.6) | collective-permute-done | bytes 524320 | tf_op jit(solution)/shard_map/ppermute | solution.py:29
  38.9 0.0 collective-permute-done.7
  38.9 0.1 fusion.45
  39.0 0.5 multiply_reduce_fusion
  39.5 2.9 %fusion = f32[192,2048]{1,0:T(8,128)S(1)} fusion(bf16[2048,2048]{1,0:T(8,128)(2,1)S(1)} %get-tuple-element.26.slab, f32[2048]{0:T(1024)S(1)} %bitcast.159, f32[192]{0:T(256)S(1)} %get-tuple-element.44, bf16[64,2048]{1,0:T(8,128)(2,1)S(1)} %get-tuple-element.64, bf16[64,2048]{1,0:T(8,128)(2,1)S(1)} %get-tuple-element.76, ...), kind=kOutput, calls=%fused_computation.2 | convolution fusion | flops 1614151680 | bytes 10756864 | tf_op jit(solution)/shard_map/dot_general | solution.py:219
  42.5 0.1 collective-permute-start.10
  42.6 2.9 %fusion.1.refs_1_ = f32[192,2048]{1,0:T(8,128)S(1)} fusion(bf16[2048,2048]{1,0:T(8,128)(2,1)S(1)} %get-tuple-element.26.slab, f32[192]{0:T(256)S(1)} %get-tuple-element.43, f32[2048]{0:T(1024)S(1)} %bitcast.160, bf16[64,2048]{1,0:T(8,128)(2,1)S(1)} %get-tuple-element.65, bf16[64,2048]{1,0:T(8,128)(2,1)S(1)} %get-tuple-element.75, ...), kind=kOutput, calls=%fused_computation.3 | convolution fusion | flops 1614151680 | bytes 10756864 | tf_op jit(solution)/shard_map/dot_general | solution.py:219
  45.5 0.0 collective-permute-done.11.refs_0_
  45.5 0.9 %add_into.2.refs_2_ = f32[512,2048]{1,0:T(8,128)S(1)} custom-call(s32[4]{0:T(128)S(1)} %pad_add_fusion.place, f32[320,2048]{1,0:T(8,128)S(1)} %collective-permute-done.11.refs_0_, f32[512,2048]{1,0:T(8,128)S(1)} %get-tuple-element.33.refs_1_), custom_call_target="tpu_custom_call", output_to_operand_aliasing={{}: (2, {})} | custom-call | bytes 65536 | tf_op jit(solution)/shard_map/add_into/pallas_call | solution.py:165
  46.4 0.0 collective-permute-done.10.refs_0_
  46.4 0.7 add_into.3
  47.1 0.1 fusion.5
  47.2 0.1 slice_bitcast_fusion.3
  47.4 0.8 collective-permute-start.12
  48.2 2.0 %collective-permute-start.13 = (f16[2,2,32,1024]{3,2,1,0:T(8,128)(2,1)S(1)}, f16[2,2,32,1024]{3,2,1,0:T(8,128)(2,1)S(1)}, u32[]{:S(2)}, u32[]{:S(2)}) collective-permute-start(f16[2,2,32,1024]{3,2,1,0:T(8,128)(2,1)S(1)} %fusion.6), channel_id=1, source_target_pairs={{0,2},{2,4},{4,6},{6,8},{8,10},{10,12},{12,14},{14,0},{1,3},{3,5},... | collective-permute-start | bytes 786440 | tf_op jit(solution)/shard_map/ppermute | solution.py:29
  50.3 0.2 collective-permute-start.14
  50.5 4.5 %collective-permute-start.15 = (f16[2,16,1024]{2,1,0:T(8,128)(2,1)S(1)}, f16[2,16,1024]{2,1,0:T(8,128)(2,1)S(1)}, u32[]{:S(2)}, u32[]{:S(2)}) collective-permute-start(f16[2,16,1024]{2,1,0:T(8,128)(2,1)S(1)} %get-tuple-element.71), channel_id=1, source_target_pairs={{0,4},{2,6},{4,8},{6,10},{8,12},{10,14},{12,0},{14,2},{1,5},{3,7},... | collective-permute-start | bytes 196616 | tf_op jit(solution)/shard_map/ppermute | solution.py:29
  55.0 1.1 %collective-permute-start.16 = (f16[2,16,1024]{2,1,0:T(8,128)(2,1)S(1)}, f16[2,16,1024]{2,1,0:T(8,128)(2,1)S(1)}, u32[]{:S(2)}, u32[]{:S(2)}) collective-permute-start(f16[2,16,1024]{2,1,0:T(8,128)(2,1)S(1)} %get-tuple-element.70), channel_id=1, source_target_pairs={{0,12},{2,14},{4,0},{6,2},{8,4},{10,6},{12,8},{14,10},{1,13},{3,15... | collective-permute-start | bytes 196616 | tf_op jit(solution)/shard_map/ppermute | solution.py:29
  56.0 6.3 %collective-permute-done.15 = f16[2,16,1024]{2,1,0:T(8,128)(2,1)S(1)} collective-permute-done((f16[2,16,1024]{2,1,0:T(8,128)(2,1)S(1)}, f16[2,16,1024]{2,1,0:T(8,128)(2,1)S(1)}, u32[]{:S(2)}, u32[]{:S(2)}) %collective-permute-start.15) | collective-permute-done | bytes 65568 | tf_op jit(solution)/shard_map/ppermute | solution.py:29
  62.3 0.3 collective-permute-done.16
  62.6 0.0 collective-permute-done.13
  62.6 0.0 collective-permute-done.14
  62.6 0.0 collective-permute-done.12
  62.7 0.2 fusion.12
  63.0 1.4 %collective-permute-start.17 = (f16[3,32,1024]{2,1,0:T(8,128)(2,1)S(1)}, f16[3,32,1024]{2,1,0:T(8,128)(2,1)S(1)}, u32[]{:S(2)}, u32[]{:S(2)}) collective-permute-start(f16[3,32,1024]{2,1,0:T(8,128)(2,1)S(1)} %fusion.8), channel_id=1, source_target_pairs={{0,16},{16,0},{1,17},{17,1},{2,18},{18,2},{3,19},{19,3},{4,20},{20... | collective-permute-start | bytes 589832 | tf_op jit(solution)/shard_map/ppermute | solution.py:29
  64.4 0.1 fusion.35
  64.5 4.4 %collective-permute-start.18 = (f16[2,32,1024]{2,1,0:T(8,128)(2,1)S(1)}, f16[2,32,1024]{2,1,0:T(8,128)(2,1)S(1)}, u32[]{:S(2)}, u32[]{:S(2)}) collective-permute-start(f16[2,32,1024]{2,1,0:T(8,128)(2,1)S(1)} %fusion.15), channel_id=1, source_target_pairs={{0,2},{2,4},{4,6},{6,8},{8,10},{10,12},{12,14},{14,0},{1,3},{3,5},... | collective-permute-start | bytes 393224 | tf_op jit(solution)/shard_map/ppermute | solution.py:29
  69.0 0.3 collective-permute-start.19
  69.3 1.5 %collective-permute-start.20 = (f16[32,1024]{1,0:T(8,128)(2,1)S(1)}, f16[32,1024]{1,0:T(8,128)(2,1)S(1)}, u32[]{:S(2)}, u32[]{:S(2)}) collective-permute-start(f16[32,1024]{1,0:T(8,128)(2,1)S(1)} %fusion.33), channel_id=1, source_target_pairs={{0,4},{2,6},{4,8},{6,10},{8,12},{10,14},{12,0},{14,2},{1,5},{3,7},... | collective-permute-start | bytes 196616 | tf_op jit(solution)/shard_map/ppermute | solution.py:29
  70.9 5.7 %collective-permute-done.20 = f16[32,1024]{1,0:T(8,128)(2,1)S(1)} collective-permute-done((f16[32,1024]{1,0:T(8,128)(2,1)S(1)}, f16[32,1024]{1,0:T(8,128)(2,1)S(1)}, u32[]{:S(2)}, u32[]{:S(2)}) %collective-permute-start.20) | collective-permute-done | bytes 65568 | tf_op jit(solution)/shard_map/ppermute | solution.py:29
  76.5 0.0 collective-permute-done.18
  76.5 0.0 collective-permute-done.19
  76.5 0.0 collective-permute-done.17
  76.6 0.1 fusion.27
  76.6 0.1 fusion.29
  76.8 0.1 collective-permute-start.22
  76.9 4.2 %collective-permute-start.21 = (f16[32,2048]{1,0:T(8,128)(2,1)S(1)}, f16[32,2048]{1,0:T(8,128)(2,1)S(1)}, u32[]{:S(2)}, u32[]{:S(2)}) collective-permute-start(f16[32,2048]{1,0:T(8,128)(2,1)S(1)} %fusion.21), channel_id=1, source_target_pairs={{0,12},{2,14},{4,0},{6,2},{8,4},{10,6},{12,8},{14,10},{1,13},{3,15... | collective-permute-start | bytes 393224 | tf_op jit(solution)/shard_map/ppermute | solution.py:29
  81.7 3.5 %collective-permute-done.22 = f16[32,2048]{1,0:T(8,128)(2,1)S(1)} collective-permute-done((f16[32,2048]{1,0:T(8,128)(2,1)S(1)}, f16[32,2048]{1,0:T(8,128)(2,1)S(1)}, u32[]{:S(2)}, u32[]{:S(2)}) %collective-permute-start.22) | collective-permute-done | bytes 131104 | tf_op jit(solution)/shard_map/ppermute | solution.py:29
  85.3 0.0 collective-permute-done.21
  85.3 0.8 fusion.20
  (22 shorter events, 0.5 us)
Async XLA Ops:
  0.0 13.7 %copy-start = (f32[256]{0:T(256)S(1)}, f32[256]{0:T(256)}, u32[]{:S(2)}) copy-start(f32[256]{0:T(256)} %param.8) | copy-start | bytes 3076
  0.0 13.7 %copy-start.1 = (s32[2048]{0:T(1024)S(1)}, s32[2048]{0:T(1024)}, u32[]{:S(2)}) copy-start(s32[2048]{0:T(1024)} %param.7) | copy-start | bytes 24580
  1.1 9.3 %collective-permute-start.2 = (bf16[64,2048]{1,0:T(8,128)(2,1)S(1)}, bf16[64,2048]{1,0:T(8,128)(2,1)S(1)}, u32[]{:S(2)}, u32[]{:S(2)}) collective-permute-start(bf16[64,2048]{1,0:T(8,128)(2,1)S(1)} %bitcast.150), channel_id=1, source_target_pairs={{0,64},{64,128},{128,192},{192,0},{1,65},{65,129},{129,193},{193,1... | collective-permute-start | bytes 786440 | tf_op jit(solution)/shard_map/ppermute | solution.py:29
  2.7 8.0 %collective-permute-start = (bf16[64,2048]{1,0:T(8,128)(2,1)S(1)}, bf16[64,2048]{1,0:T(8,128)(2,1)S(1)}, u32[]{:S(2)}, u32[]{:S(2)}) collective-permute-start(bf16[64,2048]{1,0:T(8,128)(2,1)S(1)} %bitcast.154), channel_id=1, source_target_pairs={{0,192},{64,0},{128,64},{192,128},{1,193},{65,1},{129,65},{193,129... | collective-permute-start | bytes 786440 | tf_op jit(solution)/shard_map/ppermute | solution.py:29
  4.5 21.9 %collective-permute-start.5 = (bf16[128,2048]{1,0:T(8,128)(2,1)S(1)}, bf16[128,2048]{1,0:T(8,128)(2,1)S(1)}, u32[]{:S(2)}, u32[]{:S(2)}) collective-permute-start(bf16[128,2048]{1,0:T(8,128)(2,1)S(1)} %pad_maximum_fusion.3), channel_id=1, source_target_pairs={{0,32},{32,0},{1,33},{33,1},{2,34},{34,2},{3,35},{35,3},{4,36},{36... | collective-permute-start | bytes 1572872 | tf_op jit(solution)/shard_map/ppermute | solution.py:29
  10.4 12.5 %collective-permute-start.3 = (bf16[64,2048]{1,0:T(8,128)(2,1)S(1)}, bf16[64,2048]{1,0:T(8,128)(2,1)S(1)}, u32[]{:S(2)}, u32[]{:S(2)}) collective-permute-start(bf16[64,2048]{1,0:T(8,128)(2,1)S(1)} %collective-permute-done.2.refs_7_), channel_id=1, source_target_pairs={{0,64},{64,128},{128,192},{192,0},{1,65},{65,129},{129,193},{193,1... | collective-permute-start | bytes 786440 | tf_op jit(solution)/shard_map/ppermute | solution.py:29
  10.7 12.3 %collective-permute-start.1 = (bf16[64,2048]{1,0:T(8,128)(2,1)S(1)}, bf16[64,2048]{1,0:T(8,128)(2,1)S(1)}, u32[]{:S(2)}, u32[]{:S(2)}) collective-permute-start(bf16[64,2048]{1,0:T(8,128)(2,1)S(1)} %collective-permute-done.refs_3_), channel_id=1, source_target_pairs={{0,192},{64,0},{128,64},{192,128},{1,193},{65,1},{129,65},{193,129... | collective-permute-start | bytes 786440 | tf_op jit(solution)/shard_map/ppermute | solution.py:29
  14.7 14.9 %collective-permute-start.8 = (bf16[64,2048]{1,0:T(8,128)(2,1)S(1)}, bf16[64,2048]{1,0:T(8,128)(2,1)S(1)}, u32[]{:S(2)}, u32[]{:S(2)}) collective-permute-start(bf16[64,2048]{1,0:T(8,128)(2,1)S(1)} %bitcast.156), channel_id=1, source_target_pairs={{0,64},{64,128},{128,192},{192,0},{1,65},{65,129},{129,193},{193,1... | collective-permute-start | bytes 786440 | tf_op jit(solution)/shard_map/ppermute | solution.py:29
  14.8 14.8 %collective-permute-start.9 = (bf16[64,2048]{1,0:T(8,128)(2,1)S(1)}, bf16[64,2048]{1,0:T(8,128)(2,1)S(1)}, u32[]{:S(2)}, u32[]{:S(2)}) collective-permute-start(bf16[64,2048]{1,0:T(8,128)(2,1)S(1)} %bitcast.152), channel_id=1, source_target_pairs={{0,192},{64,0},{128,64},{192,128},{1,193},{65,1},{129,65},{193,129... | collective-permute-start | bytes 786440 | tf_op jit(solution)/shard_map/ppermute | solution.py:29
  23.0 14.4 %collective-permute-start.4 = (bf16[128,2048]{1,0:T(8,128)(2,1)S(1)}, bf16[128,2048]{1,0:T(8,128)(2,1)S(1)}, u32[]{:S(2)}, u32[]{:S(2)}) collective-permute-start(bf16[128,2048]{1,0:T(8,128)(2,1)S(1)} %pad_maximum_fusion.2), channel_id=1, source_target_pairs={{0,32},{32,0},{1,33},{33,1},{2,34},{34,2},{3,35},{35,3},{4,36},{36... | collective-permute-start | bytes 1572872 | tf_op jit(solution)/shard_map/ppermute | solution.py:29
  26.3 12.6 %collective-permute-start.6 = (bf16[128,2048]{1,0:T(8,128)(2,1)S(1)}, bf16[128,2048]{1,0:T(8,128)(2,1)S(1)}, u32[]{:S(2)}, u32[]{:S(2)}) collective-permute-start(bf16[128,2048]{1,0:T(8,128)(2,1)S(1)} %collective-permute-done.5), channel_id=1, source_target_pairs={{0,64},{64,128},{128,192},{192,0},{1,65},{65,129},{129,193},{193,1... | collective-permute-start | bytes 1572872 | tf_op jit(solution)/shard_map/ppermute | solution.py:29
  26.3 12.6 %collective-permute-start.7 = (bf16[128,2048]{1,0:T(8,128)(2,1)S(1)}, bf16[128,2048]{1,0:T(8,128)(2,1)S(1)}, u32[]{:S(2)}, u32[]{:S(2)}) collective-permute-start(bf16[128,2048]{1,0:T(8,128)(2,1)S(1)} %collective-permute-done.5), channel_id=1, source_target_pairs={{0,192},{64,0},{128,64},{192,128},{1,193},{65,1},{129,65},{193,129... | collective-permute-start | bytes 1572872 | tf_op jit(solution)/shard_map/ppermute | solution.py:29
  37.2 8.3 %collective-permute-start.11 = (f32[320,2048]{1,0:T(8,128)S(1)}, f32[320,2048]{1,0:T(8,128)S(1)}, u32[]{:S(2)}, u32[]{:S(2)}) collective-permute-start(f32[320,2048]{1,0:T(8,128)S(1)} %get-tuple-element.29), channel_id=1, source_target_pairs={{0,1},{1,0},{2,3},{3,2},{4,5},{5,4},{6,7},{7,6},{8,9},{9,8},{10,11... | collective-permute-start | bytes 7864328 | tf_op jit(solution)/shard_map/ppermute | solution.py:29
  42.5 4.0 %collective-permute-start.10 = (f32[192,2048]{1,0:T(8,128)S(1)}, f32[192,2048]{1,0:T(8,128)S(1)}, u32[]{:S(2)}, u32[]{:S(2)}) collective-permute-start(f32[192,2048]{1,0:T(8,128)S(1)} %fusion), channel_id=1, source_target_pairs={{0,1},{1,0},{2,3},{3,2},{4,5},{5,4},{6,7},{7,6},{8,9},{9,8},{10,11... | collective-permute-start | bytes 4718600 | tf_op jit(solution)/shard_map/ppermute | solution.py:29
  47.4 15.3 %collective-permute-start.12 = (f16[8,32,1024]{2,1,0:T(8,128)(2,1)S(1)}, f16[8,32,1024]{2,1,0:T(8,128)(2,1)S(1)}, u32[]{:S(2)}, u32[]{:S(2)}) collective-permute-start(f16[8,32,1024]{2,1,0:T(8,128)(2,1)S(1)} %fusion.5), channel_id=1, source_target_pairs={{0,16},{16,0},{1,17},{17,1},{2,18},{18,2},{3,19},{19,3},{4,20},{20... | collective-permute-start | bytes 1572872 | tf_op jit(solution)/shard_map/ppermute | solution.py:29
  48.2 14.4 %collective-permute-start.13 = (f16[2,2,32,1024]{3,2,1,0:T(8,128)(2,1)S(1)}, f16[2,2,32,1024]{3,2,1,0:T(8,128)(2,1)S(1)}, u32[]{:S(2)}, u32[]{:S(2)}) collective-permute-start(f16[2,2,32,1024]{3,2,1,0:T(8,128)(2,1)S(1)} %fusion.6), channel_id=1, source_target_pairs={{0,2},{2,4},{4,6},{6,8},{8,10},{10,12},{12,14},{14,0},{1,3},{3,5},... | collective-permute-start | bytes 786440 | tf_op jit(solution)/shard_map/ppermute | solution.py:29
  50.3 12.4 %collective-permute-start.14 = (f16[2,2,32,1024]{3,2,1,0:T(8,128)(2,1)S(1)}, f16[2,2,32,1024]{3,2,1,0:T(8,128)(2,1)S(1)}, u32[]{:S(2)}, u32[]{:S(2)}) collective-permute-start(f16[2,2,32,1024]{3,2,1,0:T(8,128)(2,1)S(1)} %fusion.7), channel_id=1, source_target_pairs={{0,14},{2,0},{4,2},{6,4},{8,6},{10,8},{12,10},{14,12},{1,15},{3,1}... | collective-permute-start | bytes 786440 | tf_op jit(solution)/shard_map/ppermute | solution.py:29
  50.5 11.9 %collective-permute-start.15 = (f16[2,16,1024]{2,1,0:T(8,128)(2,1)S(1)}, f16[2,16,1024]{2,1,0:T(8,128)(2,1)S(1)}, u32[]{:S(2)}, u32[]{:S(2)}) collective-permute-start(f16[2,16,1024]{2,1,0:T(8,128)(2,1)S(1)} %get-tuple-element.71), channel_id=1, source_target_pairs={{0,4},{2,6},{4,8},{6,10},{8,12},{10,14},{12,0},{14,2},{1,5},{3,7},... | collective-permute-start | bytes 196616 | tf_op jit(solution)/shard_map/ppermute | solution.py:29
  55.0 7.7 %collective-permute-start.16 = (f16[2,16,1024]{2,1,0:T(8,128)(2,1)S(1)}, f16[2,16,1024]{2,1,0:T(8,128)(2,1)S(1)}, u32[]{:S(2)}, u32[]{:S(2)}) collective-permute-start(f16[2,16,1024]{2,1,0:T(8,128)(2,1)S(1)} %get-tuple-element.70), channel_id=1, source_target_pairs={{0,12},{2,14},{4,0},{6,2},{8,4},{10,6},{12,8},{14,10},{1,13},{3,15... | collective-permute-start | bytes 196616 | tf_op jit(solution)/shard_map/ppermute | solution.py:29
  63.0 13.6 %collective-permute-start.17 = (f16[3,32,1024]{2,1,0:T(8,128)(2,1)S(1)}, f16[3,32,1024]{2,1,0:T(8,128)(2,1)S(1)}, u32[]{:S(2)}, u32[]{:S(2)}) collective-permute-start(f16[3,32,1024]{2,1,0:T(8,128)(2,1)S(1)} %fusion.8), channel_id=1, source_target_pairs={{0,16},{16,0},{1,17},{17,1},{2,18},{18,2},{3,19},{19,3},{4,20},{20... | collective-permute-start | bytes 589832 | tf_op jit(solution)/shard_map/ppermute | solution.py:29
  64.5 12.0 %collective-permute-start.18 = (f16[2,32,1024]{2,1,0:T(8,128)(2,1)S(1)}, f16[2,32,1024]{2,1,0:T(8,128)(2,1)S(1)}, u32[]{:S(2)}, u32[]{:S(2)}) collective-permute-start(f16[2,32,1024]{2,1,0:T(8,128)(2,1)S(1)} %fusion.15), channel_id=1, source_target_pairs={{0,2},{2,4},{4,6},{6,8},{8,10},{10,12},{12,14},{14,0},{1,3},{3,5},... | collective-permute-start | bytes 393224 | tf_op jit(solution)/shard_map/ppermute | solution.py:29
  69.0 7.6 %collective-permute-start.19 = (f16[2,32,1024]{2,1,0:T(8,128)(2,1)S(1)}, f16[2,32,1024]{2,1,0:T(8,128)(2,1)S(1)}, u32[]{:S(2)}, u32[]{:S(2)}) collective-permute-start(f16[2,32,1024]{2,1,0:T(8,128)(2,1)S(1)} %fusion.16), channel_id=1, source_target_pairs={{0,14},{2,0},{4,2},{6,4},{8,6},{10,8},{12,10},{14,12},{1,15},{3,1}... | collective-permute-start | bytes 393224 | tf_op jit(solution)/shard_map/ppermute | solution.py:29
  69.3 7.2 %collective-permute-start.20 = (f16[32,1024]{1,0:T(8,128)(2,1)S(1)}, f16[32,1024]{1,0:T(8,128)(2,1)S(1)}, u32[]{:S(2)}, u32[]{:S(2)}) collective-permute-start(f16[32,1024]{1,0:T(8,128)(2,1)S(1)} %fusion.33), channel_id=1, source_target_pairs={{0,4},{2,6},{4,8},{6,10},{8,12},{10,14},{12,0},{14,2},{1,5},{3,7},... | collective-permute-start | bytes 196616 | tf_op jit(solution)/shard_map/ppermute | solution.py:29
  76.8 8.5 %collective-permute-start.22 = (f16[32,2048]{1,0:T(8,128)(2,1)S(1)}, f16[32,2048]{1,0:T(8,128)(2,1)S(1)}, u32[]{:S(2)}, u32[]{:S(2)}) collective-permute-start(f16[32,2048]{1,0:T(8,128)(2,1)S(1)} %fusion.22), channel_id=1, source_target_pairs={{0,4},{2,6},{4,8},{6,10},{8,12},{10,14},{12,0},{14,2},{1,5},{3,7},... | collective-permute-start | bytes 393224 | tf_op jit(solution)/shard_map/ppermute | solution.py:29
  76.9 8.4 %collective-permute-start.21 = (f16[32,2048]{1,0:T(8,128)(2,1)S(1)}, f16[32,2048]{1,0:T(8,128)(2,1)S(1)}, u32[]{:S(2)}, u32[]{:S(2)}) collective-permute-start(f16[32,2048]{1,0:T(8,128)(2,1)S(1)} %fusion.21), channel_id=1, source_target_pairs={{0,12},{2,14},{4,0},{6,2},{8,4},{10,6},{12,8},{14,10},{1,13},{3,15... | collective-permute-start | bytes 393224 | tf_op jit(solution)/shard_map/ppermute | solution.py:29

commit v5 on v4

--- a/solution.py
+++ b/solution.py
@@ -86,7 +86,7 @@
             pltpu.SemaphoreType.DMA((SLOTS,)),
         ],
         compiler_params=params(44),
-        cost_estimate=cost(0, 2**20),
+        cost_estimate=cost(10**10, 2**20),
         name="prepare",
     )(weight, slab)
 
@@ -191,6 +191,7 @@
     weight_of = jnp.dot(one_hot_table, degree_weight, precision=lax.Precision.HIGHEST)[None, :]
     next_other, next_mine, weight_of = lax.optimization_barrier((own_other, own_mine, weight_of))
     left_other, right_mine = shift(next_other, "x", 1), shift(next_mine, "x", -1)
+    weight_of, pair = lax.optimization_barrier((weight_of, pair))
     weighted_slab, slab_norm = prepare(weight_of, slab)
 
     far_other, far_mine = shift(right_other, "x", -1), shift(left_mine, "x", 1)

time: 87.4 us -> 86.8 us (level)
  transfers between devices with their start and end apart: 23 -> 23, of which waited for: 6 -> 7; matrix products, arithmetic and copies ran while one was open for 9% -> 9% of each run, Pallas kernels for 15% -> 16%
where the time goes in v5:
time: 86.8 us; the launch traced here: 85.6 us
  starting transfers between devices  39.7 us (46%)
  waiting for transfers between devices  20.3 us (23%)
  Pallas kernels  14 us (16%)
  matrix products  6.83 us (8%)
  other arithmetic  2.28 us (3%)
  local copies, waits for them, and re-layouts  1.41 us (2%)
  between operations  1 us (1%)
    ppermute x23, starting transfers between devices, shift(): lax.ppermute(value, axis, [(i, (i + by) % size) for i in range(size)])  39.7 us
    ppermute x23, waiting for transfers between devices, shift(): lax.ppermute(value, axis, [(i, (i + by) % size) for i in range(size)])  20.3 us
    pallas_call x1, Pallas kernels, early_partial(): pl.pallas_call(functools.partial(early_kernel, offsets), in_specs=[SMEM]...  7.56 us
    dot_general x2, matrix products, partial(): lax.dot_general(rows, weighted_slab, (((1,), (1,)), ((), ())), preferred_...  5.79 us
    pallas_call x1, Pallas kernels, prepare(): pl.pallas_call(prepare_kernel, in_specs=[VMEM, pl.BlockSpec(memory_space=...  4.89 us
  transfers between devices with their start and end apart: 23, of which 7 were waited for; matrix products, arithmetic and copies ran while one was open for 9% of the time, Pallas kernels for 16%

profile of v5, /device:TPU:32, one launch (start us, length us, event | category | flops | bytes accessed | tf_op | source)
XLA Modules:
  0.0 85.6 jit_solution(10938169518021112008)
XLA Ops:
  0.0 1.1 %constant_dynamic-slice_fusion = (bf16[2,1,32,2048]{3,2,1,0:T(8,128)(2,1)S(1)}, bf16[2,1,32,2048]{3,2,1,0:T(8,128)(2,1)S(1)}) fusion(bf16[2,2,32,2048]{3,2,1,0:T(8,128)(2,1)} %bitcast.161, s32[]{:T(128)S(6)} %select_n.8, s32[]{:T(128)S(6)} %select_n.7), kind=kLoop, calls=%fused_computation.85 | loop fusion | bytes 1048584 | tf_op jit(solution)/shard_map/jit(dynamic_index_in_dim)/dynamic_slice | solution.py:183
  1.1 1.6 %collective-permute-start.2 = (bf16[64,2048]{1,0:T(8,128)(2,1)S(1)}, bf16[64,2048]{1,0:T(8,128)(2,1)S(1)}, u32[]{:S(2)}, u32[]{:S(2)}) collective-permute-start(bf16[64,2048]{1,0:T(8,128)(2,1)S(1)} %bitcast.150), channel_id=1, source_target_pairs={{0,64},{64,128},{128,192},{192,0},{1,65},{65,129},{129,193},{193,1... | collective-permute-start | bytes 786440 | tf_op jit(solution)/shard_map/ppermute | solution.py:29
  2.7 1.7 %collective-permute-start = (bf16[64,2048]{1,0:T(8,128)(2,1)S(1)}, bf16[64,2048]{1,0:T(8,128)(2,1)S(1)}, u32[]{:S(2)}, u32[]{:S(2)}) collective-permute-start(bf16[64,2048]{1,0:T(8,128)(2,1)S(1)} %bitcast.154), channel_id=1, source_target_pairs={{0,192},{64,0},{128,64},{192,128},{1,193},{65,1},{129,65},{193,129... | collective-permute-start | bytes 786440 | tf_op jit(solution)/shard_map/ppermute | solution.py:29
  4.5 3.3 %collective-permute-start.5 = (bf16[128,2048]{1,0:T(8,128)(2,1)S(1)}, bf16[128,2048]{1,0:T(8,128)(2,1)S(1)}, u32[]{:S(2)}, u32[]{:S(2)}) collective-permute-start(bf16[128,2048]{1,0:T(8,128)(2,1)S(1)} %pad_maximum_fusion.3), channel_id=1, source_target_pairs={{0,32},{32,0},{1,33},{33,1},{2,34},{34,2},{3,35},{35,3},{4,36},{36... | collective-permute-start | bytes 1572872 | tf_op jit(solution)/shard_map/ppermute | solution.py:29
  7.7 2.7 %collective-permute-done.2.refs_7_ = bf16[64,2048]{1,0:T(8,128)(2,1)S(1)} collective-permute-done((bf16[64,2048]{1,0:T(8,128)(2,1)S(1)}, bf16[64,2048]{1,0:T(8,128)(2,1)S(1)}, u32[]{:S(2)}, u32[]{:S(2)}) %collective-permute-start.2) | collective-permute-done | bytes 262176 | tf_op jit(solution)/shard_map/ppermute | solution.py:29
  10.4 0.3 collective-permute-start.3
  10.7 0.0 collective-permute-done.refs_3_
  10.7 3.0 %collective-permute-start.1 = (bf16[64,2048]{1,0:T(8,128)(2,1)S(1)}, bf16[64,2048]{1,0:T(8,128)(2,1)S(1)}, u32[]{:S(2)}, u32[]{:S(2)}) collective-permute-start(bf16[64,2048]{1,0:T(8,128)(2,1)S(1)} %collective-permute-done.refs_3_), channel_id=1, source_target_pairs={{0,192},{64,0},{128,64},{192,128},{1,193},{65,1},{129,65},{193,129... | collective-permute-start | bytes 786440 | tf_op jit(solution)/shard_map/ppermute | solution.py:29
  13.7 1.0 %fusion.2.weight = f32[1,2048]{1,0:T(1,128)S(1)} fusion(f32[256,1]{0,1:T(1,128)S(1)} %bitcast.143, s32[2048]{0:T(1024)S(1)} %copy-done.1), kind=kOutput, calls=%fused_computation.5 | convolution fusion | flops 6815744 | bytes 17408 | tf_op jit(solution)/shard_map/dot_general | solution.py:191
  14.7 0.0 collective-permute-start.8
  14.8 3.2 %collective-permute-start.9 = (bf16[64,2048]{1,0:T(8,128)(2,1)S(1)}, bf16[64,2048]{1,0:T(8,128)(2,1)S(1)}, u32[]{:S(2)}, u32[]{:S(2)}) collective-permute-start(bf16[64,2048]{1,0:T(8,128)(2,1)S(1)} %bitcast.152), channel_id=1, source_target_pairs={{0,192},{64,0},{128,64},{192,128},{1,193},{65,1},{129,65},{193,129... | collective-permute-start | bytes 786440 | tf_op jit(solution)/shard_map/ppermute | solution.py:29
  18.0 0.1 pad_add_fusion.place
  18.1 1.1 %collective-permute-done.5 = bf16[128,2048]{1,0:T(8,128)(2,1)S(1)} collective-permute-done((bf16[128,2048]{1,0:T(8,128)(2,1)S(1)}, bf16[128,2048]{1,0:T(8,128)(2,1)S(1)}, u32[]{:S(2)}, u32[]{:S(2)}) %collective-permute-start.5) | collective-permute-done | bytes 524320 | tf_op jit(solution)/shard_map/ppermute | solution.py:29
  19.1 0.3 collective-permute-start.6
  19.4 1.2 %collective-permute-done.3.refs_9_ = bf16[64,2048]{1,0:T(8,128)(2,1)S(1)} collective-permute-done((bf16[64,2048]{1,0:T(8,128)(2,1)S(1)}, bf16[64,2048]{1,0:T(8,128)(2,1)S(1)}, u32[]{:S(2)}, u32[]{:S(2)}) %collective-permute-start.3) | collective-permute-done | bytes 262176 | tf_op jit(solution)/shard_map/ppermute | solution.py:29
  20.6 1.8 %collective-permute-start.7 = (bf16[128,2048]{1,0:T(8,128)(2,1)S(1)}, bf16[128,2048]{1,0:T(8,128)(2,1)S(1)}, u32[]{:S(2)}, u32[]{:S(2)}) collective-permute-start(bf16[128,2048]{1,0:T(8,128)(2,1)S(1)} %collective-permute-done.5), channel_id=1, source_target_pairs={{0,192},{64,0},{128,64},{192,128},{1,193},{65,1},{129,65},{193,129... | collective-permute-start | bytes 1572872 | tf_op jit(solution)/shard_map/ppermute | solution.py:29
  22.4 0.0 collective-permute-done.1.refs_4_
  22.4 3.3 %collective-permute-start.4 = (bf16[128,2048]{1,0:T(8,128)(2,1)S(1)}, bf16[128,2048]{1,0:T(8,128)(2,1)S(1)}, u32[]{:S(2)}, u32[]{:S(2)}) collective-permute-start(bf16[128,2048]{1,0:T(8,128)(2,1)S(1)} %pad_maximum_fusion.2), channel_id=1, source_target_pairs={{0,32},{32,0},{1,33},{33,1},{2,34},{34,2},{3,35},{35,3},{4,36},{36... | collective-permute-start | bytes 1572872 | tf_op jit(solution)/shard_map/ppermute | solution.py:29
  25.7 4.9 %prepare.1 = (bf16[2048,2048]{1,0:T(8,128)(2,1)S(1)}, f32[1,2048]{1,0:T(1,128)S(1)}) custom-call(f32[1,2048]{1,0:T(1,128)S(1)} %fusion.2.weight, bf16[2048,2048]{1,0:T(8,128)(2,1)} %slab.1), custom_call_target="tpu_custom_call" | custom-call | flops 10000000000 | bytes 1048576 | tf_op jit(solution)/shard_map/prepare/pallas_call | solution.py:76
  30.7 0.0 collective-permute-done.8.refs_2_
  30.7 0.0 collective-permute-done.9.refs_8_
  30.7 7.6 %early_partial.1 = (f32[320,2048]{1,0:T(8,128)S(1)}, f32[512,2048]{1,0:T(8,128)S(1)}) custom-call(s32[4]{0:T(128)S(1)} %pad_add_fusion.place, f32[1,2048]{1,0:T(1,128)S(1)} %fusion.2.weight, f32[1,2048]{1,0:T(1,128)S(1)} %get-tuple-element.29.slab_norm, bf16[2048,2048]{1,0:T(8,128)(2,1)S(1)} %get-tuple-element.30.slab, bf16[64,2048]{1,0:T(8,128)(2,1)S(1)} %bitcast.157, ...), custom_call_target="tpu_custom_call" | custom-call | flops 30000001024 | bytes 65536 | tf_op jit(solution)/shard_map/early_partial/pallas_call | solution.py:133
  38.2 0.3 collective-permute-start.11
  38.5 0.0 collective-permute-done.4
  38.5 0.0 collective-permute-done.6
  38.6 0.0 collective-permute-done.7
  38.6 0.1 fusion.45
  38.7 0.5 multiply_reduce_fusion
  39.2 2.9 %fusion = f32[192,2048]{1,0:T(8,128)S(1)} fusion(bf16[2048,2048]{1,0:T(8,128)(2,1)S(1)} %get-tuple-element.30.slab, f32[2048]{0:T(1024)S(1)} %bitcast.159, f32[192]{0:T(256)S(1)} %get-tuple-element.48, bf16[64,2048]{1,0:T(8,128)(2,1)S(1)} %get-tuple-element.68, bf16[64,2048]{1,0:T(8,128)(2,1)S(1)} %get-tuple-element.80, ...), kind=kOutput, calls=%fused_computation.2 | convolution fusion | flops 1614151680 | bytes 10756864 | tf_op jit(solution)/shard_map/dot_general | solution.py:220
  42.1 0.6 collective-permute-start.10
  42.6 2.9 %fusion.1.refs_1_ = f32[192,2048]{1,0:T(8,128)S(1)} fusion(bf16[2048,2048]{1,0:T(8,128)(2,1)S(1)} %get-tuple-element.30.slab, f32[192]{0:T(256)S(1)} %get-tuple-element.47, f32[2048]{0:T(1024)S(1)} %bitcast.160, bf16[64,2048]{1,0:T(8,128)(2,1)S(1)} %get-tuple-element.69, bf16[64,2048]{1,0:T(8,128)(2,1)S(1)} %get-tuple-element.79, ...), kind=kOutput, calls=%fused_computation.3 | convolution fusion | flops 1614151680 | bytes 10756864 | tf_op jit(solution)/shard_map/dot_general | solution.py:220
  45.5 0.0 collective-permute-done.11.refs_0_
  45.6 0.9 %add_into.2.refs_2_ = f32[512,2048]{1,0:T(8,128)S(1)} custom-call(s32[4]{0:T(128)S(1)} %pad_add_fusion.place, f32[320,2048]{1,0:T(8,128)S(1)} %collective-permute-done.11.refs_0_, f32[512,2048]{1,0:T(8,128)S(1)} %get-tuple-element.37.refs_1_), custom_call_target="tpu_custom_call", output_to_operand_aliasing={{}: (2, {})} | custom-call | bytes 65536 | tf_op jit(solution)/shard_map/add_into/pallas_call | solution.py:165
  46.4 0.0 collective-permute-done.10.refs_0_
  46.5 0.7 add_into.3
  47.2 0.1 fusion.5
  47.3 0.1 slice_bitcast_fusion.3
  47.4 0.8 collective-permute-start.12
  48.3 2.0 %collective-permute-start.13 = (f16[2,2,32,1024]{3,2,1,0:T(8,128)(2,1)S(1)}, f16[2,2,32,1024]{3,2,1,0:T(8,128)(2,1)S(1)}, u32[]{:S(2)}, u32[]{:S(2)}) collective-permute-start(f16[2,2,32,1024]{3,2,1,0:T(8,128)(2,1)S(1)} %fusion.6), channel_id=1, source_target_pairs={{0,2},{2,4},{4,6},{6,8},{8,10},{10,12},{12,14},{14,0},{1,3},{3,5},... | collective-permute-start | bytes 786440 | tf_op jit(solution)/shard_map/ppermute | solution.py:29
  50.3 0.2 collective-permute-start.14
  50.5 4.5 %collective-permute-start.15 = (f16[2,16,1024]{2,1,0:T(8,128)(2,1)S(1)}, f16[2,16,1024]{2,1,0:T(8,128)(2,1)S(1)}, u32[]{:S(2)}, u32[]{:S(2)}) collective-permute-start(f16[2,16,1024]{2,1,0:T(8,128)(2,1)S(1)} %get-tuple-element.75), channel_id=1, source_target_pairs={{0,4},{2,6},{4,8},{6,10},{8,12},{10,14},{12,0},{14,2},{1,5},{3,7},... | collective-permute-start | bytes 196616 | tf_op jit(solution)/shard_map/ppermute | solution.py:29
  55.0 1.1 %collective-permute-start.16 = (f16[2,16,1024]{2,1,0:T(8,128)(2,1)S(1)}, f16[2,16,1024]{2,1,0:T(8,128)(2,1)S(1)}, u32[]{:S(2)}, u32[]{:S(2)}) collective-permute-start(f16[2,16,1024]{2,1,0:T(8,128)(2,1)S(1)} %get-tuple-element.74), channel_id=1, source_target_pairs={{0,12},{2,14},{4,0},{6,2},{8,4},{10,6},{12,8},{14,10},{1,13},{3,15... | collective-permute-start | bytes 196616 | tf_op jit(solution)/shard_map/ppermute | solution.py:29
  56.1 6.0 %collective-permute-done.15 = f16[2,16,1024]{2,1,0:T(8,128)(2,1)S(1)} collective-permute-done((f16[2,16,1024]{2,1,0:T(8,128)(2,1)S(1)}, f16[2,16,1024]{2,1,0:T(8,128)(2,1)S(1)}, u32[]{:S(2)}, u32[]{:S(2)}) %collective-permute-start.15) | collective-permute-done | bytes 65568 | tf_op jit(solution)/shard_map/ppermute | solution.py:29
  62.1 0.2 collective-permute-done.16
  62.3 0.0 collective-permute-done.13
  62.3 0.0 collective-permute-done.14
  62.3 0.0 collective-permute-done.12
  62.3 0.2 fusion.12
  62.6 1.4 %collective-permute-start.17 = (f16[3,32,1024]{2,1,0:T(8,128)(2,1)S(1)}, f16[3,32,1024]{2,1,0:T(8,128)(2,1)S(1)}, u32[]{:S(2)}, u32[]{:S(2)}) collective-permute-start(f16[3,32,1024]{2,1,0:T(8,128)(2,1)S(1)} %fusion.8), channel_id=1, source_target_pairs={{0,16},{16,0},{1,17},{17,1},{2,18},{18,2},{3,19},{19,3},{4,20},{20... | collective-permute-start | bytes 589832 | tf_op jit(solution)/shard_map/ppermute | solution.py:29
  64.0 0.1 fusion.35
  64.2 4.4 %collective-permute-start.18 = (f16[2,32,1024]{2,1,0:T(8,128)(2,1)S(1)}, f16[2,32,1024]{2,1,0:T(8,128)(2,1)S(1)}, u32[]{:S(2)}, u32[]{:S(2)}) collective-permute-start(f16[2,32,1024]{2,1,0:T(8,128)(2,1)S(1)} %fusion.15), channel_id=1, source_target_pairs={{0,2},{2,4},{4,6},{6,8},{8,10},{10,12},{12,14},{14,0},{1,3},{3,5},... | collective-permute-start | bytes 393224 | tf_op jit(solution)/shard_map/ppermute | solution.py:29
  68.6 0.3 collective-permute-start.19
  68.9 1.5 %collective-permute-start.20 = (f16[32,1024]{1,0:T(8,128)(2,1)S(1)}, f16[32,1024]{1,0:T(8,128)(2,1)S(1)}, u32[]{:S(2)}, u32[]{:S(2)}) collective-permute-start(f16[32,1024]{1,0:T(8,128)(2,1)S(1)} %fusion.33), channel_id=1, source_target_pairs={{0,4},{2,6},{4,8},{6,10},{8,12},{10,14},{12,0},{14,2},{1,5},{3,7},... | collective-permute-start | bytes 196616 | tf_op jit(solution)/shard_map/ppermute | solution.py:29
  70.5 5.7 %collective-permute-done.20 = f16[32,1024]{1,0:T(8,128)(2,1)S(1)} collective-permute-done((f16[32,1024]{1,0:T(8,128)(2,1)S(1)}, f16[32,1024]{1,0:T(8,128)(2,1)S(1)}, u32[]{:S(2)}, u32[]{:S(2)}) %collective-permute-start.20) | collective-permute-done | bytes 65568 | tf_op jit(solution)/shard_map/ppermute | solution.py:29
  76.2 0.0 collective-permute-done.18
  76.2 0.0 collective-permute-done.19
  76.2 0.0 collective-permute-done.17
  76.2 0.1 fusion.27
  76.2 0.1 fusion.29
  76.4 0.1 collective-permute-start.22
  76.5 4.2 %collective-permute-start.21 = (f16[32,2048]{1,0:T(8,128)(2,1)S(1)}, f16[32,2048]{1,0:T(8,128)(2,1)S(1)}, u32[]{:S(2)}, u32[]{:S(2)}) collective-permute-start(f16[32,2048]{1,0:T(8,128)(2,1)S(1)} %fusion.21), channel_id=1, source_target_pairs={{0,12},{2,14},{4,0},{6,2},{8,4},{10,6},{12,8},{14,10},{1,13},{3,15... | collective-permute-start | bytes 393224 | tf_op jit(solution)/shard_map/ppermute | solution.py:29
  81.4 3.4 %collective-permute-done.22 = f16[32,2048]{1,0:T(8,128)(2,1)S(1)} collective-permute-done((f16[32,2048]{1,0:T(8,128)(2,1)S(1)}, f16[32,2048]{1,0:T(8,128)(2,1)S(1)}, u32[]{:S(2)}, u32[]{:S(2)}) %collective-permute-start.22) | collective-permute-done | bytes 131104 | tf_op jit(solution)/shard_map/ppermute | solution.py:29
  84.8 0.0 collective-permute-done.21
  84.8 0.8 fusion.20
  (22 shorter events, 0.5 us)
Async XLA Ops:
  0.0 13.7 %copy-start = (f32[256]{0:T(256)S(1)}, f32[256]{0:T(256)}, u32[]{:S(2)}) copy-start(f32[256]{0:T(256)} %param.8) | copy-start | bytes 3076
  0.0 13.7 %copy-start.1 = (s32[2048]{0:T(1024)S(1)}, s32[2048]{0:T(1024)}, u32[]{:S(2)}) copy-start(s32[2048]{0:T(1024)} %param.7) | copy-start | bytes 24580
  1.1 9.3 %collective-permute-start.2 = (bf16[64,2048]{1,0:T(8,128)(2,1)S(1)}, bf16[64,2048]{1,0:T(8,128)(2,1)S(1)}, u32[]{:S(2)}, u32[]{:S(2)}) collective-permute-start(bf16[64,2048]{1,0:T(8,128)(2,1)S(1)} %bitcast.150), channel_id=1, source_target_pairs={{0,64},{64,128},{128,192},{192,0},{1,65},{65,129},{129,193},{193,1... | collective-permute-start | bytes 786440 | tf_op jit(solution)/shard_map/ppermute | solution.py:29
  2.7 8.0 %collective-permute-start = (bf16[64,2048]{1,0:T(8,128)(2,1)S(1)}, bf16[64,2048]{1,0:T(8,128)(2,1)S(1)}, u32[]{:S(2)}, u32[]{:S(2)}) collective-permute-start(bf16[64,2048]{1,0:T(8,128)(2,1)S(1)} %bitcast.154), channel_id=1, source_target_pairs={{0,192},{64,0},{128,64},{192,128},{1,193},{65,1},{129,65},{193,129... | collective-permute-start | bytes 786440 | tf_op jit(solution)/shard_map/ppermute | solution.py:29
  4.5 14.7 %collective-permute-start.5 = (bf16[128,2048]{1,0:T(8,128)(2,1)S(1)}, bf16[128,2048]{1,0:T(8,128)(2,1)S(1)}, u32[]{:S(2)}, u32[]{:S(2)}) collective-permute-start(bf16[128,2048]{1,0:T(8,128)(2,1)S(1)} %pad_maximum_fusion.3), channel_id=1, source_target_pairs={{0,32},{32,0},{1,33},{33,1},{2,34},{34,2},{3,35},{35,3},{4,36},{36... | collective-permute-start | bytes 1572872 | tf_op jit(solution)/shard_map/ppermute | solution.py:29
  10.4 10.2 %collective-permute-start.3 = (bf16[64,2048]{1,0:T(8,128)(2,1)S(1)}, bf16[64,2048]{1,0:T(8,128)(2,1)S(1)}, u32[]{:S(2)}, u32[]{:S(2)}) collective-permute-start(bf16[64,2048]{1,0:T(8,128)(2,1)S(1)} %collective-permute-done.2.refs_7_), channel_id=1, source_target_pairs={{0,64},{64,128},{128,192},{192,0},{1,65},{65,129},{129,193},{193,1... | collective-permute-start | bytes 786440 | tf_op jit(solution)/shard_map/ppermute | solution.py:29
  10.7 11.7 %collective-permute-start.1 = (bf16[64,2048]{1,0:T(8,128)(2,1)S(1)}, bf16[64,2048]{1,0:T(8,128)(2,1)S(1)}, u32[]{:S(2)}, u32[]{:S(2)}) collective-permute-start(bf16[64,2048]{1,0:T(8,128)(2,1)S(1)} %collective-permute-done.refs_3_), channel_id=1, source_target_pairs={{0,192},{64,0},{128,64},{192,128},{1,193},{65,1},{129,65},{193,129... | collective-permute-start | bytes 786440 | tf_op jit(solution)/shard_map/ppermute | solution.py:29
  14.7 15.9 %collective-permute-start.8 = (bf16[64,2048]{1,0:T(8,128)(2,1)S(1)}, bf16[64,2048]{1,0:T(8,128)(2,1)S(1)}, u32[]{:S(2)}, u32[]{:S(2)}) collective-permute-start(bf16[64,2048]{1,0:T(8,128)(2,1)S(1)} %bitcast.156), channel_id=1, source_target_pairs={{0,64},{64,128},{128,192},{192,0},{1,65},{65,129},{129,193},{193,1... | collective-permute-start | bytes 786440 | tf_op jit(solution)/shard_map/ppermute | solution.py:29
  14.8 15.9 %collective-permute-start.9 = (bf16[64,2048]{1,0:T(8,128)(2,1)S(1)}, bf16[64,2048]{1,0:T(8,128)(2,1)S(1)}, u32[]{:S(2)}, u32[]{:S(2)}) collective-permute-start(bf16[64,2048]{1,0:T(8,128)(2,1)S(1)} %bitcast.152), channel_id=1, source_target_pairs={{0,192},{64,0},{128,64},{192,128},{1,193},{65,1},{129,65},{193,129... | collective-permute-start | bytes 786440 | tf_op jit(solution)/shard_map/ppermute | solution.py:29
  19.1 19.4 %collective-permute-start.6 = (bf16[128,2048]{1,0:T(8,128)(2,1)S(1)}, bf16[128,2048]{1,0:T(8,128)(2,1)S(1)}, u32[]{:S(2)}, u32[]{:S(2)}) collective-permute-start(bf16[128,2048]{1,0:T(8,128)(2,1)S(1)} %collective-permute-done.5), channel_id=1, source_target_pairs={{0,64},{64,128},{128,192},{192,0},{1,65},{65,129},{129,193},{193,1... | collective-permute-start | bytes 1572872 | tf_op jit(solution)/shard_map/ppermute | solution.py:29
  20.6 18.0 %collective-permute-start.7 = (bf16[128,2048]{1,0:T(8,128)(2,1)S(1)}, bf16[128,2048]{1,0:T(8,128)(2,1)S(1)}, u32[]{:S(2)}, u32[]{:S(2)}) collective-permute-start(bf16[128,2048]{1,0:T(8,128)(2,1)S(1)} %collective-permute-done.5), channel_id=1, source_target_pairs={{0,192},{64,0},{128,64},{192,128},{1,193},{65,1},{129,65},{193,129... | collective-permute-start | bytes 1572872 | tf_op jit(solution)/shard_map/ppermute | solution.py:29
  22.4 16.1 %collective-permute-start.4 = (bf16[128,2048]{1,0:T(8,128)(2,1)S(1)}, bf16[128,2048]{1,0:T(8,128)(2,1)S(1)}, u32[]{:S(2)}, u32[]{:S(2)}) collective-permute-start(bf16[128,2048]{1,0:T(8,128)(2,1)S(1)} %pad_maximum_fusion.2), channel_id=1, source_target_pairs={{0,32},{32,0},{1,33},{33,1},{2,34},{34,2},{3,35},{35,3},{4,36},{36... | collective-permute-start | bytes 1572872 | tf_op jit(solution)/shard_map/ppermute | solution.py:29
  38.2 7.3 %collective-permute-start.11 = (f32[320,2048]{1,0:T(8,128)S(1)}, f32[320,2048]{1,0:T(8,128)S(1)}, u32[]{:S(2)}, u32[]{:S(2)}) collective-permute-start(f32[320,2048]{1,0:T(8,128)S(1)} %get-tuple-element.33), channel_id=1, source_target_pairs={{0,1},{1,0},{2,3},{3,2},{4,5},{5,4},{6,7},{7,6},{8,9},{9,8},{10,11... | collective-permute-start | bytes 7864328 | tf_op jit(solution)/shard_map/ppermute | solution.py:29
  42.1 4.4 %collective-permute-start.10 = (f32[192,2048]{1,0:T(8,128)S(1)}, f32[192,2048]{1,0:T(8,128)S(1)}, u32[]{:S(2)}, u32[]{:S(2)}) collective-permute-start(f32[192,2048]{1,0:T(8,128)S(1)} %fusion), channel_id=1, source_target_pairs={{0,1},{1,0},{2,3},{3,2},{4,5},{5,4},{6,7},{7,6},{8,9},{9,8},{10,11... | collective-permute-start | bytes 4718600 | tf_op jit(solution)/shard_map/ppermute | solution.py:29
  47.4 14.9 %collective-permute-start.12 = (f16[8,32,1024]{2,1,0:T(8,128)(2,1)S(1)}, f16[8,32,1024]{2,1,0:T(8,128)(2,1)S(1)}, u32[]{:S(2)}, u32[]{:S(2)}) collective-permute-start(f16[8,32,1024]{2,1,0:T(8,128)(2,1)S(1)} %fusion.5), channel_id=1, source_target_pairs={{0,16},{16,0},{1,17},{17,1},{2,18},{18,2},{3,19},{19,3},{4,20},{20... | collective-permute-start | bytes 1572872 | tf_op jit(solution)/shard_map/ppermute | solution.py:29
  48.3 14.0 %collective-permute-start.13 = (f16[2,2,32,1024]{3,2,1,0:T(8,128)(2,1)S(1)}, f16[2,2,32,1024]{3,2,1,0:T(8,128)(2,1)S(1)}, u32[]{:S(2)}, u32[]{:S(2)}) collective-permute-start(f16[2,2,32,1024]{3,2,1,0:T(8,128)(2,1)S(1)} %fusion.6), channel_id=1, source_target_pairs={{0,2},{2,4},{4,6},{6,8},{8,10},{10,12},{12,14},{14,0},{1,3},{3,5},... | collective-permute-start | bytes 786440 | tf_op jit(solution)/shard_map/ppermute | solution.py:29
  50.3 12.0 %collective-permute-start.14 = (f16[2,2,32,1024]{3,2,1,0:T(8,128)(2,1)S(1)}, f16[2,2,32,1024]{3,2,1,0:T(8,128)(2,1)S(1)}, u32[]{:S(2)}, u32[]{:S(2)}) collective-permute-start(f16[2,2,32,1024]{3,2,1,0:T(8,128)(2,1)S(1)} %fusion.7), channel_id=1, source_target_pairs={{0,14},{2,0},{4,2},{6,4},{8,6},{10,8},{12,10},{14,12},{1,15},{3,1}... | collective-permute-start | bytes 786440 | tf_op jit(solution)/shard_map/ppermute | solution.py:29
  50.5 11.5 %collective-permute-start.15 = (f16[2,16,1024]{2,1,0:T(8,128)(2,1)S(1)}, f16[2,16,1024]{2,1,0:T(8,128)(2,1)S(1)}, u32[]{:S(2)}, u32[]{:S(2)}) collective-permute-start(f16[2,16,1024]{2,1,0:T(8,128)(2,1)S(1)} %get-tuple-element.75), channel_id=1, source_target_pairs={{0,4},{2,6},{4,8},{6,10},{8,12},{10,14},{12,0},{14,2},{1,5},{3,7},... | collective-permute-start | bytes 196616 | tf_op jit(solution)/shard_map/ppermute | solution.py:29
  55.0 7.3 %collective-permute-start.16 = (f16[2,16,1024]{2,1,0:T(8,128)(2,1)S(1)}, f16[2,16,1024]{2,1,0:T(8,128)(2,1)S(1)}, u32[]{:S(2)}, u32[]{:S(2)}) collective-permute-start(f16[2,16,1024]{2,1,0:T(8,128)(2,1)S(1)} %get-tuple-element.74), channel_id=1, source_target_pairs={{0,12},{2,14},{4,0},{6,2},{8,4},{10,6},{12,8},{14,10},{1,13},{3,15... | collective-permute-start | bytes 196616 | tf_op jit(solution)/shard_map/ppermute | solution.py:29
  62.6 13.6 %collective-permute-start.17 = (f16[3,32,1024]{2,1,0:T(8,128)(2,1)S(1)}, f16[3,32,1024]{2,1,0:T(8,128)(2,1)S(1)}, u32[]{:S(2)}, u32[]{:S(2)}) collective-permute-start(f16[3,32,1024]{2,1,0:T(8,128)(2,1)S(1)} %fusion.8), channel_id=1, source_target_pairs={{0,16},{16,0},{1,17},{17,1},{2,18},{18,2},{3,19},{19,3},{4,20},{20... | collective-permute-start | bytes 589832 | tf_op jit(solution)/shard_map/ppermute | solution.py:29
  64.2 12.0 %collective-permute-start.18 = (f16[2,32,1024]{2,1,0:T(8,128)(2,1)S(1)}, f16[2,32,1024]{2,1,0:T(8,128)(2,1)S(1)}, u32[]{:S(2)}, u32[]{:S(2)}) collective-permute-start(f16[2,32,1024]{2,1,0:T(8,128)(2,1)S(1)} %fusion.15), channel_id=1, source_target_pairs={{0,2},{2,4},{4,6},{6,8},{8,10},{10,12},{12,14},{14,0},{1,3},{3,5},... | collective-permute-start | bytes 393224 | tf_op jit(solution)/shard_map/ppermute | solution.py:29
  68.6 7.6 %collective-permute-start.19 = (f16[2,32,1024]{2,1,0:T(8,128)(2,1)S(1)}, f16[2,32,1024]{2,1,0:T(8,128)(2,1)S(1)}, u32[]{:S(2)}, u32[]{:S(2)}) collective-permute-start(f16[2,32,1024]{2,1,0:T(8,128)(2,1)S(1)} %fusion.16), channel_id=1, source_target_pairs={{0,14},{2,0},{4,2},{6,4},{8,6},{10,8},{12,10},{14,12},{1,15},{3,1}... | collective-permute-start | bytes 393224 | tf_op jit(solution)/shard_map/ppermute | solution.py:29
  68.9 7.2 %collective-permute-start.20 = (f16[32,1024]{1,0:T(8,128)(2,1)S(1)}, f16[32,1024]{1,0:T(8,128)(2,1)S(1)}, u32[]{:S(2)}, u32[]{:S(2)}) collective-permute-start(f16[32,1024]{1,0:T(8,128)(2,1)S(1)} %fusion.33), channel_id=1, source_target_pairs={{0,4},{2,6},{4,8},{6,10},{8,12},{10,14},{12,0},{14,2},{1,5},{3,7},... | collective-permute-start | bytes 196616 | tf_op jit(solution)/shard_map/ppermute | solution.py:29
  76.4 8.4 %collective-permute-start.22 = (f16[32,2048]{1,0:T(8,128)(2,1)S(1)}, f16[32,2048]{1,0:T(8,128)(2,1)S(1)}, u32[]{:S(2)}, u32[]{:S(2)}) collective-permute-start(f16[32,2048]{1,0:T(8,128)(2,1)S(1)} %fusion.22), channel_id=1, source_target_pairs={{0,4},{2,6},{4,8},{6,10},{8,12},{10,14},{12,0},{14,2},{1,5},{3,7},... | collective-permute-start | bytes 393224 | tf_op jit(solution)/shard_map/ppermute | solution.py:29
  76.5 8.3 %collective-permute-start.21 = (f16[32,2048]{1,0:T(8,128)(2,1)S(1)}, f16[32,2048]{1,0:T(8,128)(2,1)S(1)}, u32[]{:S(2)}, u32[]{:S(2)}) collective-permute-start(f16[32,2048]{1,0:T(8,128)(2,1)S(1)} %fusion.21), channel_id=1, source_target_pairs={{0,12},{2,14},{4,0},{6,2},{8,4},{10,6},{12,8},{14,10},{1,13},{3,15... | collective-permute-start | bytes 393224 | tf_op jit(solution)/shard_map/ppermute | solution.py:29

commit v6 on v5

--- a/solution.py
+++ b/solution.py
@@ -148,30 +148,31 @@
     )(*arguments)
 
 
-def add_kernel(offsets, count, place, *refs):
-    parts, more, (held, out) = refs[:count], refs[count:-2], refs[-2:]
-    for i, offset in enumerate(offsets):
-        for low in range(2):
-            start = (i * 2 + low) * GROUP
-            at = pl.ds(row_offset(place, offset, low), GROUP)
-            total = more[0][start : start + GROUP, :] if more else held[at, :]
-            part, start = (parts[0], start) if count == 1 else (parts[i], low * GROUP)
-            out[at, :] = total + part[start : start + GROUP, :]
-
-
-def add_into(offsets, place, parts, mine, held, estimate):
-    more = [] if mine is None else [mine]
-    count = len(parts) + len(more)
+def add_kernel(groups, place, *refs):
+    refs, (held, out) = list(refs[:-2]), refs[-2:]
+    for offsets, has_mine in groups:
+        received = refs.pop(0)
+        mine = refs.pop(0) if has_mine else None
+        for i, offset in enumerate(offsets):
+            for low in range(2):
+                start = (i * 2 + low) * GROUP
+                at = pl.ds(row_offset(place, offset, low), GROUP)
+                total = held[at, :] if mine is None else mine[start : start + GROUP, :]
+                out[at, :] = total + received[start : start + GROUP, :]
+
+
+def add_into(groups, place, held, estimate):
+    parts = [p for _, received, mine in groups for p in (received, mine) if p is not None]
     return pl.pallas_call(
-        functools.partial(add_kernel, offsets, len(parts)),
-        in_specs=[SMEM] + [VMEM] * (count + 1),
+        functools.partial(add_kernel, [(offsets, mine is not None) for offsets, _, mine in groups]),
+        in_specs=[SMEM] + [VMEM] * (len(parts) + 1),
         out_specs=VMEM,
         out_shape=jax.ShapeDtypeStruct(held.shape, held.dtype),
-        input_output_aliases={count + 1: 0},
-        compiler_params=params(16),
+        input_output_aliases={len(parts) + 1: 0},
+        compiler_params=params(20),
         cost_estimate=estimate,
         name="add_into",
-    )(place, *parts, *more, held)
+    )(place, *parts, held)
 
 
 def body(queries, slab, degree, degree_weight, spread):
@@ -191,6 +192,7 @@
     weight_of = jnp.dot(one_hot_table, degree_weight, precision=lax.Precision.HIGHEST)[None, :]
     next_other, next_mine, weight_of = lax.optimization_barrier((own_other, own_mine, weight_of))
     left_other, right_mine = shift(next_other, "x", 1), shift(next_mine, "x", -1)
+
     weight_of, pair = lax.optimization_barrier((weight_of, pair))
     weighted_slab, slab_norm = prepare(weight_of, slab)
 
@@ -210,8 +212,7 @@
         + [own_mine, pair[KEPT:], left_mine, right_mine, far_mine],
         cost(3 * 10**10, 2**16),
     )
-    pieces = [shift(early_other, "core", 1)]
-    held = add_into(EARLY, place, pieces, None, held, small)
+    early = EARLY, shift(early_other, "core", 1), None
 
     def partial(blocks):
         rows = jnp.concatenate(blocks)
@@ -225,7 +226,7 @@
     late = lax.optimization_barrier((pair_far, pair_left, pair_right, early_other))[:3]
     late_other = shift(partial([b[:KEPT] for b in late]), "core", 1)
     late_mine = partial([b[KEPT:] for b in late])
-    held = add_into(LATE, place, [late_other], late_mine, held, small)
+    held = add_into([early, (LATE, late_other, late_mine)], place, held, small)
 
     held = held.reshape(YL, Z, GROUP, columns)
 

time: 86.8 us -> 87.5 us (level); the launches traced: 85.6 us -> 87.4 us
  waiting for transfers between devices: 20.3 us -> 25.5 us
  starting transfers between devices: 39.7 us -> 36.9 us
    ppermute x23, waiting for transfers between devices: 20.3 us -> 25.5 us  [shift(): lax.ppermute(value, axis, [(i, (i + by) % size) for i in range(size)])]
    ppermute x23, starting transfers between devices: 39.7 us -> 36.9 us  [shift(): lax.ppermute(value, axis, [(i, (i + by) % size) for i in range(size)])]
  transfers between devices with their start and end apart: 23 -> 23, of which waited for: 7 -> 8; matrix products, arithmetic and copies ran while one was open for 9% -> 9% of each run, Pallas kernels for 16% -> 14%
where the time goes in v6:
time: 87.5 us; the launch traced here: 87.4 us
  starting transfers between devices  36.9 us (42%)
  waiting for transfers between devices  25.5 us (29%)
  Pallas kernels  13.5 us (15%)
  matrix products  6.83 us (8%)
  other arithmetic  2.29 us (3%)
  local copies, waits for them, and re-layouts  1.41 us (2%)
  between operations  0.99 us (1%)
    ppermute x23, starting transfers between devices, shift(): lax.ppermute(value, axis, [(i, (i + by) % size) for i in range(size)])  36.9 us
    ppermute x23, waiting for transfers between devices, shift(): lax.ppermute(value, axis, [(i, (i + by) % size) for i in range(size)])  25.5 us
    pallas_call x1, Pallas kernels, early_partial(): pl.pallas_call(functools.partial(early_kernel, offsets), in_specs=[SMEM]...  7.56 us
    dot_general x2, matrix products, partial(): lax.dot_general(rows, weighted_slab, (((1,), (1,)), ((), ())), preferred_...  5.79 us
    pallas_call x1, Pallas kernels, prepare(): pl.pallas_call(prepare_kernel, in_specs=[VMEM, pl.BlockSpec(memory_space=...  4.89 us
  transfers between devices with their start and end apart: 23, of which 8 were waited for; matrix products, arithmetic and copies ran while one was open for 9% of the time, Pallas kernels for 14%

profile of v6, /device:TPU:32, one launch (start us, length us, event | category | flops | bytes accessed | tf_op | source)
XLA Modules:
  0.0 87.4 jit_solution(13839898305953775249)
XLA Ops:
  0.0 0.0 copy-start
  0.0 1.1 %constant_dynamic-slice_fusion = (bf16[2,1,32,2048]{3,2,1,0:T(8,128)(2,1)S(1)}, bf16[2,1,32,2048]{3,2,1,0:T(8,128)(2,1)S(1)}) fusion(bf16[2,2,32,2048]{3,2,1,0:T(8,128)(2,1)} %bitcast.161, s32[]{:T(128)S(6)} %select_n.8, s32[]{:T(128)S(6)} %select_n.7), kind=kLoop, calls=%fused_computation.85 | loop fusion | bytes 1048584 | tf_op jit(solution)/shard_map/jit(dynamic_index_in_dim)/dynamic_slice | solution.py:184
  1.1 2.8 %collective-permute-start.2 = (bf16[64,2048]{1,0:T(8,128)(2,1)S(1)}, bf16[64,2048]{1,0:T(8,128)(2,1)S(1)}, u32[]{:S(2)}, u32[]{:S(2)}) collective-permute-start(bf16[64,2048]{1,0:T(8,128)(2,1)S(1)} %bitcast.154), channel_id=1, source_target_pairs={{0,192},{64,0},{128,64},{192,128},{1,193},{65,1},{129,65},{193,129... | collective-permute-start | bytes 786440 | tf_op jit(solution)/shard_map/ppermute | solution.py:29
  3.9 0.0 collective-permute-start.4
  4.0 3.3 %collective-permute-start = (bf16[128,2048]{1,0:T(8,128)(2,1)S(1)}, bf16[128,2048]{1,0:T(8,128)(2,1)S(1)}, u32[]{:S(2)}, u32[]{:S(2)}) collective-permute-start(bf16[128,2048]{1,0:T(8,128)(2,1)S(1)} %pad_maximum_fusion.2), channel_id=1, source_target_pairs={{0,32},{32,0},{1,33},{33,1},{2,34},{34,2},{3,35},{35,3},{4,36},{36... | collective-permute-start | bytes 1572872 | tf_op jit(solution)/shard_map/ppermute | solution.py:29
  7.3 2.2 %collective-permute-done.2.refs_3_ = bf16[64,2048]{1,0:T(8,128)(2,1)S(1)} collective-permute-done((bf16[64,2048]{1,0:T(8,128)(2,1)S(1)}, bf16[64,2048]{1,0:T(8,128)(2,1)S(1)}, u32[]{:S(2)}, u32[]{:S(2)}) %collective-permute-start.2) | collective-permute-done | bytes 262176 | tf_op jit(solution)/shard_map/ppermute | solution.py:29
  9.5 3.7 %collective-permute-start.3 = (bf16[64,2048]{1,0:T(8,128)(2,1)S(1)}, bf16[64,2048]{1,0:T(8,128)(2,1)S(1)}, u32[]{:S(2)}, u32[]{:S(2)}) collective-permute-start(bf16[64,2048]{1,0:T(8,128)(2,1)S(1)} %collective-permute-done.2.refs_3_), channel_id=1, source_target_pairs={{0,192},{64,0},{128,64},{192,128},{1,193},{65,1},{129,65},{193,129... | collective-permute-start | bytes 786440 | tf_op jit(solution)/shard_map/ppermute | solution.py:29
  13.2 0.0 collective-permute-done.4.refs_7_
  13.2 0.0 collective-permute-start.6
  13.2 1.0 %fusion.2.weight = f32[1,2048]{1,0:T(1,128)S(1)} fusion(f32[256,1]{0,1:T(1,128)S(1)} %bitcast.143, s32[2048]{0:T(1024)S(1)} %copy-done.1), kind=kOutput, calls=%fused_computation.5 | convolution fusion | flops 6815744 | bytes 17408 | tf_op jit(solution)/shard_map/dot_general | solution.py:192
  14.3 0.0 collective-permute-start.1
  14.3 3.3 %collective-permute-start.5 = (bf16[64,2048]{1,0:T(8,128)(2,1)S(1)}, bf16[64,2048]{1,0:T(8,128)(2,1)S(1)}, u32[]{:S(2)}, u32[]{:S(2)}) collective-permute-start(bf16[64,2048]{1,0:T(8,128)(2,1)S(1)} %bitcast.152), channel_id=1, source_target_pairs={{0,192},{64,0},{128,64},{192,128},{1,193},{65,1},{129,65},{193,129... | collective-permute-start | bytes 786440 | tf_op jit(solution)/shard_map/ppermute | solution.py:29
  17.6 0.1 pad_add_fusion.place
  17.7 1.3 %collective-permute-done = bf16[128,2048]{1,0:T(8,128)(2,1)S(1)} collective-permute-done((bf16[128,2048]{1,0:T(8,128)(2,1)S(1)}, bf16[128,2048]{1,0:T(8,128)(2,1)S(1)}, u32[]{:S(2)}, u32[]{:S(2)}) %collective-permute-start) | collective-permute-done | bytes 524320 | tf_op jit(solution)/shard_map/ppermute | solution.py:29
  19.0 3.0 %collective-permute-start.10 = (bf16[128,2048]{1,0:T(8,128)(2,1)S(1)}, bf16[128,2048]{1,0:T(8,128)(2,1)S(1)}, u32[]{:S(2)}, u32[]{:S(2)}) collective-permute-start(bf16[128,2048]{1,0:T(8,128)(2,1)S(1)} %collective-permute-done), channel_id=1, source_target_pairs={{0,192},{64,0},{128,64},{192,128},{1,193},{65,1},{129,65},{193,129... | collective-permute-start | bytes 1572872 | tf_op jit(solution)/shard_map/ppermute | solution.py:29
  21.9 0.0 collective-permute-done.3.refs_4_
  21.9 0.0 collective-permute-start.9
  21.9 1.7 %collective-permute-done.6.refs_9_ = bf16[64,2048]{1,0:T(8,128)(2,1)S(1)} collective-permute-done((bf16[64,2048]{1,0:T(8,128)(2,1)S(1)}, bf16[64,2048]{1,0:T(8,128)(2,1)S(1)}, u32[]{:S(2)}, u32[]{:S(2)}) %collective-permute-start.6) | collective-permute-done | bytes 262176 | tf_op jit(solution)/shard_map/ppermute | solution.py:29
  23.7 3.3 %collective-permute-start.8 = (bf16[128,2048]{1,0:T(8,128)(2,1)S(1)}, bf16[128,2048]{1,0:T(8,128)(2,1)S(1)}, u32[]{:S(2)}, u32[]{:S(2)}) collective-permute-start(bf16[128,2048]{1,0:T(8,128)(2,1)S(1)} %pad_maximum_fusion.3), channel_id=1, source_target_pairs={{0,32},{32,0},{1,33},{33,1},{2,34},{34,2},{3,35},{35,3},{4,36},{36... | collective-permute-start | bytes 1572872 | tf_op jit(solution)/shard_map/ppermute | solution.py:29
  27.0 4.9 %prepare.1 = (bf16[2048,2048]{1,0:T(8,128)(2,1)S(1)}, f32[1,2048]{1,0:T(1,128)S(1)}) custom-call(f32[1,2048]{1,0:T(1,128)S(1)} %fusion.2.weight, bf16[2048,2048]{1,0:T(8,128)(2,1)} %slab.1), custom_call_target="tpu_custom_call" | custom-call | flops 10000000000 | bytes 1048576 | tf_op jit(solution)/shard_map/prepare/pallas_call | solution.py:76
  31.9 0.0 collective-permute-done.1.refs_2_
  31.9 0.0 collective-permute-done.5.refs_8_
  31.9 7.6 %early_partial.1 = (f32[320,2048]{1,0:T(8,128)S(1)}, f32[512,2048]{1,0:T(8,128)S(1)}) custom-call(s32[4]{0:T(128)S(1)} %pad_add_fusion.place, f32[1,2048]{1,0:T(1,128)S(1)} %fusion.2.weight, f32[1,2048]{1,0:T(1,128)S(1)} %get-tuple-element.28.slab_norm, bf16[2048,2048]{1,0:T(8,128)(2,1)S(1)} %get-tuple-element.29.slab, bf16[64,2048]{1,0:T(8,128)(2,1)S(1)} %bitcast.157, ...), custom_call_target="tpu_custom_call" | custom-call | flops 30000001024 | bytes 65536 | tf_op jit(solution)/shard_map/early_partial/pallas_call | solution.py:133
  39.5 0.3 collective-permute-start.7
  39.8 0.0 collective-permute-done.10
  39.8 0.0 collective-permute-done.9
  39.8 0.0 collective-permute-done.8
  39.8 0.1 fusion.45
  39.9 0.5 multiply_reduce_fusion
  40.4 2.9 %fusion = f32[192,2048]{1,0:T(8,128)S(1)} fusion(bf16[2048,2048]{1,0:T(8,128)(2,1)S(1)} %get-tuple-element.29.slab, f32[2048]{0:T(1024)S(1)} %bitcast.159, f32[192]{0:T(256)S(1)} %get-tuple-element.48, bf16[64,2048]{1,0:T(8,128)(2,1)S(1)} %get-tuple-element.68, bf16[64,2048]{1,0:T(8,128)(2,1)S(1)} %get-tuple-element.80, ...), kind=kOutput, calls=%fused_computation.2 | convolution fusion | flops 1614151680 | bytes 10756864 | tf_op jit(solution)/shard_map/dot_general | solution.py:221
  43.3 0.6 collective-permute-start.11
  43.9 2.9 %fusion.1.refs_2_ = f32[192,2048]{1,0:T(8,128)S(1)} fusion(bf16[2048,2048]{1,0:T(8,128)(2,1)S(1)} %get-tuple-element.29.slab, f32[192]{0:T(256)S(1)} %get-tuple-element.47, f32[2048]{0:T(1024)S(1)} %bitcast.160, bf16[64,2048]{1,0:T(8,128)(2,1)S(1)} %get-tuple-element.69, bf16[64,2048]{1,0:T(8,128)(2,1)S(1)} %get-tuple-element.79, ...), kind=kOutput, calls=%fused_computation.3 | convolution fusion | flops 1614151680 | bytes 10756864 | tf_op jit(solution)/shard_map/dot_general | solution.py:221
  46.8 0.1 collective-permute-done.11.refs_1_
  46.9 0.0 collective-permute-done.7.refs_0_
  46.9 1.0 %add_into.1 = f32[512,2048]{1,0:T(8,128)S(1)} custom-call(s32[4]{0:T(128)S(1)} %pad_add_fusion.place, f32[320,2048]{1,0:T(8,128)S(1)} %collective-permute-done.7.refs_0_, f32[192,2048]{1,0:T(8,128)S(1)} %collective-permute-done.11.refs_1_, f32[192,2048]{1,0:T(8,128)S(1)} %fusion.1.refs_2_, ...), custom_call_target="tpu_custom_call", output_to_operand_aliasing={{}: (4, {})} | custom-call | bytes 65536 | tf_op jit(solution)/shard_map/add_into/pallas_call | solution.py:166
  48.0 0.1 slice_bitcast_fusion.3
  48.1 0.1 fusion.5
  48.3 0.8 collective-permute-start.12
  49.1 0.2 collective-permute-start.14
  49.3 2.0 %collective-permute-start.13 = (f16[2,2,32,1024]{3,2,1,0:T(8,128)(2,1)S(1)}, f16[2,2,32,1024]{3,2,1,0:T(8,128)(2,1)S(1)}, u32[]{:S(2)}, u32[]{:S(2)}) collective-permute-start(f16[2,2,32,1024]{3,2,1,0:T(8,128)(2,1)S(1)} %fusion.6), channel_id=1, source_target_pairs={{0,2},{2,4},{4,6},{6,8},{8,10},{10,12},{12,14},{14,0},{1,3},{3,5},... | collective-permute-start | bytes 786440 | tf_op jit(solution)/shard_map/ppermute | solution.py:29
  51.3 4.6 %collective-permute-start.15 = (f16[2,16,1024]{2,1,0:T(8,128)(2,1)S(1)}, f16[2,16,1024]{2,1,0:T(8,128)(2,1)S(1)}, u32[]{:S(2)}, u32[]{:S(2)}) collective-permute-start(f16[2,16,1024]{2,1,0:T(8,128)(2,1)S(1)} %get-tuple-element.75), channel_id=1, source_target_pairs={{0,4},{2,6},{4,8},{6,10},{8,12},{10,14},{12,0},{14,2},{1,5},{3,7},... | collective-permute-start | bytes 196616 | tf_op jit(solution)/shard_map/ppermute | solution.py:29
  55.9 2.2 %collective-permute-start.16 = (f16[2,16,1024]{2,1,0:T(8,128)(2,1)S(1)}, f16[2,16,1024]{2,1,0:T(8,128)(2,1)S(1)}, u32[]{:S(2)}, u32[]{:S(2)}) collective-permute-start(f16[2,16,1024]{2,1,0:T(8,128)(2,1)S(1)} %get-tuple-element.74), channel_id=1, source_target_pairs={{0,12},{2,14},{4,0},{6,2},{8,4},{10,6},{12,8},{14,10},{1,13},{3,15... | collective-permute-start | bytes 196616 | tf_op jit(solution)/shard_map/ppermute | solution.py:29
  58.1 8.6 %collective-permute-done.15 = f16[2,16,1024]{2,1,0:T(8,128)(2,1)S(1)} collective-permute-done((f16[2,16,1024]{2,1,0:T(8,128)(2,1)S(1)}, f16[2,16,1024]{2,1,0:T(8,128)(2,1)S(1)}, u32[]{:S(2)}, u32[]{:S(2)}) %collective-permute-start.15) | collective-permute-done | bytes 65568 | tf_op jit(solution)/shard_map/ppermute | solution.py:29
  66.7 0.0 collective-permute-done.16
  66.7 0.0 collective-permute-done.14
  66.7 0.0 collective-permute-done.13
  66.7 0.0 collective-permute-done.12
  66.7 0.1 fusion.35
  66.9 0.1 collective-permute-start.19
  67.0 2.1 %collective-permute-start.18 = (f16[2,32,1024]{2,1,0:T(8,128)(2,1)S(1)}, f16[2,32,1024]{2,1,0:T(8,128)(2,1)S(1)}, u32[]{:S(2)}, u32[]{:S(2)}) collective-permute-start(f16[2,32,1024]{2,1,0:T(8,128)(2,1)S(1)} %fusion.15), channel_id=1, source_target_pairs={{0,2},{2,4},{4,6},{6,8},{8,10},{10,12},{12,14},{14,0},{1,3},{3,5},... | collective-permute-start | bytes 393224 | tf_op jit(solution)/shard_map/ppermute | solution.py:29
  69.1 0.2 fusion.12
  69.4 1.7 %collective-permute-start.17 = (f16[3,32,1024]{2,1,0:T(8,128)(2,1)S(1)}, f16[3,32,1024]{2,1,0:T(8,128)(2,1)S(1)}, u32[]{:S(2)}, u32[]{:S(2)}) collective-permute-start(f16[3,32,1024]{2,1,0:T(8,128)(2,1)S(1)} %fusion.8), channel_id=1, source_target_pairs={{0,16},{16,0},{1,17},{17,1},{2,18},{18,2},{3,19},{19,3},{4,20},{20... | collective-permute-start | bytes 589832 | tf_op jit(solution)/shard_map/ppermute | solution.py:29
  71.1 0.1 collective-permute-start.20
  71.2 6.5 %collective-permute-done.20 = f16[32,1024]{1,0:T(8,128)(2,1)S(1)} collective-permute-done((f16[32,1024]{1,0:T(8,128)(2,1)S(1)}, f16[32,1024]{1,0:T(8,128)(2,1)S(1)}, u32[]{:S(2)}, u32[]{:S(2)}) %collective-permute-start.20) | collective-permute-done | bytes 65568 | tf_op jit(solution)/shard_map/ppermute | solution.py:29
  77.6 0.0 collective-permute-done.19
  77.6 0.0 collective-permute-done.18
  77.6 0.0 collective-permute-done.17
  77.7 0.1 fusion.27
  77.7 0.1 fusion.29
  77.9 0.6 collective-permute-start.21
  78.5 2.4 %collective-permute-start.22 = (f16[32,2048]{1,0:T(8,128)(2,1)S(1)}, f16[32,2048]{1,0:T(8,128)(2,1)S(1)}, u32[]{:S(2)}, u32[]{:S(2)}) collective-permute-start(f16[32,2048]{1,0:T(8,128)(2,1)S(1)} %fusion.22), channel_id=1, source_target_pairs={{0,4},{2,6},{4,8},{6,10},{8,12},{10,14},{12,0},{14,2},{1,5},{3,7},... | collective-permute-start | bytes 393224 | tf_op jit(solution)/shard_map/ppermute | solution.py:29
  81.6 2.8 %collective-permute-done.21 = f16[32,2048]{1,0:T(8,128)(2,1)S(1)} collective-permute-done((f16[32,2048]{1,0:T(8,128)(2,1)S(1)}, f16[32,2048]{1,0:T(8,128)(2,1)S(1)}, u32[]{:S(2)}, u32[]{:S(2)}) %collective-permute-start.21) | collective-permute-done | bytes 131104 | tf_op jit(solution)/shard_map/ppermute | solution.py:29
  84.4 2.2 %collective-permute-done.22 = f16[32,2048]{1,0:T(8,128)(2,1)S(1)} collective-permute-done((f16[32,2048]{1,0:T(8,128)(2,1)S(1)}, f16[32,2048]{1,0:T(8,128)(2,1)S(1)}, u32[]{:S(2)}, u32[]{:S(2)}) %collective-permute-start.22) | collective-permute-done | bytes 131104 | tf_op jit(solution)/shard_map/ppermute | solution.py:29
  86.6 0.8 fusion.20
  (21 shorter events, 0.5 us)
Async XLA Ops:
  0.0 13.2 %copy-start = (f32[256]{0:T(256)S(1)}, f32[256]{0:T(256)}, u32[]{:S(2)}) copy-start(f32[256]{0:T(256)} %param.8) | copy-start | bytes 3076
  0.0 13.2 %copy-start.1 = (s32[2048]{0:T(1024)S(1)}, s32[2048]{0:T(1024)}, u32[]{:S(2)}) copy-start(s32[2048]{0:T(1024)} %param.7) | copy-start | bytes 24580
  1.1 8.4 %collective-permute-start.2 = (bf16[64,2048]{1,0:T(8,128)(2,1)S(1)}, bf16[64,2048]{1,0:T(8,128)(2,1)S(1)}, u32[]{:S(2)}, u32[]{:S(2)}) collective-permute-start(bf16[64,2048]{1,0:T(8,128)(2,1)S(1)} %bitcast.154), channel_id=1, source_target_pairs={{0,192},{64,0},{128,64},{192,128},{1,193},{65,1},{129,65},{193,129... | collective-permute-start | bytes 786440 | tf_op jit(solution)/shard_map/ppermute | solution.py:29
  3.9 9.3 %collective-permute-start.4 = (bf16[64,2048]{1,0:T(8,128)(2,1)S(1)}, bf16[64,2048]{1,0:T(8,128)(2,1)S(1)}, u32[]{:S(2)}, u32[]{:S(2)}) collective-permute-start(bf16[64,2048]{1,0:T(8,128)(2,1)S(1)} %bitcast.150), channel_id=1, source_target_pairs={{0,64},{64,128},{128,192},{192,0},{1,65},{65,129},{129,193},{193,1... | collective-permute-start | bytes 786440 | tf_op jit(solution)/shard_map/ppermute | solution.py:29
  4.0 15.0 %collective-permute-start = (bf16[128,2048]{1,0:T(8,128)(2,1)S(1)}, bf16[128,2048]{1,0:T(8,128)(2,1)S(1)}, u32[]{:S(2)}, u32[]{:S(2)}) collective-permute-start(bf16[128,2048]{1,0:T(8,128)(2,1)S(1)} %pad_maximum_fusion.2), channel_id=1, source_target_pairs={{0,32},{32,0},{1,33},{33,1},{2,34},{34,2},{3,35},{35,3},{4,36},{36... | collective-permute-start | bytes 1572872 | tf_op jit(solution)/shard_map/ppermute | solution.py:29
  9.5 12.4 %collective-permute-start.3 = (bf16[64,2048]{1,0:T(8,128)(2,1)S(1)}, bf16[64,2048]{1,0:T(8,128)(2,1)S(1)}, u32[]{:S(2)}, u32[]{:S(2)}) collective-permute-start(bf16[64,2048]{1,0:T(8,128)(2,1)S(1)} %collective-permute-done.2.refs_3_), channel_id=1, source_target_pairs={{0,192},{64,0},{128,64},{192,128},{1,193},{65,1},{129,65},{193,129... | collective-permute-start | bytes 786440 | tf_op jit(solution)/shard_map/ppermute | solution.py:29
  13.2 10.5 %collective-permute-start.6 = (bf16[64,2048]{1,0:T(8,128)(2,1)S(1)}, bf16[64,2048]{1,0:T(8,128)(2,1)S(1)}, u32[]{:S(2)}, u32[]{:S(2)}) collective-permute-start(bf16[64,2048]{1,0:T(8,128)(2,1)S(1)} %collective-permute-done.4.refs_7_), channel_id=1, source_target_pairs={{0,64},{64,128},{128,192},{192,0},{1,65},{65,129},{129,193},{193,1... | collective-permute-start | bytes 786440 | tf_op jit(solution)/shard_map/ppermute | solution.py:29
  14.3 17.7 %collective-permute-start.1 = (bf16[64,2048]{1,0:T(8,128)(2,1)S(1)}, bf16[64,2048]{1,0:T(8,128)(2,1)S(1)}, u32[]{:S(2)}, u32[]{:S(2)}) collective-permute-start(bf16[64,2048]{1,0:T(8,128)(2,1)S(1)} %bitcast.156), channel_id=1, source_target_pairs={{0,64},{64,128},{128,192},{192,0},{1,65},{65,129},{129,193},{193,1... | collective-permute-start | bytes 786440 | tf_op jit(solution)/shard_map/ppermute | solution.py:29
  14.3 17.6 %collective-permute-start.5 = (bf16[64,2048]{1,0:T(8,128)(2,1)S(1)}, bf16[64,2048]{1,0:T(8,128)(2,1)S(1)}, u32[]{:S(2)}, u32[]{:S(2)}) collective-permute-start(bf16[64,2048]{1,0:T(8,128)(2,1)S(1)} %bitcast.152), channel_id=1, source_target_pairs={{0,192},{64,0},{128,64},{192,128},{1,193},{65,1},{129,65},{193,129... | collective-permute-start | bytes 786440 | tf_op jit(solution)/shard_map/ppermute | solution.py:29
  19.0 20.8 %collective-permute-start.10 = (bf16[128,2048]{1,0:T(8,128)(2,1)S(1)}, bf16[128,2048]{1,0:T(8,128)(2,1)S(1)}, u32[]{:S(2)}, u32[]{:S(2)}) collective-permute-start(bf16[128,2048]{1,0:T(8,128)(2,1)S(1)} %collective-permute-done), channel_id=1, source_target_pairs={{0,192},{64,0},{128,64},{192,128},{1,193},{65,1},{129,65},{193,129... | collective-permute-start | bytes 1572872 | tf_op jit(solution)/shard_map/ppermute | solution.py:29
  21.9 17.9 %collective-permute-start.9 = (bf16[128,2048]{1,0:T(8,128)(2,1)S(1)}, bf16[128,2048]{1,0:T(8,128)(2,1)S(1)}, u32[]{:S(2)}, u32[]{:S(2)}) collective-permute-start(bf16[128,2048]{1,0:T(8,128)(2,1)S(1)} %collective-permute-done), channel_id=1, source_target_pairs={{0,64},{64,128},{128,192},{192,0},{1,65},{65,129},{129,193},{193,1... | collective-permute-start | bytes 1572872 | tf_op jit(solution)/shard_map/ppermute | solution.py:29
  23.7 16.1 %collective-permute-start.8 = (bf16[128,2048]{1,0:T(8,128)(2,1)S(1)}, bf16[128,2048]{1,0:T(8,128)(2,1)S(1)}, u32[]{:S(2)}, u32[]{:S(2)}) collective-permute-start(bf16[128,2048]{1,0:T(8,128)(2,1)S(1)} %pad_maximum_fusion.3), channel_id=1, source_target_pairs={{0,32},{32,0},{1,33},{33,1},{2,34},{34,2},{3,35},{35,3},{4,36},{36... | collective-permute-start | bytes 1572872 | tf_op jit(solution)/shard_map/ppermute | solution.py:29
  39.5 7.4 %collective-permute-start.7 = (f32[320,2048]{1,0:T(8,128)S(1)}, f32[320,2048]{1,0:T(8,128)S(1)}, u32[]{:S(2)}, u32[]{:S(2)}) collective-permute-start(f32[320,2048]{1,0:T(8,128)S(1)} %get-tuple-element.33), channel_id=1, source_target_pairs={{0,1},{1,0},{2,3},{3,2},{4,5},{5,4},{6,7},{7,6},{8,9},{9,8},{10,11... | collective-permute-start | bytes 7864328 | tf_op jit(solution)/shard_map/ppermute | solution.py:29
  43.3 3.6 %collective-permute-start.11 = (f32[192,2048]{1,0:T(8,128)S(1)}, f32[192,2048]{1,0:T(8,128)S(1)}, u32[]{:S(2)}, u32[]{:S(2)}) collective-permute-start(f32[192,2048]{1,0:T(8,128)S(1)} %fusion), channel_id=1, source_target_pairs={{0,1},{1,0},{2,3},{3,2},{4,5},{5,4},{6,7},{7,6},{8,9},{9,8},{10,11... | collective-permute-start | bytes 4718600 | tf_op jit(solution)/shard_map/ppermute | solution.py:29
  48.3 18.5 %collective-permute-start.12 = (f16[8,32,1024]{2,1,0:T(8,128)(2,1)S(1)}, f16[8,32,1024]{2,1,0:T(8,128)(2,1)S(1)}, u32[]{:S(2)}, u32[]{:S(2)}) collective-permute-start(f16[8,32,1024]{2,1,0:T(8,128)(2,1)S(1)} %fusion.5), channel_id=1, source_target_pairs={{0,16},{16,0},{1,17},{17,1},{2,18},{18,2},{3,19},{19,3},{4,20},{20... | collective-permute-start | bytes 1572872 | tf_op jit(solution)/shard_map/ppermute | solution.py:29
  49.1 17.6 %collective-permute-start.14 = (f16[2,2,32,1024]{3,2,1,0:T(8,128)(2,1)S(1)}, f16[2,2,32,1024]{3,2,1,0:T(8,128)(2,1)S(1)}, u32[]{:S(2)}, u32[]{:S(2)}) collective-permute-start(f16[2,2,32,1024]{3,2,1,0:T(8,128)(2,1)S(1)} %fusion.7), channel_id=1, source_target_pairs={{0,14},{2,0},{4,2},{6,4},{8,6},{10,8},{12,10},{14,12},{1,15},{3,1}... | collective-permute-start | bytes 786440 | tf_op jit(solution)/shard_map/ppermute | solution.py:29
  49.3 17.4 %collective-permute-start.13 = (f16[2,2,32,1024]{3,2,1,0:T(8,128)(2,1)S(1)}, f16[2,2,32,1024]{3,2,1,0:T(8,128)(2,1)S(1)}, u32[]{:S(2)}, u32[]{:S(2)}) collective-permute-start(f16[2,2,32,1024]{3,2,1,0:T(8,128)(2,1)S(1)} %fusion.6), channel_id=1, source_target_pairs={{0,2},{2,4},{4,6},{6,8},{8,10},{10,12},{12,14},{14,0},{1,3},{3,5},... | collective-permute-start | bytes 786440 | tf_op jit(solution)/shard_map/ppermute | solution.py:29
  51.3 15.4 %collective-permute-start.15 = (f16[2,16,1024]{2,1,0:T(8,128)(2,1)S(1)}, f16[2,16,1024]{2,1,0:T(8,128)(2,1)S(1)}, u32[]{:S(2)}, u32[]{:S(2)}) collective-permute-start(f16[2,16,1024]{2,1,0:T(8,128)(2,1)S(1)} %get-tuple-element.75), channel_id=1, source_target_pairs={{0,4},{2,6},{4,8},{6,10},{8,12},{10,14},{12,0},{14,2},{1,5},{3,7},... | collective-permute-start | bytes 196616 | tf_op jit(solution)/shard_map/ppermute | solution.py:29
  55.9 10.8 %collective-permute-start.16 = (f16[2,16,1024]{2,1,0:T(8,128)(2,1)S(1)}, f16[2,16,1024]{2,1,0:T(8,128)(2,1)S(1)}, u32[]{:S(2)}, u32[]{:S(2)}) collective-permute-start(f16[2,16,1024]{2,1,0:T(8,128)(2,1)S(1)} %get-tuple-element.74), channel_id=1, source_target_pairs={{0,12},{2,14},{4,0},{6,2},{8,4},{10,6},{12,8},{14,10},{1,13},{3,15... | collective-permute-start | bytes 196616 | tf_op jit(solution)/shard_map/ppermute | solution.py:29
  66.9 10.8 %collective-permute-start.19 = (f16[2,32,1024]{2,1,0:T(8,128)(2,1)S(1)}, f16[2,32,1024]{2,1,0:T(8,128)(2,1)S(1)}, u32[]{:S(2)}, u32[]{:S(2)}) collective-permute-start(f16[2,32,1024]{2,1,0:T(8,128)(2,1)S(1)} %fusion.16), channel_id=1, source_target_pairs={{0,14},{2,0},{4,2},{6,4},{8,6},{10,8},{12,10},{14,12},{1,15},{3,1}... | collective-permute-start | bytes 393224 | tf_op jit(solution)/shard_map/ppermute | solution.py:29
  67.0 10.7 %collective-permute-start.18 = (f16[2,32,1024]{2,1,0:T(8,128)(2,1)S(1)}, f16[2,32,1024]{2,1,0:T(8,128)(2,1)S(1)}, u32[]{:S(2)}, u32[]{:S(2)}) collective-permute-start(f16[2,32,1024]{2,1,0:T(8,128)(2,1)S(1)} %fusion.15), channel_id=1, source_target_pairs={{0,2},{2,4},{4,6},{6,8},{8,10},{10,12},{12,14},{14,0},{1,3},{3,5},... | collective-permute-start | bytes 393224 | tf_op jit(solution)/shard_map/ppermute | solution.py:29
  69.4 8.3 %collective-permute-start.17 = (f16[3,32,1024]{2,1,0:T(8,128)(2,1)S(1)}, f16[3,32,1024]{2,1,0:T(8,128)(2,1)S(1)}, u32[]{:S(2)}, u32[]{:S(2)}) collective-permute-start(f16[3,32,1024]{2,1,0:T(8,128)(2,1)S(1)} %fusion.8), channel_id=1, source_target_pairs={{0,16},{16,0},{1,17},{17,1},{2,18},{18,2},{3,19},{19,3},{4,20},{20... | collective-permute-start | bytes 589832 | tf_op jit(solution)/shard_map/ppermute | solution.py:29
  71.1 6.6 %collective-permute-start.20 = (f16[32,1024]{1,0:T(8,128)(2,1)S(1)}, f16[32,1024]{1,0:T(8,128)(2,1)S(1)}, u32[]{:S(2)}, u32[]{:S(2)}) collective-permute-start(f16[32,1024]{1,0:T(8,128)(2,1)S(1)} %fusion.33), channel_id=1, source_target_pairs={{0,4},{2,6},{4,8},{6,10},{8,12},{10,14},{12,0},{14,2},{1,5},{3,7},... | collective-permute-start | bytes 196616 | tf_op jit(solution)/shard_map/ppermute | solution.py:29
  77.9 6.5 %collective-permute-start.21 = (f16[32,2048]{1,0:T(8,128)(2,1)S(1)}, f16[32,2048]{1,0:T(8,128)(2,1)S(1)}, u32[]{:S(2)}, u32[]{:S(2)}) collective-permute-start(f16[32,2048]{1,0:T(8,128)(2,1)S(1)} %fusion.21), channel_id=1, source_target_pairs={{0,12},{2,14},{4,0},{6,2},{8,4},{10,6},{12,8},{14,10},{1,13},{3,15... | collective-permute-start | bytes 393224 | tf_op jit(solution)/shard_map/ppermute | solution.py:29
  78.5 8.1 %collective-permute-start.22 = (f16[32,2048]{1,0:T(8,128)(2,1)S(1)}, f16[32,2048]{1,0:T(8,128)(2,1)S(1)}, u32[]{:S(2)}, u32[]{:S(2)}) collective-permute-start(f16[32,2048]{1,0:T(8,128)(2,1)S(1)} %fusion.22), channel_id=1, source_target_pairs={{0,4},{2,6},{4,8},{6,10},{8,12},{10,14},{12,0},{14,2},{1,5},{3,7},... | collective-permute-start | bytes 393224 | tf_op jit(solution)/shard_map/ppermute | solution.py:29
